TPU v7x, 128 devices: a whole 4x4x4 slice. The times are simulated.
128 devices in a mesh: fsdp: 8 (over y, z_hi), ctx: 16 (over x, z_lo, core).
Axes of the slice: x: 4, y: 4, z: 4 (z_hi: 2, z_lo: 2; z = z_hi * 2 + z_lo), core: 2. Of those that a mesh axis runs over, the one named last changes fastest.
Arguments:
- tokens: bfloat16 [16384, 2048], P(('fsdp', 'ctx')), may hold values from -6 to 6
- out_grad: bfloat16 [16384, 2048], P(('fsdp', 'ctx')), may hold values from -6 to 6
- seq_lengths: int32 [8, 2], P('fsdp'), may hold values from 1 to 1792, as said below
- span_order: int32 [32], replicated, may hold values from 0 to 31, as said below
- attn_in: float32 [2048, 2560], P(('fsdp', 'ctx')), may hold values from -0.125 to 0.125
- attn_out: float32 [2048, 2048], P(('fsdp', 'ctx')), may hold values from -1.5 to 1.5
- gate_up: float32 [2048, 11264], P(('fsdp', 'ctx')), may hold values from -0.125 to 0.125
- down_proj: float32 [5632, 2048], P(('fsdp', 'ctx')), may hold values from -0.078125 to 0.078125
- norm_gains: float32 [2, 2048], P(None, ('fsdp', 'ctx')), may hold values from 0.5 to 1.5
- first_attn_in: float32 [2048, 2560], P(('fsdp', 'ctx')), may hold values from -128 to 128
- second_attn_in: float32 [2048, 2560], P(('fsdp', 'ctx')), may hold values from 983.04 to 6553.6
- first_attn_out: float32 [2048, 2048], P(('fsdp', 'ctx')), may hold values from -6 to 6
- second_attn_out: float32 [2048, 2048], P(('fsdp', 'ctx')), may hold values from 12.288 to 81.92
- first_gate_up: float32 [2048, 11264], P(('fsdp', 'ctx')), may hold values from -24 to 24
- second_gate_up: float32 [2048, 11264], P(('fsdp', 'ctx')), may hold values from 44.2368 to 294.912
- first_down_proj: float32 [5632, 2048], P(('fsdp', 'ctx')), may hold values from -48 to 48
- second_down_proj: float32 [5632, 2048], P(('fsdp', 'ctx')), may hold values from 180.224 to 1179.648
- first_norm_gains: float32 [2, 2048], P(None, ('fsdp', 'ctx')), may hold values from -80 to 80
- second_norm_gains: float32 [2, 2048], P(None, ('fsdp', 'ctx')), may hold values from 491.52 to 3276.8
Outputs:
- block_out: bfloat16 [16384, 2048], P(('fsdp', 'ctx'))
- in_grad: bfloat16 [16384, 2048], P(('fsdp', 'ctx'))
- first_attn_in_next: float32 [2048, 2560], P(('fsdp', 'ctx'))
- second_attn_in_next: float32 [2048, 2560], P(('fsdp', 'ctx'))
- attn_in_next: float32 [2048, 2560], P(('fsdp', 'ctx'))
- first_attn_out_next: float32 [2048, 2048], P(('fsdp', 'ctx'))
- second_attn_out_next: float32 [2048, 2048], P(('fsdp', 'ctx'))
- attn_out_next: float32 [2048, 2048], P(('fsdp', 'ctx'))
- first_gate_up_next: float32 [2048, 11264], P(('fsdp', 'ctx'))
- second_gate_up_next: float32 [2048, 11264], P(('fsdp', 'ctx'))
- gate_up_next: float32 [2048, 11264], P(('fsdp', 'ctx'))
- first_down_proj_next: float32 [5632, 2048], P(('fsdp', 'ctx'))
- second_down_proj_next: float32 [5632, 2048], P(('fsdp', 'ctx'))
- down_proj_next: float32 [5632, 2048], P(('fsdp', 'ctx'))
- first_norm_gains_next: float32 [2, 2048], P(None, ('fsdp', 'ctx'))
- second_norm_gains_next: float32 [2, 2048], P(None, ('fsdp', 'ctx'))
- norm_gains_next: float32 [2, 2048], P(None, ('fsdp', 'ctx'))
Inputs may be any that keep to these rules, and one draw needn't show every extreme that they name: `seq_lengths`: row g lists the lengths of the 2 sequences of group g, laid end to end from position 0; the first is at least 1024 and in some group exactly 1792; a group's lengths sum to at most 2048, slots after them are unused. `span_order`: entry 2 c is a block from 0 to 15 and entry 2 c + 1 a block from 16 to 31; every block appears once. Block b holds positions b * 64 up to (b + 1) * 64 - 1.
All inputs are finite; a program needn't handle non-finite values.
Results may differ from a plain program's by a relative error of at most 0.035.
Values may be sent and summed in bfloat16 or wider, within the bound.
No kernel may reach another device: no remote copies, remote signals or barrier semaphores. Data moves between devices by JAX's collectives and lax.ppermute only.
A program may use at most 448 MiB of HBM per device.

v0:
```python
import jax
import jax.numpy as jnp
from jax import lax
from jax.sharding import PartitionSpec as P

FF = 5632
HEADS = 32
KV_HEADS = 4
HEAD_DIM = 64
STEP = 10
QDIM = 2048
KVDIM = 256


norm_eps = 1e-05
beta_one = 0.9
beta_two = 0.95
adam_eps = 1e-08
big_negative = -1e30
step_rates = (0.15, 0.3, 0.06, 0.04, 2.0)
decay_rates = (0.1, 0.1, 0.1, 0.1, 0.0)


def shifted(block, axis, distance):
    devices = range(lax.axis_size(axis))
    route = [((i - distance) % len(devices), i) for i in devices]
    return lax.ppermute(block, axis, route)


def slot_positions(slot_index, span_order, tok_rows):
    half_rows = tok_rows // 2
    holder = slot_index // tok_rows
    within = slot_index % tok_rows
    column = 2 * holder + within // half_rows
    onehot_table = (
        column[:, None] == jnp.arange(span_order.shape[0], dtype=jnp.int32)[None, :]
    ).astype(jnp.int32)
    span_ids = jnp.sum(onehot_table * span_order[None, :], axis=1)
    return span_ids * half_rows + within % half_rows


def doc_numbers(positions, lengths):
    bounds = jnp.cumsum(lengths)
    return jnp.sum((positions[:, None] >= bounds[None, :]).astype(jnp.int32), axis=1)


def adam_update(master, grad_sum, first_old, second_old, step_rate, decay_rate):
    first_new = beta_one * first_old + (1.0 - beta_one) * grad_sum
    second_new = beta_two * second_old + (1.0 - beta_two) * grad_sum * grad_sum
    first_fix = first_new / (1.0 - beta_one**STEP)
    second_fix = second_new / (1.0 - beta_two**STEP)
    master_new = master - step_rate * (
        first_fix / (jnp.sqrt(second_fix) + adam_eps) + decay_rate * master
    )
    return (first_new, second_new, master_new)


def row_contract(left_side, right_side):
    return lax.dot_general(
        left_side, right_side, (((0,), (0,)), ((), ())), preferred_element_type=jnp.float32
    )


def col_contract(left_side, right_side):
    return lax.dot_general(
        left_side, right_side, (((1,), (1,)), ((), ())), preferred_element_type=jnp.float32
    )


def head_scores(query_heads, key_part, kv_heads, head_size):
    key_heads = key_part.reshape(key_part.shape[0], kv_heads, head_size)
    return jnp.einsum(
        "rhgd,khd->hgrk", query_heads, key_heads, preferred_element_type=jnp.float32
    ) * head_size ** (-0.5)


def allowed_pairs(query_pos, query_doc, key_pos, key_doc, seq_count):
    return (
        (key_doc[None, :] == query_doc[:, None])
        & (key_pos[None, :] <= query_pos[:, None])
        & (query_doc[:, None] < seq_count)
    )


def norm_back(grad_normed, normed_hat, row_scale, gain_row, grad_rest):
    grad_hat = grad_normed * gain_row
    return grad_rest + row_scale * (
        grad_hat - normed_hat * jnp.mean(grad_hat * normed_hat, axis=-1, keepdims=True)
    )


def body(
    tokens,
    out_grad,
    seq_lengths,
    span_order,
    attn_in,
    attn_out,
    gate_up,
    down_proj,
    norm_gains,
    first_attn_in,
    second_attn_in,
    first_attn_out,
    second_attn_out,
    first_gate_up,
    second_gate_up,
    first_down_proj,
    second_down_proj,
    first_norm_gains,
    second_norm_gains,
):
    cycle_size = lax.axis_size("ctx")
    cycle_rank = lax.axis_index("ctx")
    tok_rows = tokens.shape[0]
    group_size = HEADS // KV_HEADS
    seq_count = seq_lengths.shape[1]
    lengths_here = seq_lengths[0]
    own_slots = cycle_rank * tok_rows + jnp.arange(tok_rows, dtype=jnp.int32)
    own_pos = slot_positions(own_slots, span_order, tok_rows)
    own_doc = doc_numbers(own_pos, lengths_here)
    shards = (
        attn_in.astype(jnp.bfloat16),
        attn_out.astype(jnp.bfloat16),
        gate_up.astype(jnp.bfloat16),
        down_proj.astype(jnp.bfloat16),
        norm_gains.astype(jnp.bfloat16),
    )
    w_qkv, w_out, w_gu, w_down, gain_pair = (
        lax.all_gather(shards[0], ("fsdp", "ctx"), axis=0, tiled=True),
        lax.all_gather(shards[1], ("fsdp", "ctx"), axis=0, tiled=True),
        lax.all_gather(shards[2], ("fsdp", "ctx"), axis=0, tiled=True),
        lax.all_gather(shards[3], ("fsdp", "ctx"), axis=0, tiled=True),
        lax.all_gather(shards[4], ("fsdp", "ctx"), axis=1, tiled=True),
    )
    gain_one = gain_pair[0].astype(jnp.float32)
    gain_two = gain_pair[1].astype(jnp.float32)
    inputs = tokens.astype(jnp.float32)
    scale_one = lax.rsqrt(jnp.mean(inputs * inputs, axis=-1, keepdims=True) + norm_eps)
    hat_one = inputs * scale_one
    normed_one = (hat_one * gain_one).astype(jnp.bfloat16)
    projected = jnp.dot(normed_one, w_qkv, preferred_element_type=jnp.float32).astype(jnp.bfloat16)
    query_heads = projected[:, :QDIM].reshape(tok_rows, KV_HEADS, group_size, HEAD_DIM)
    key_values = projected[:, QDIM:]
    head_shape = (KV_HEADS, group_size, tok_rows)
    shard_rows = lax.all_gather(key_values, "ctx", axis=0, tiled=True)
    run_max = jnp.full(head_shape, big_negative, jnp.float32)
    amount = shard_rows.shape[0]
    slot_ids = jnp.arange(amount, dtype=jnp.int32)
    key_pos = slot_positions(slot_ids, span_order, tok_rows)
    key_doc = doc_numbers(key_pos, lengths_here)
    scores = head_scores(query_heads, shard_rows[:, :KVDIM], KV_HEADS, HEAD_DIM)
    allowed = allowed_pairs(own_pos, own_doc, key_pos, key_doc, seq_count)
    masked = jnp.where(allowed, scores, big_negative)
    max_new = jnp.maximum(run_max, jnp.max(masked, axis=-1))
    raised = jnp.where(allowed, jnp.exp(masked - max_new[..., None]), 0.0)
    value_heads = shard_rows[:, KVDIM:].reshape(amount, KV_HEADS, HEAD_DIM)
    weighted = jnp.einsum(
        "hgrk,khd->hgrd",
        raised.astype(jnp.bfloat16),
        value_heads,
        preferred_element_type=jnp.float32,
    )
    run_max, run_sum, weighted = (max_new, jnp.sum(raised, axis=-1), weighted)
    live_rows = (own_doc < seq_count)[None, None, :]
    safe_sum = jnp.where(live_rows, run_sum, 1.0)
    row_lse = run_max + jnp.log(safe_sum)
    attended_heads = weighted / safe_sum[..., None]
    attended_low = (
        jnp.transpose(attended_heads, (2, 0, 1, 3)).reshape(tok_rows, QDIM).astype(jnp.bfloat16)
    )
    hidden_one = inputs + jnp.dot(attended_low, w_out, preferred_element_type=jnp.float32)
    scale_two = lax.rsqrt(jnp.mean(hidden_one * hidden_one, axis=-1, keepdims=True) + norm_eps)
    hat_two = hidden_one * scale_two
    normed_two = (hat_two * gain_two).astype(jnp.bfloat16)
    gate_up_val = jnp.dot(normed_two, w_gu, preferred_element_type=jnp.float32)
    gate_part = gate_up_val[:, :FF]
    up_part = gate_up_val[:, FF:]
    sigmoid_gate = jax.nn.sigmoid(gate_part)
    silu_gate = gate_part * sigmoid_gate
    activated = (silu_gate * up_part).astype(jnp.bfloat16)
    block_out = (
        hidden_one + jnp.dot(activated, w_down, preferred_element_type=jnp.float32)
    ).astype(jnp.bfloat16)
    w_qkv, w_out, w_gu, w_down = (
        lax.all_gather(shards[0], ("fsdp", "ctx"), axis=0, tiled=True),
        lax.all_gather(shards[1], ("fsdp", "ctx"), axis=0, tiled=True),
        lax.all_gather(shards[2], ("fsdp", "ctx"), axis=0, tiled=True),
        lax.all_gather(shards[3], ("fsdp", "ctx"), axis=0, tiled=True),
    )
    grad_down_term = row_contract(activated, out_grad)
    grad_act = col_contract(out_grad, w_down)
    grad_gate = grad_act * up_part * sigmoid_gate * (1.0 + gate_part * (1.0 - sigmoid_gate))
    grad_up = grad_act * silu_gate
    grad_gu = jnp.concatenate([grad_gate, grad_up], axis=1).astype(jnp.bfloat16)
    grad_gu_term = row_contract(normed_two, grad_gu)
    grad_norm_two = col_contract(grad_gu, w_gu)
    gu_sum, down_sum = (
        lax.psum_scatter(grad_gu_term, ("fsdp", "ctx"), scatter_dimension=0, tiled=True),
        lax.psum_scatter(grad_down_term, ("fsdp", "ctx"), scatter_dimension=0, tiled=True),
    )
    gain_two_term = jnp.sum(grad_norm_two * hat_two, axis=0)
    grad_hidden = norm_back(
        grad_norm_two, hat_two, scale_two, gain_two, out_grad.astype(jnp.float32)
    )
    grad_hidden_low = grad_hidden.astype(jnp.bfloat16)
    grad_out_term = row_contract(attended_low, grad_hidden_low)
    grad_attended = col_contract(grad_hidden_low, w_out).astype(jnp.bfloat16)
    grad_heads = grad_attended.reshape(tok_rows, KV_HEADS, group_size, HEAD_DIM)
    delta_rows = jnp.einsum("rhgd,hgrd->hgr", grad_heads.astype(jnp.float32), attended_heads)

    def grads_from(key_block, slot_ids):
        amount = key_block.shape[0]
        key_pos = slot_positions(slot_ids, span_order, tok_rows)
        key_doc = doc_numbers(key_pos, lengths_here)
        key_heads = key_block[:, :KVDIM].reshape(amount, KV_HEADS, HEAD_DIM)
        value_heads = key_block[:, KVDIM:].reshape(amount, KV_HEADS, HEAD_DIM)
        scores = head_scores(query_heads, key_block[:, :KVDIM], KV_HEADS, HEAD_DIM)
        allowed = allowed_pairs(own_pos, own_doc, key_pos, key_doc, seq_count)
        attn_probs = jnp.where(allowed, jnp.exp(scores - row_lse[..., None]), 0.0)
        grad_probs = jnp.einsum(
            "rhgd,khd->hgrk", grad_heads, value_heads, preferred_element_type=jnp.float32
        )
        grad_scores = (attn_probs * (grad_probs - delta_rows[..., None])).astype(jnp.bfloat16)
        score_scale = HEAD_DIM ** (-0.5)
        grad_query = (
            jnp.einsum("hgrk,khd->rhgd", grad_scores, key_heads, preferred_element_type=jnp.float32)
            * score_scale
        )
        grad_key = (
            jnp.einsum(
                "hgrk,rhgd->khd", grad_scores, query_heads, preferred_element_type=jnp.float32
            )
            * score_scale
        )
        grad_value = jnp.einsum(
            "hgrk,rhgd->khd",
            attn_probs.astype(jnp.bfloat16),
            grad_heads,
            preferred_element_type=jnp.float32,
        )
        return (
            grad_query,
            jnp.concatenate(
                [grad_key.reshape(amount, KVDIM), grad_value.reshape(amount, KVDIM)], axis=1
            ),
        )

    zero_query = jnp.zeros((tok_rows, KV_HEADS, group_size, HEAD_DIM), jnp.float32)
    local_rows = jnp.arange(tok_rows, dtype=jnp.int32)

    def cycle_turn(turn_index, loop_state):
        key_block, carried, grad_query = loop_state
        arriving = shifted(key_block, "ctx", 1)
        source = (cycle_rank - turn_index) % cycle_size
        query_part, key_part = grads_from(key_block, source * tok_rows + local_rows)
        carried = shifted((carried + key_part).astype(jnp.bfloat16), "ctx", 1).astype(jnp.float32)
        return (arriving, carried, grad_query + query_part)

    returned, grad_kv, grad_query = lax.fori_loop(
        0,
        cycle_size,
        cycle_turn,
        (key_values, jnp.zeros((tok_rows, 2 * KVDIM), jnp.float32), zero_query),
    )
    grad_mixed = jnp.concatenate([grad_query.reshape(tok_rows, QDIM), grad_kv], axis=1).astype(
        jnp.bfloat16
    )
    grad_qkv_term = row_contract(normed_one, grad_mixed)
    grad_norm_one = col_contract(grad_mixed, w_qkv)
    gain_one_term = jnp.sum(grad_norm_one * hat_one, axis=0)
    grad_inputs = norm_back(grad_norm_one, hat_one, scale_one, gain_one, grad_hidden)
    gain_terms = jnp.stack([gain_one_term, gain_two_term])
    qkv_sum, out_sum, gains_sum = (
        lax.psum_scatter(grad_qkv_term, ("fsdp", "ctx"), scatter_dimension=0, tiled=True),
        lax.psum_scatter(grad_out_term, ("fsdp", "ctx"), scatter_dimension=0, tiled=True),
        lax.psum_scatter(gain_terms, ("fsdp", "ctx"), scatter_dimension=1, tiled=True),
    )
    qkv_new = adam_update(
        attn_in, qkv_sum, first_attn_in, second_attn_in, step_rates[0], decay_rates[0]
    )
    out_new = adam_update(
        attn_out, out_sum, first_attn_out, second_attn_out, step_rates[1], decay_rates[1]
    )
    gu_new = adam_update(
        gate_up, gu_sum, first_gate_up, second_gate_up, step_rates[2], decay_rates[2]
    )
    down_new = adam_update(
        down_proj, down_sum, first_down_proj, second_down_proj, step_rates[3], decay_rates[3]
    )
    gains_new = adam_update(
        norm_gains, gains_sum, first_norm_gains, second_norm_gains, step_rates[4], decay_rates[4]
    )
    return (
        block_out,
        grad_inputs.astype(jnp.bfloat16),
        qkv_new[0],
        qkv_new[1],
        qkv_new[2],
        out_new[0],
        out_new[1],
        out_new[2],
        gu_new[0],
        gu_new[1],
        gu_new[2],
        down_new[0],
        down_new[1],
        down_new[2],
        gains_new[0],
        gains_new[1],
        gains_new[2],
    )


def solution(mesh):
    in_specs = (
        P(("fsdp", "ctx"), None),
        P(("fsdp", "ctx"), None),
        P("fsdp", None),
        P(),
        P(("fsdp", "ctx"), None),
        P(("fsdp", "ctx"), None),
        P(("fsdp", "ctx"), None),
        P(("fsdp", "ctx"), None),
        P(None, ("fsdp", "ctx")),
        P(("fsdp", "ctx"), None),
        P(("fsdp", "ctx"), None),
        P(("fsdp", "ctx"), None),
        P(("fsdp", "ctx"), None),
        P(("fsdp", "ctx"), None),
        P(("fsdp", "ctx"), None),
        P(("fsdp", "ctx"), None),
        P(("fsdp", "ctx"), None),
        P(None, ("fsdp", "ctx")),
        P(None, ("fsdp", "ctx")),
    )
    out_specs = (
        P(("fsdp", "ctx"), None),
        P(("fsdp", "ctx"), None),
        P(("fsdp", "ctx"), None),
        P(("fsdp", "ctx"), None),
        P(("fsdp", "ctx"), None),
        P(("fsdp", "ctx"), None),
        P(("fsdp", "ctx"), None),
        P(("fsdp", "ctx"), None),
        P(("fsdp", "ctx"), None),
        P(("fsdp", "ctx"), None),
        P(("fsdp", "ctx"), None),
        P(("fsdp", "ctx"), None),
        P(("fsdp", "ctx"), None),
        P(("fsdp", "ctx"), None),
        P(None, ("fsdp", "ctx")),
        P(None, ("fsdp", "ctx")),
        P(None, ("fsdp", "ctx")),
    )
    return jax.shard_map(body, mesh=mesh, in_specs=in_specs, out_specs=out_specs, check_vma=False)
```

profile of v0, /device:TPU:17, one launch (start us, length us, event | category | flops | bytes accessed | tf_op | source)
XLA Modules:
  0.0 4291.1 jit_solution(4192066588937546015)
XLA Ops:
  9.6 156.5 %all-gather = bf16[128,16,2]{1,2,0:T(2,128)(2,1)S(1)} all-gather(bf16[1,16,2]{1,2,0:T(2,128)(2,1)S(1)} %convert_bitcast_fusion.1), channel_id=1, replica_groups=mesh['fsdp'=8,'ctx'=16] {'fsdp','ctx'}, dimensions={0}, use_global_device_ids=true | all-gather | bytes 8256 | tf_op jit(solution)/shard_map/all_gather | solution.py:134
  167.5 50.4 %all-gather.8.cloned.1.call-done = bf16[2048,2560]{1,0:T(8,128)(2,1)} async-done(((bf16[16,2560]{1,0:T(8,128)(2,1)}), bf16[2048,2560]{1,0:T(8,128)(2,1)}) %all-gather.8.cloned.1.call-update) | async-done | bytes 10485776 | tf_op jit(solution)/shard_map/all_gather | solution.py:130
  231.7 27.0 all-gather.10.cloned.1.call-done
  266.2 14.6 fusion.16
  280.8 15.1 fusion.17
  296.5 15.7 fusion.39
  312.2 150.3 %all-gather.12.cloned.1.call-done = bf16[2048,2048]{1,0:T(8,128)(2,1)} async-done(((bf16[16,2048]{1,0:T(8,128)(2,1)}), bf16[2048,2048]{1,0:T(8,128)(2,1)}) %all-gather.12.cloned.1.call-update) | async-done | bytes 8388624 | tf_op jit(solution)/shard_map/all_gather | solution.py:131
  467.5 223.3 %all-gather.16.cloned.1.call-done = bf16[128,44,2048]{2,1,0:T(8,128)(2,1)} async-done(((bf16[1,44,2048]{2,1,0:T(8,128)(2,1)}), bf16[128,44,2048]{2,1,0:T(8,128)(2,1)}) %all-gather.16.cloned.1.call-update) | async-done | bytes 23068688 | tf_op jit(solution)/shard_map/all_gather | solution.py:133
  690.8 30.4 reshape.425
  721.2 230.9 %all-gather.14.cloned.1.call-done = bf16[2048,11264]{1,0:T(8,128)(2,1)} async-done(((bf16[16,11264]{1,0:T(8,128)(2,1)}), bf16[2048,11264]{1,0:T(8,128)(2,1)}) %all-gather.14.cloned.1.call-update) | async-done | bytes 46137360 | tf_op jit(solution)/shard_map/all_gather | solution.py:132
  952.1 20.2 fusion.77
  972.2 14.9 multiply_convert_fusion.1
  987.1 22.9 multiply_reduce_fusion
  1012.5 7.1 convolution_convert_fusion.1
  1023.0 264.4 %while.21 = (s32[]{:T(128)}, bf16[128,512]{0,1:T(8,128)(2,1)}, f32[128,512]{0,1:T(8,128)S(1)}, f32[128,4,8,64]{0,3,2,1:T(8,128)S(1)}, s32[]{:T(128)}, /*index=5*...) while((s32[]{:T(128)}, bf16[128,512]{0,1:T(8,128)(2,1)}, ...), condition=%wide.region_14.15_spmd.clone, body=%wide.region_11.14_spmd.clone.sunk | while | flops 340447616 | bytes 17046320 | solution.py:260
  1129.0 6.4 collective-permute-done.1
  1287.6 8.8 fusion.36
  1297.9 8.2 fusion.44
  1307.1 8.9 fusion.41
  1316.6 33.8 fusion.24
  1351.5 19.2 fusion.85
  1370.7 546.0 %fusion.2 = f32[48,2048]{1,0:T(8,128)S(1)} fusion(f32[5632,2048]{1,0:T(8,128)} %fusion.85), kind=kCustom, calls=%all-reduce-scatter | all-reduce-scatter fusion | flops 12582913 | bytes 46530560
  1922.7 9.7 collective-permute-start.10
  1937.7 6.4 collective-permute-start.8
  1946.0 12.0 fusion.23
  1968.2 18.5 collective-permute-start.4
  1999.4 18.9 collective-permute-done.4
  2019.8 6.4 collective-permute-done.2
  2026.3 30.9 concatenate.22
  2059.6 498.5 %reduce-scatter.11.cloned.1.call-done = f32[16,2048]{1,0:T(8,128)} async-done(((f32[2048,2048]{1,0:T(8,128)}), f32[16,2048]{1,0:T(8,128)}) %reduce-scatter.11.cloned.1.call-update) | async-done | bytes 131088 | tf_op jit(solution)/shard_map/reduce_scatter | solution.py:276
  2560.0 653.2 %reduce-scatter.9.cloned.1.call-done = f32[16,2560]{1,0:T(8,128)} async-done(((f32[2048,2560]{1,0:T(8,128)}), f32[16,2560]{1,0:T(8,128)}) %reduce-scatter.9.cloned.1.call-update) | async-done | bytes 163856 | tf_op jit(solution)/shard_map/reduce_scatter | solution.py:275
  3215.0 1066.5 %reduce-scatter.13.cloned.1.call-done = f32[16,11264]{1,0:T(8,128)} async-done(((f32[2048,11264]{1,0:T(8,128)}), f32[16,11264]{1,0:T(8,128)}) %reduce-scatter.13.cloned.1.call-update) | async-done | bytes 720912 | tf_op jit(solution)/shard_map/reduce_scatter | solution.py:199
  (496 shorter events, 343.1 us)
Async XLA Ops:
  7.2 210.7 %all-gather.8.cloned.1.call-start = ((), (), s32[]{:S(2)}) async-start(), calls=%async_computation.4 | async-start | bytes 10567680 | tf_op jit(solution)/shard_map/all_gather | solution.py:130
  8.8 249.9 %all-gather.10.cloned.1.call-start = ((), (), s32[]{:S(2)}) async-start(), calls=%async_computation.5 | async-start | bytes 2228224 | tf_op jit(solution)/shard_map/all_gather | solution.py:146
  224.4 238.1 %all-gather.12.cloned.1.call-start = ((), (), s32[]{:S(2)}) async-start(), calls=%async_computation.6 | async-start | bytes 8454144 | tf_op jit(solution)/shard_map/all_gather | solution.py:131
  225.1 465.7 %all-gather.16.cloned.1.call-start = ((), (), s32[]{:S(2)}) async-start(), calls=%async_computation.11 | async-start | bytes 25362432 | tf_op jit(solution)/shard_map/all_gather | solution.py:133
  225.9 726.1 %all-gather.14.cloned.1.call-start = ((), (), s32[]{:S(2)}) async-start(), calls=%async_computation.7 | async-start | bytes 46497792 | tf_op jit(solution)/shard_map/all_gather | solution.py:132
  226.8 1766.5 %reduce-scatter.15.cloned.1.call-start = ((), (), s32[]{:S(2)}) async-start(), calls=%async_computation.12 | async-start | bytes 1056768
  1053.3 15.9 collective-permute-start
  1070.1 15.9 collective-permute-start
  1086.9 15.9 collective-permute-start
  1103.7 15.9 collective-permute-start
  1120.5 15.9 collective-permute-start
  1137.3 15.9 collective-permute-start
  1170.8 15.9 collective-permute-start
  1187.6 15.9 collective-permute-start
  1204.4 15.9 collective-permute-start
  1221.2 15.9 collective-permute-start
  1238.0 15.9 collective-permute-start
  1271.6 15.9 collective-permute-start
  1297.8 1260.3 %reduce-scatter.11.cloned.1.call-start = ((), (), s32[]{:S(2)}) async-start(), calls=%async_computation.9 | async-start | bytes 16908288 | tf_op jit(solution)/shard_map/reduce_scatter | solution.py:276
  1306.0 1907.2 %reduce-scatter.9.cloned.1.call-start = ((), (), s32[]{:S(2)}) async-start(), calls=%async_computation.8 | async-start | bytes 21135360 | tf_op jit(solution)/shard_map/reduce_scatter | solution.py:275
  1316.0 2965.6 %reduce-scatter.13.cloned.1.call-start = ((), (), s32[]{:S(2)}) async-start(), calls=%async_computation.10 | async-start | bytes 92995584 | tf_op jit(solution)/shard_map/reduce_scatter | solution.py:199
  1917.4 26.7 collective-permute-start.12
  1920.6 37.4 collective-permute-start.11
  1922.7 38.8 collective-permute-start.10
  1932.4 35.7 collective-permute-start.9
  1937.7 49.0 %collective-permute-start.8 = (f32[48,2048]{1,0:T(8,128)S(1)}, f32[48,2048]{1,0:T(8,128)S(1)}, u32[]{:S(2)}, u32[]{:S(2)}) collective-permute-start(f32[48,2048]{1,0:T(8,128)S(1)} %fusion.2), channel_id=1, source_target_pairs={{0,7},{1,8},{2,9},{3,10},{4,11},{5,12},{6,13},{7,14},{8,15},{9,16}... | collective-permute-start | bytes 1179656
  1944.1 44.5 %collective-permute-start.7 = (f32[48,2048]{1,0:T(8,128)S(1)}, f32[48,2048]{1,0:T(8,128)S(1)}, u32[]{:S(2)}, u32[]{:S(2)}) collective-permute-start(f32[48,2048]{1,0:T(8,128)S(1)} %fusion.2), channel_id=1, source_target_pairs={{0,6},{1,7},{2,8},{3,9},{4,10},{5,11},{6,12},{7,13},{8,14},{9,15},... | collective-permute-start | bytes 1179656
  1958.1 41.1 collective-permute-start.6
  1961.5 37.9 collective-permute-start.5
  1968.2 50.2 %collective-permute-start.4 = (f32[48,2048]{1,0:T(8,128)S(1)}, f32[48,2048]{1,0:T(8,128)}, u32[]{:S(2)}, u32[]{:S(2)}) collective-permute-start(f32[48,2048]{1,0:T(8,128)S(1)} %fusion.2), channel_id=1, source_target_pairs={{0,3},{1,4},{2,5},{3,6},{4,7},{5,8},{6,9},{7,10},{8,11},{9,12},{10... | collective-permute-start | bytes 1179656
  1986.7 33.1 collective-permute-start.3
  1988.7 37.6 collective-permute-start.2
  (72 other events, 11528.3 us)
Sparse Core Ops, SparseCore 0:
  10.3 207.4 all-gather.7
  224.5 34.1 all-gather.9
  261.0 201.4 all-gather.11
  464.7 226.0 all-gather.15
  693.0 259.0 all-gather.13
  1297.9 560.0 reduce-scatter.14
  1860.5 697.6 reduce-scatter.10
  2560.7 652.4 reduce-scatter.8
  3215.8 1065.7 reduce-scatter.12
where the time goes:
time: 4300 us; the launch traced here: 4290 us
  waiting for transfers between devices  3030 us (70%)
  blocking collectives  703 us (16%)
  matrix products  264 us (6%)
  other arithmetic  111 us (3%)
  local copies, waits for them, and re-layouts  105 us (2%)
  starting transfers between devices  66.1 us (2%)
    reduce_scatter x1, waiting for transfers between devices, body(): lax.psum_scatter(grad_gu_term, ('fsdp', 'ctx'), scatter_dimension=0, tile...  1070 us
    reduce_scatter x1, waiting for transfers between devices, body(): lax.psum_scatter(grad_qkv_term, ('fsdp', 'ctx'), scatter_dimension=0, til...  653 us
    unnamed x1, blocking collectives  546 us
    reduce_scatter x1, waiting for transfers between devices, body(): lax.psum_scatter(grad_out_term, ('fsdp', 'ctx'), scatter_dimension=0, til...  499 us
    all_gather x1, waiting for transfers between devices, body(): lax.all_gather(shards[2], ('fsdp', 'ctx'), axis=0, tiled=True)  231 us
    all_gather x1, waiting for transfers between devices, body(): lax.all_gather(shards[3], ('fsdp', 'ctx'), axis=0, tiled=True)  223 us
    all_gather x1, blocking collectives, body(): lax.all_gather(shards[4], ('fsdp', 'ctx'), axis=1, tiled=True)  157 us
    all_gather x1, waiting for transfers between devices, body(): lax.all_gather(shards[1], ('fsdp', 'ctx'), axis=0, tiled=True)  150 us
  transfers between devices with their start and end apart: 52, of which 30 were waited for; matrix products, arithmetic and copies ran while one was open for 21% of the time, Pallas kernels for 0%

commit v1 on v0

v1 whole, which is shorter than its diff:
```python
import jax
import jax.numpy as jnp
from jax import lax
from jax.experimental import pallas as pl
from jax.experimental.pallas import tpu as pltpu
from jax.sharding import Mesh
from jax.sharding import PartitionSpec as P

BF = jnp.bfloat16
F32 = jnp.float32
ALL = ("y", "zh", "x", "zl", "c")
TP = ("x", "c")
REP = ("y", "zh", "zl")

FF = 5632
FT = 704
FP = 768
HD = 64
STEP = 10
ROWS = 1024
KEYS = 2048

norm_eps = 1e-05
beta_one = 0.9
beta_two = 0.95
adam_eps = 1e-08
big_negative = -1e30
step_rates = (0.15, 0.3, 0.06, 0.04, 2.0)
decay_rates = (0.1, 0.1, 0.1, 0.1, 0.0)


def flat_index(f, x, zl, c):
    return ((f * 4 + x) * 2 + zl) * 2 + c


NATURAL = [
    (flat_index(f, 2 * h + a, b, c), flat_index(f, 2 * a + b, h, c))
    for f in range(8)
    for h in range(2)
    for a in range(2)
    for b in range(2)
    for c in range(2)
]
SPREAD = [
    (t * 16 + k, flat_index(k // 2, t // 2, k % 2, t % 2)) for t in range(8) for k in range(16)
]


def back(route):
    return [(b, a) for a, b in route]


def adam_update(master, grad_sum, first_old, second_old, step_rate, decay_rate):
    first_new = beta_one * first_old + (1.0 - beta_one) * grad_sum
    second_new = beta_two * second_old + (1.0 - beta_two) * grad_sum * grad_sum
    first_fix = first_new / (1.0 - beta_one**STEP)
    second_fix = second_new / (1.0 - beta_two**STEP)
    master_new = master - step_rate * (
        first_fix / (jnp.sqrt(second_fix) + adam_eps) + decay_rate * master
    )
    return (first_new, second_new, master_new)


def dot_nn(a, b):
    return lax.dot_general(a, b, (((1,), (0,)), ((), ())), preferred_element_type=F32)


def dot_nt(a, b):
    return lax.dot_general(a, b, (((1,), (1,)), ((), ())), preferred_element_type=F32)


def dot_tn(a, b):
    return lax.dot_general(a, b, (((0,), (0,)), ((), ())), preferred_element_type=F32)


QB = 256


def attend_kernel(q_ref, k_ref, vt_ref, kp_ref, lo_ref, hi_ref, o_ref, lse_ref):
    key_pos = kp_ref[...]
    high = hi_ref[...]
    allowed = (key_pos >= lo_ref[...]) & (key_pos <= high)
    keys = k_ref[...]
    for h in range(4):
        cols = slice(h * HD, (h + 1) * HD)
        s = jnp.where(allowed, dot_nt(keys, q_ref[:, cols]), big_negative)
        peak = jnp.max(s, axis=0, keepdims=True)
        p = jnp.exp(s - peak)
        total = jnp.sum(p, axis=0, keepdims=True)
        out = dot_nn(vt_ref[...], p.astype(BF))
        out = out * jnp.where(high >= 0, 1.0 / total, 0.0)
        o_ref[:, cols] = out.T.astype(BF)
        lse_ref[h : h + 1, :] = peak + jnp.log(total)


def attend(q, k, vt, kp, lo, hi):
    whole = lambda shape: pl.BlockSpec(shape, lambda i: (0, 0))
    row = pl.BlockSpec((1, QB), lambda i: (0, i))
    block = pl.BlockSpec((QB, 256), lambda i: (i, 0))
    return pl.pallas_call(
        attend_kernel,
        grid=(ROWS // QB,),
        in_specs=[block, whole((KEYS, HD)), whole((HD, KEYS)), whole((KEYS, QB)), row, row],
        out_specs=[block, pl.BlockSpec((4, QB), lambda i: (0, i))],
        out_shape=[
            jax.ShapeDtypeStruct((ROWS, 256), BF),
            jax.ShapeDtypeStruct((4, ROWS), F32),
        ],
        compiler_params=pltpu.CompilerParams(vmem_limit_bytes=40 * 1024 * 1024),
        cost_estimate=pl.CostEstimate(
            flops=4 * 4 * ROWS * KEYS * HD, bytes_accessed=8 << 20, transcendentals=4 * ROWS * KEYS
        ),
        name="attend",
    )(q, k, vt, kp, lo, hi)


def attend_back_kernel(
    q_ref, do_ref, o_ref, k_ref, kt_ref, v_ref, kp_ref, lo_ref, hi_ref, lse_ref, dq_ref, dk_ref, dv_ref
):
    @pl.when(pl.program_id(0) == 0)
    def _():
        dk_ref[...] = jnp.zeros_like(dk_ref)
        dv_ref[...] = jnp.zeros_like(dv_ref)

    key_pos = kp_ref[...]
    allowed = (key_pos >= lo_ref[...]) & (key_pos <= hi_ref[...])
    keys = k_ref[...]
    values = v_ref[...]
    delta_all = (do_ref[...].astype(F32) * o_ref[...].astype(F32)).T
    for h in range(4):
        cols = slice(h * HD, (h + 1) * HD)
        qh = q_ref[:, cols]
        doh = do_ref[:, cols]
        delta = jnp.sum(delta_all[cols], axis=0, keepdims=True)
        s = dot_nt(keys, qh)
        p = jnp.where(allowed, jnp.exp(s - lse_ref[h : h + 1, :]), 0.0)
        ds = (p * (dot_nt(values, doh) - delta)).astype(BF)
        dv_ref[...] += dot_nn(p.astype(BF), doh)
        dk_ref[...] += dot_nn(ds, qh)
        dq_ref[:, cols] = (dot_nn(kt_ref[...], ds) * HD**-0.5).T.astype(BF)


def attend_back(q, do, o, k, kt, v, kp, lo, hi, lse):
    whole = lambda shape: pl.BlockSpec(shape, lambda i: (0, 0))
    row = pl.BlockSpec((1, QB), lambda i: (0, i))
    block = pl.BlockSpec((QB, 256), lambda i: (i, 0))
    return pl.pallas_call(
        attend_back_kernel,
        grid=(ROWS // QB,),
        in_specs=[
            block,
            block,
            block,
            whole((KEYS, HD)),
            whole((HD, KEYS)),
            whole((KEYS, HD)),
            whole((KEYS, QB)),
            row,
            row,
            pl.BlockSpec((4, QB), lambda i: (0, i)),
        ],
        out_specs=[block, whole((KEYS, HD)), whole((KEYS, HD))],
        out_shape=[
            jax.ShapeDtypeStruct((ROWS, 256), BF),
            jax.ShapeDtypeStruct((KEYS, HD), F32),
            jax.ShapeDtypeStruct((KEYS, HD), F32),
        ],
        compiler_params=pltpu.CompilerParams(vmem_limit_bytes=48 * 1024 * 1024),
        cost_estimate=pl.CostEstimate(
            flops=10 * 4 * ROWS * KEYS * HD, bytes_accessed=8 << 20, transcendentals=4 * ROWS * KEYS
        ),
        name="attend_back",
    )(q, do, o, k, kt, v, kp, lo, hi, lse)


def gather_rows(block):
    return lax.all_gather(block, TP, axis=0, tiled=True)


def scatter_rows(partial):
    return lax.psum_scatter(partial, TP, scatter_dimension=0, tiled=True).astype(F32)


def row_positions(span_order, zl):
    spans = lax.dynamic_index_in_dim(span_order.reshape(4, 2, 4), zl, axis=1, keepdims=False)
    return (spans.reshape(16, 1) * 64 + jnp.arange(64, dtype=jnp.int32)[None, :]).reshape(ROWS)


def norm_scale(rows):
    return lax.rsqrt(jnp.mean(rows * rows, axis=-1, keepdims=True) + norm_eps)


def norm_back(grad_hat, hat, scale, rest):
    return rest + scale * (grad_hat - hat * jnp.mean(grad_hat * hat, axis=-1, keepdims=True))


def body(
    tokens,
    out_grad,
    seq_lengths,
    span_order,
    attn_in,
    attn_out,
    gate_up,
    down_proj,
    norm_gains,
    first_attn_in,
    second_attn_in,
    first_attn_out,
    second_attn_out,
    first_gate_up,
    second_gate_up,
    first_down_proj,
    second_down_proj,
    first_norm_gains,
    second_norm_gains,
):
    zl = lax.axis_index("zl")
    gains = norm_gains.astype(BF).astype(F32)
    gain_one = gains[0][:, None]
    gain_two = gains[1][:, None]
    low_qkv = attn_in.astype(BF).astype(F32)
    low_gu = gate_up.astype(BF).astype(F32)

    scaled_qkv = (low_qkv * gain_one).astype(BF)
    kv_cols = scaled_qkv[:, 2048:].reshape(16, 2, 4, 1, HD)
    kv_cols = jnp.broadcast_to(kv_cols, (16, 2, 4, 2, HD)).reshape(16, 2, 8, HD)
    qkv_cols = jnp.concatenate(
        [scaled_qkv[:, :2048].reshape(16, 8, 256), kv_cols[:, 0], kv_cols[:, 1]], axis=2
    ).transpose(1, 0, 2)
    gu_cols = (low_gu * gain_two).astype(BF).reshape(16, 2, 8, FT)
    gu_cols = jnp.pad(gu_cols, ((0, 0), (0, 0), (0, 0), (0, FP - FT)))
    gu_cols = gu_cols.transpose(2, 0, 1, 3).reshape(8, 16, 2 * FP)

    def to_rank(cols):
        moved = lax.ppermute(cols, ALL, NATURAL)
        return lax.all_to_all(moved, TP, 0, 0, tiled=True).reshape(128, cols.shape[2])

    qkv_part = to_rank(qkv_cols)
    gu_part = to_rank(gu_cols)
    out_part = lax.ppermute(attn_out.astype(BF), ALL, SPREAD)
    down_part = lax.ppermute(down_proj.astype(BF), ALL, SPREAD)
    w_qkv = lax.all_gather(qkv_part, REP, axis=0, tiled=True)
    w_out = lax.all_gather(out_part, REP, axis=0, tiled=True)
    w_gu = lax.all_gather(gu_part, REP, axis=0, tiled=True)
    w_down = lax.all_gather(down_part, REP, axis=0, tiled=False).reshape(FT, 2048)

    own_pos = row_positions(span_order, zl)
    other_pos = row_positions(span_order, 1 - zl)
    lengths = seq_lengths[0]
    bound_one = lengths[0]
    bound_two = lengths[0] + lengths[1]
    low_pos = jnp.where(own_pos < bound_one, 0, bound_one)[None, :]
    high_pos = jnp.where(own_pos < bound_two, own_pos, -1)[None, :]
    key_pos = jnp.concatenate([own_pos, other_pos])
    key_pos = jnp.broadcast_to(key_pos[:, None], (KEYS, QB))

    inputs = tokens.astype(F32)
    scale_one = norm_scale(inputs)
    hat_one = inputs * scale_one
    all_hat_one = gather_rows(hat_one.astype(BF))
    all_grad = gather_rows(out_grad)
    projected = dot_nn(all_hat_one, w_qkv).astype(BF)
    queries = projected[:, :256] * BF(HD**-0.5)
    own_kv = projected[:, 256:]
    other_kv = lax.ppermute(own_kv, "zl", [(0, 1), (1, 0)])
    kv = jnp.concatenate([own_kv, other_kv], axis=0)
    keys = kv[:, :HD]
    values = kv[:, HD:]
    att, lse = attend(queries, keys, values.T, key_pos, low_pos, high_pos)
    hidden = inputs + scatter_rows(dot_nn(att, w_out).astype(BF))

    scale_two = norm_scale(hidden)
    hat_two = hidden * scale_two
    all_hat_two = gather_rows(hat_two.astype(BF))
    w_gate = w_gu[:, :FT]
    w_up = w_gu[:, FP : FP + FT]
    gate = dot_nn(all_hat_two, w_gate)
    up = dot_nn(all_hat_two, w_up)
    sig = jax.nn.sigmoid(gate)
    silu = gate * sig
    hid = (silu * up).astype(BF)
    block_out = (hidden + scatter_rows(dot_nn(hid, w_down).astype(BF))).astype(BF)

    grad_hid = dot_nt(all_grad, w_down)
    grad_gate = (grad_hid * up * sig * (1.0 + gate * (1.0 - sig))).astype(BF)
    grad_up = (grad_hid * silu).astype(BF)
    grad_hat_two = scatter_rows((dot_nt(grad_gate, w_gate) + dot_nt(grad_up, w_up)).astype(BF))
    sum_down = dot_tn(hid, all_grad).astype(BF)
    grad_gu = jnp.concatenate(
        [
            jnp.pad(grad_gate, ((0, 0), (0, FP - FT))),
            jnp.pad(grad_up, ((0, 0), (0, FP - FT))),
        ],
        axis=1,
    )
    sum_gu = dot_tn(all_hat_two, grad_gu).astype(BF)
    sum_gu = lax.psum_scatter(sum_gu, REP, scatter_dimension=0, tiled=True)
    sum_down = lax.psum_scatter(sum_down.reshape(16, 44, 2048), REP, scatter_dimension=0, tiled=False)

    grad_hidden = norm_back(grad_hat_two, hat_two, scale_two, out_grad.astype(F32))
    all_grad_hidden = gather_rows(grad_hidden.astype(BF))
    grad_att = dot_nt(all_grad_hidden, w_out).astype(BF)
    sum_out = dot_tn(att, all_grad_hidden).astype(BF)
    sum_out = lax.psum_scatter(sum_out, REP, scatter_dimension=0, tiled=True)

    grad_q, grad_k, grad_v = attend_back(
        queries, grad_att, att, keys, keys.T, values, key_pos, low_pos, high_pos, lse
    )
    grad_kv = jnp.concatenate([grad_k, grad_v], axis=1)
    arrived = lax.ppermute(grad_kv[ROWS:].astype(BF), "zl", [(0, 1), (1, 0)])
    grad_mixed = jnp.concatenate(
        [grad_q, (grad_kv[:ROWS] + arrived.astype(F32)).astype(BF)], axis=1
    )
    grad_hat_one = scatter_rows(dot_nt(grad_mixed, w_qkv).astype(BF))
    in_grad = norm_back(grad_hat_one, hat_one, scale_one, grad_hidden).astype(BF)
    sum_qkv = dot_tn(all_hat_one, grad_mixed).astype(BF)
    sum_qkv = lax.psum_scatter(sum_qkv, REP, scatter_dimension=0, tiled=True)

    def to_shard(rows):
        mixed = lax.all_to_all(rows.reshape(8, 16, rows.shape[1]), TP, 0, 0, tiled=True)
        return lax.ppermute(mixed, ALL, back(NATURAL)).astype(F32)

    got_gu = to_shard(sum_gu).reshape(8, 16, 2, FP)[..., :FT]
    got_gu = got_gu.transpose(1, 2, 0, 3).reshape(16, 2 * FF)
    got_qkv = to_shard(sum_qkv).transpose(1, 0, 2)
    got_kv = got_qkv[:, :, 256:].reshape(16, 4, 2, 2, HD).sum(axis=2)
    got_qkv = jnp.concatenate(
        [
            got_qkv[:, :, :256].reshape(16, 2048),
            got_kv[:, :, 0].reshape(16, 256),
            got_kv[:, :, 1].reshape(16, 256),
        ],
        axis=1,
    )
    got_out = lax.ppermute(sum_out, ALL, back(SPREAD)).astype(F32)
    got_down = lax.ppermute(sum_down, ALL, back(SPREAD)).astype(F32)
    gain_sums = jnp.stack(
        [jnp.sum(low_qkv * got_qkv, axis=1), jnp.sum(low_gu * got_gu, axis=1)], axis=0
    )
    qkv_new = adam_update(
        attn_in, got_qkv * gain_one, first_attn_in, second_attn_in, step_rates[0], decay_rates[0]
    )
    out_new = adam_update(
        attn_out, got_out, first_attn_out, second_attn_out, step_rates[1], decay_rates[1]
    )
    gu_new = adam_update(
        gate_up, got_gu * gain_two, first_gate_up, second_gate_up, step_rates[2], decay_rates[2]
    )
    down_new = adam_update(
        down_proj, got_down, first_down_proj, second_down_proj, step_rates[3], decay_rates[3]
    )
    gains_new = adam_update(
        norm_gains, gain_sums, first_norm_gains, second_norm_gains, step_rates[4], decay_rates[4]
    )
    return (block_out, in_grad, *qkv_new, *out_new, *gu_new, *down_new, *gains_new)


def solution(mesh):
    split = Mesh(mesh.devices.reshape(4, 2, 4, 2, 2), ALL)
    rows = P(ALL, None)
    cols = P(None, ALL)
    group = P(("y", "zh"), None)
    in_specs = (rows, rows, group, P()) + (rows,) * 4 + (cols,) + (rows,) * 8 + (cols,) * 2
    out_specs = (rows,) * 14 + (cols,) * 3
    return jax.shard_map(body, mesh=split, in_specs=in_specs, out_specs=out_specs, check_vma=False)
```

time: 4300 us -> 905 us (0.21)
  waiting for transfers between devices: 3030 us -> 596 us
  blocking collectives: 703 us -> 47.9 us
  matrix products: 264 us -> 80 us
  local copies, waits for them, and re-layouts: 105 us -> 19.3 us
  other arithmetic: 111 us -> 29.2 us
  Pallas kernels: 0 us -> 47.1 us
    reduce_scatter x3 -> x7, waiting for transfers between devices: 2220 us -> 246 us  [the longest x4 95.2 us: scatter_rows(): lax.psum_scatter(partial, TP, scatter_dimension=0, tiled=True).astype(F32)]
    unnamed x1 -> x0, blocking collectives: 546 us -> none
    all_gather x5 -> x8, waiting for transfers between devices: 682 us -> 244 us  [the longest x4 112 us: gather_rows(): return lax.all_gather(block, TP, axis=0, tiled=True)]
    dot_general x94 -> x14, matrix products: 264 us -> 80 us  [the longest x5 28.3 us: dot_nn(): lax.dot_general(a, b, (((1,), (0,)), ((), ())), preferred_element_type=F32)]
    all_gather x1 -> x0, blocking collectives: 157 us -> none  [body(): lax.all_gather(shards[4], ('fsdp', 'ctx'), axis=1, tiled=True)]
    unnamed x79, local copies, waits for them, and re-layouts: 69.6 us -> 9.68 us
    unnamed x12 -> x1, starting transfers between devices: 58.3 us -> 0.04 us
    ppermute x32 -> x10, waiting for transfers between devices: 89.8 us -> 33.6 us  [the longest x1 11.1 us: body(): arrived = lax.ppermute(grad_kv[ROWS:].astype(BF), 'zl', [(0, 1), (1, 0)])]
  transfers between devices with their start and end apart: 52 -> 28, of which waited for: 30 -> 21; matrix products, arithmetic and copies ran while one was open for 21% -> 10% of each run, Pallas kernels for 0% -> 5%
where the time goes in v1:
time: 905 us; the launch traced here: 891 us
  waiting for transfers between devices  596 us (66%)
  matrix products  80 us (9%)
  starting transfers between devices  55.5 us (6%)
  blocking collectives  47.9 us (5%)
  Pallas kernels  47.1 us (5%)
  other arithmetic  29.2 us (3%)
  local copies, waits for them, and re-layouts  19.3 us (2%)
  between operations  16.4 us (2%)
    all_gather x4, waiting for transfers between devices, gather_rows(): return lax.all_gather(block, TP, axis=0, tiled=True)  112 us
    reduce_scatter x4, waiting for transfers between devices, scatter_rows(): lax.psum_scatter(partial, TP, scatter_dimension=0, tiled=True).astype(F32)  95.2 us
    unnamed x17, waiting for transfers between devices  71.9 us
    reduce_scatter x1, waiting for transfers between devices, body(): sum_qkv = lax.psum_scatter(sum_qkv, REP, scatter_dimension=0, tiled=True)  66.6 us
    reduce_scatter x1, waiting for transfers between devices, body(): sum_out = lax.psum_scatter(sum_out, REP, scatter_dimension=0, tiled=True)  62.8 us
    all_gather x1, waiting for transfers between devices, body(): w_gu = lax.all_gather(gu_part, REP, axis=0, tiled=True)  55.3 us
    all_gather x1, waiting for transfers between devices, body(): lax.all_gather(down_part, REP, axis=0, tiled=False).reshape(FT, 2048)  48.1 us
    all_to_all x2, blocking collectives, to_rank(): lax.all_to_all(moved, TP, 0, 0, tiled=True).reshape(128, cols.shape[2])  47.9 us
  transfers between devices with their start and end apart: 28, of which 21 were waited for; matrix products, arithmetic and copies ran while one was open for 10% of the time, Pallas kernels for 5%

profile of v1, /device:TPU:17, one launch (start us, length us, event | category | flops | bytes accessed | tf_op | source)
XLA Modules:
  0.0 891.4 jit_solution(6632378668554001969)
XLA Ops:
  10.0 17.8 %all_to_all.20 = bf16[8,16,384]{2,1,0:T(8,128)(2,1)} all-to-all(bf16[8,16,384]{2,1,0:T(8,128)(2,1)S(1)} %copy.62), channel_id=1, replica_groups=mesh['y'=4,'zh'=2,'x'=4,'zl'=2,'c'=2] {'x','c'}, dimensions={0} | all-to-all | bytes 196608 | tf_op jit(solution)/shard_map/all_to_all | solution.py:237
  34.9 8.4 collective-permute-done.2
  47.0 23.1 %all-gather.13.cloned.1.call-done = bf16[2048,384]{1,0:T(8,128)(2,1)} async-done(((bf16[128,384]{1,0:T(8,128)(2,1)}), bf16[2048,384]{1,0:T(8,128)(2,1)}) %all-gather.13.cloned.1.call-update) | async-done | bytes 1572880 | tf_op jit(solution)/shard_map/all_gather | solution.py:243
  70.1 36.4 %all-gather.11.cloned.1.call-done = bf16[1024,2048]{1,0:T(8,128)(2,1)} async-done(((bf16[128,2048]{1,0:T(8,128)(2,1)}), bf16[1024,2048]{1,0:T(8,128)(2,1)}) %all-gather.11.cloned.1.call-update) | async-done | bytes 4194320 | tf_op jit(solution)/shard_map/all_gather | solution.py:177
  121.8 21.6 %attend.1 = (bf16[1024,256]{1,0:T(8,128)(2,1)S(1)}, f32[4,1024]{1,0:T(4,128)S(1)}) custom-call(bf16[1024,256]{1,0:T(8,128)(2,1)S(1)} %copy-done.1, bf16[2048,64]{1,0:T(8,128)(2,1)S(1)} %get-tuple-element.52.k_ref, bf16[64,2048]{1,0:T(8,128)(2,1)S(1)} %copy.63.vt_ref, s32[2048,256]{1,0:T(8,128)S(1)} %broadcast_in_dim.18.kp_ref, ...), custom_call_target="tpu_custom_call" | custom-call | flops 2147483648 | bytes 8388608 | tf_op jit(solution)/shard_map/attend/pallas_call | solution.py:100
  154.7 8.3 collective-permute-start.4
  163.1 7.4 collective-permute-done.4
  174.1 30.1 %all_to_all.21 = bf16[8,16,1536]{2,1,0:T(8,128)(2,1)} all-to-all(bf16[8,16,1536]{2,1,0:T(8,128)(2,1)S(1)} %collective-permute-done.3), channel_id=1, replica_groups=mesh['y'=4,'zh'=2,'x'=4,'zl'=2,'c'=2] {'x','c'}, dimensions={0} | all-to-all | bytes 786432 | tf_op jit(solution)/shard_map/all_to_all | solution.py:237
  208.2 48.1 %all-gather.25.cloned.1.call-done = bf16[16,44,2048]{2,1,0:T(8,128)(2,1)} async-done(((bf16[1,44,2048]{2,1,0:T(8,128)(2,1)}), bf16[16,44,2048]{2,1,0:T(8,128)(2,1)}) %all-gather.25.cloned.1.call-update) | async-done | bytes 2883600 | tf_op jit(solution)/shard_map/all_gather | solution.py:246
  260.6 29.7 %all-gather.21.cloned.1.call-done = bf16[1024,2048]{1,0:T(8,128)(2,1)} async-done(((bf16[128,2048]{1,0:T(8,128)(2,1)}), bf16[1024,2048]{1,0:T(8,128)(2,1)}) %all-gather.21.cloned.1.call-update) | async-done | bytes 4194320 | tf_op jit(solution)/shard_map/all_gather | solution.py:177
  290.3 7.9 fusion.61
  298.2 55.3 %all-gather.19.cloned.1.call-done = bf16[2048,1536]{1,0:T(8,128)(2,1)} async-done(((bf16[128,1536]{1,0:T(8,128)(2,1)}), bf16[2048,1536]{1,0:T(8,128)(2,1)}) %all-gather.19.cloned.1.call-update) | async-done | bytes 6291472 | tf_op jit(solution)/shard_map/all_gather | solution.py:245
  353.5 34.4 %all-gather.17.cloned.1.call-done = bf16[1024,2048]{1,0:T(8,128)(2,1)} async-done(((bf16[128,2048]{1,0:T(8,128)(2,1)}), bf16[1024,2048]{1,0:T(8,128)(2,1)}) %all-gather.17.cloned.1.call-update) | async-done | bytes 4194320 | tf_op jit(solution)/shard_map/all_gather | solution.py:177
  387.9 6.1 fusion.11
  394.9 5.8 multiply_convert_fusion.1
  409.6 34.4 %reduce-scatter.15.cloned.1.call-done = bf16[128,2048]{1,0:T(8,128)(2,1)} async-done(((bf16[1024,2048]{1,0:T(8,128)(2,1)}), bf16[128,2048]{1,0:T(8,128)(2,1)}) %reduce-scatter.15.cloned.1.call-update) | async-done | bytes 524304 | tf_op jit(solution)/shard_map/reduce_scatter | solution.py:181
  447.8 11.1 %convolution_convert_fusion = bf16[2048,1536]{1,0:T(8,128)(2,1)} fusion(bf16[1024,2048]{1,0:T(8,128)(2,1)} %all-gather.17.cloned.1.call-done, bf16[1024,704]{0,1:T(8,128)(2,1)} %copy-done.34, bf16[1024,704]{0,1:T(8,128)(2,1)} %get-tuple-element.44), kind=kOutput, calls=%fused_computation.1 | convolution fusion | flops 6458179584 | bytes 13369344 | tf_op jit(solution)/shard_map/dot_general | solution.py:73
  458.9 7.9 convolution_convert_fusion.4
  471.2 11.1 %all-gather.23.cloned.1.call-done = bf16[1024,2048]{1,0:T(8,128)(2,1)} async-done(((bf16[128,2048]{1,0:T(8,128)(2,1)}), bf16[1024,2048]{1,0:T(8,128)(2,1)}) %all-gather.23.cloned.1.call-update) | async-done | bytes 4194320 | tf_op jit(solution)/shard_map/all_gather | solution.py:177
  491.1 25.5 %attend_back.1 = (bf16[1024,256]{1,0:T(8,128)(2,1)S(1)}, f32[2048,64]{1,0:T(8,128)S(1)}, f32[2048,64]{1,0:T(8,128)S(1)}) custom-call(bf16[1024,256]{1,0:T(8,128)(2,1)S(1)} %copy-done.2, bf16[1024,256]{1,0:T(8,128)(2,1)S(1)} %convolution_convert_fusion.8.do_ref, bf16[1024,256]{1,0:T(8,128)(2,1)S(1)} %get-tuple-element.22.o_ref, ...), custom_call_target="tpu_custom_call" | custom-call | flops 5368709120 | bytes 8388608 | tf_op jit(solution)/shard_map/attend_back/pallas_call | solution.py:147
  518.2 11.1 %collective-permute-done.5 = bf16[1024,128]{1,0:T(8,128)(2,1)S(1)} collective-permute-done((bf16[1024,128]{1,0:T(8,128)(2,1)S(1)}, bf16[1024,128]{1,0:T(8,128)(2,1)S(1)}, u32[]{:S(2)}, u32[]{:S(2)}) %collective-permute-start.5) | collective-permute-done | bytes 262176 | tf_op jit(solution)/shard_map/ppermute | solution.py:311
  539.0 6.9 convolution_convert_fusion.2
  545.9 20.9 %reduce-scatter.23.cloned.1.call-done = bf16[128,1536]{1,0:T(8,128)(2,1)} async-done(((bf16[2048,1536]{1,0:T(8,128)(2,1)}), bf16[128,1536]{1,0:T(8,128)(2,1)}) %reduce-scatter.23.cloned.1.call-update) | async-done | bytes 393232 | tf_op jit(solution)/shard_map/reduce_scatter | solution.py:298
  566.8 6.0 all-to-all-start.3
  572.8 71.1 %reduce-scatter.25.cloned.1.call-done = bf16[1,44,2048]{2,1,0:T(8,128)(2,1)} async-done(((bf16[16,44,2048]{2,1,0:T(8,128)(2,1)}), bf16[1,44,2048]{2,1,0:T(8,128)(2,1)}) %reduce-scatter.25.cloned.1.call-update) | async-done | bytes 180240
  643.9 9.8 %collective-permute-start.9 = (bf16[44,2048]{1,0:T(8,128)(2,1)}, bf16[44,2048]{1,0:T(8,128)(2,1)S(1)}, u32[]{:S(2)}, u32[]{:S(2)}) collective-permute-start(bf16[44,2048]{1,0:T(8,128)(2,1)} %bitcast.79), channel_id=1, source_target_pairs={{0,0},{2,1},{16,2},{18,3},{32,4},{34,5},{48,6},{50,7},{64,8},{66,9... | collective-permute-start | bytes 540680 | tf_op jit(solution)/shard_map/ppermute | solution.py:337
  662.3 62.8 %reduce-scatter.21.cloned.1.call-done = bf16[16,2048]{1,0:T(8,128)(2,1)} async-done(((bf16[256,2048]{1,0:T(8,128)(2,1)}), bf16[16,2048]{1,0:T(8,128)(2,1)}) %reduce-scatter.21.cloned.1.call-update) | async-done | bytes 65552 | tf_op jit(solution)/shard_map/reduce_scatter | solution.py:305
  725.0 9.8 %collective-permute-start.7 = (bf16[16,2048]{1,0:T(8,128)(2,1)}, bf16[16,2048]{1,0:T(8,128)(2,1)}, u32[]{:S(2)}, u32[]{:S(2)}) collective-permute-start(bf16[16,2048]{1,0:T(8,128)(2,1)} %reduce-scatter.21.cloned.1.call-done), channel_id=1, source_target_pairs={{0,0},{2,1},{16,2},{18,3},{32,4},{34,5},{48,6},{50,7},{64,8},{66,9... | collective-permute-start | bytes 196616 | tf_op jit(solution)/shard_map/ppermute | solution.py:336
  734.8 66.6 %reduce-scatter.19.cloned.1.call-done = bf16[128,384]{1,0:T(8,128)(2,1)} async-done(((bf16[2048,384]{1,0:T(8,128)(2,1)}), bf16[128,384]{1,0:T(8,128)(2,1)}) %reduce-scatter.19.cloned.1.call-update) | async-done | bytes 98320 | tf_op jit(solution)/shard_map/reduce_scatter | solution.py:318
  801.5 7.1 all-to-all-start.2
  819.3 23.7 %reduce-scatter.17.cloned.1.call-done = bf16[128,2048]{1,0:T(8,128)(2,1)} async-done(((bf16[1024,2048]{1,0:T(8,128)(2,1)}), bf16[128,2048]{1,0:T(8,128)(2,1)}) %reduce-scatter.17.cloned.1.call-update) | async-done | bytes 524304 | tf_op jit(solution)/shard_map/reduce_scatter | solution.py:181
  844.4 37.0 %reduce-scatter.13.cloned.1.call-done = bf16[128,2048]{1,0:T(8,128)(2,1)} async-done(((bf16[1024,2048]{1,0:T(8,128)(2,1)}), bf16[128,2048]{1,0:T(8,128)(2,1)}) %reduce-scatter.13.cloned.1.call-update) | async-done | bytes 524304 | tf_op jit(solution)/shard_map/reduce_scatter | solution.py:181
  (207 shorter events, 111.7 us)
Async XLA Ops:
  7.2 62.9 %all-gather.13.cloned.1.call-start = ((), (), s32[]{:S(2)}) async-start(), calls=%async_computation.13 | async-start | bytes 1671168 | tf_op jit(solution)/shard_map/all_gather | solution.py:243
  9.3 0.7 collective-permute-start
  27.8 78.6 %all-gather.11.cloned.1.call-start = ((), (), s32[]{:S(2)}) async-start(), calls=%async_computation.12 | async-start | bytes 4718592 | tf_op jit(solution)/shard_map/all_gather | solution.py:177
  31.1 118.0 %all-gather.15.cloned.1.call-start = ((), (), s32[]{:S(2)}) async-start(), calls=%async_computation.14 | async-start | bytes 1114112 | tf_op jit(solution)/shard_map/all_gather | solution.py:244
  31.2 12.1 %collective-permute-start.2 = (bf16[16,2048]{1,0:T(8,128)(2,1)S(1)}, bf16[16,2048]{1,0:T(8,128)(2,1)S(1)}, u32[]{:S(2)}, u32[]{:S(2)}) collective-permute-start(bf16[16,2048]{1,0:T(8,128)(2,1)S(1)} %convert_element_type.130), channel_id=1, source_target_pairs={{0,0},{1,2},{2,16},{3,18},{4,32},{5,34},{6,48},{7,50},{8,64},{9,66... | collective-permute-start | bytes 196616 | tf_op jit(solution)/shard_map/ppermute | solution.py:241
  44.0 160.3 %reduce-scatter.11.cloned.1.call-start = ((), (), s32[]{:S(2)}) async-start(), calls=%async_computation.15 | async-start | bytes 4718592 | tf_op jit(solution)/shard_map/reduce_scatter | solution.py:181
  111.5 7.7 collective-permute-start.1
  153.7 102.6 %all-gather.25.cloned.1.call-start = ((), (), s32[]{:S(2)}) async-start(), calls=%async_computation.26 | async-start | bytes 3342336 | tf_op jit(solution)/shard_map/all_gather | solution.py:246
  154.7 15.8 %collective-permute-start.4 = (bf16[44,2048]{1,0:T(8,128)(2,1)S(1)}, bf16[44,2048]{1,0:T(8,128)(2,1)S(1)}, u32[]{:S(2)}, u32[]{:S(2)}) collective-permute-start(bf16[44,2048]{1,0:T(8,128)(2,1)S(1)} %convert_element_type.138), channel_id=1, source_target_pairs={{0,0},{1,2},{2,16},{3,18},{4,32},{5,34},{6,48},{7,50},{8,64},{9,66... | collective-permute-start | bytes 540680 | tf_op jit(solution)/shard_map/ppermute | solution.py:242
  171.2 119.1 %all-gather.21.cloned.1.call-start = ((), (), s32[]{:S(2)}) async-start(), calls=%async_computation.19 | async-start | bytes 4718592 | tf_op jit(solution)/shard_map/all_gather | solution.py:177
  171.8 181.7 %all-gather.19.cloned.1.call-start = ((), (), s32[]{:S(2)}) async-start(), calls=%async_computation.17 | async-start | bytes 6684672 | tf_op jit(solution)/shard_map/all_gather | solution.py:245
  173.4 0.7 collective-permute-start.3
  204.2 183.6 %all-gather.17.cloned.1.call-start = ((), (), s32[]{:S(2)}) async-start(), calls=%async_computation.16 | async-start | bytes 4718592 | tf_op jit(solution)/shard_map/all_gather | solution.py:177
  207.7 236.4 %reduce-scatter.15.cloned.1.call-start = ((), (), s32[]{:S(2)}) async-start(), calls=%async_computation.20 | async-start | bytes 4718592 | tf_op jit(solution)/shard_map/reduce_scatter | solution.py:181
  409.4 72.9 %all-gather.23.cloned.1.call-start = ((), (), s32[]{:S(2)}) async-start(), calls=%async_computation.21 | async-start | bytes 4718592 | tf_op jit(solution)/shard_map/all_gather | solution.py:177
  447.7 119.1 %reduce-scatter.23.cloned.1.call-start = ((), (), s32[]{:S(2)}) async-start(), calls=%async_computation.25 | async-start | bytes 6684672 | tf_op jit(solution)/shard_map/reduce_scatter | solution.py:298
  458.9 185.1 %reduce-scatter.25.cloned.1.call-start = ((), (), s32[]{:S(2)}) async-start(), calls=%async_computation.27 | async-start | bytes 3342336
  471.2 253.9 %reduce-scatter.21.cloned.1.call-start = ((), (), s32[]{:S(2)}) async-start(), calls=%async_computation.24 | async-start | bytes 1114112 | tf_op jit(solution)/shard_map/reduce_scatter | solution.py:305
  486.8 314.7 %reduce-scatter.19.cloned.1.call-start = ((), (), s32[]{:S(2)}) async-start(), calls=%async_computation.23 | async-start | bytes 1671168 | tf_op jit(solution)/shard_map/reduce_scatter | solution.py:318
  516.8 12.5 %collective-permute-start.5 = (bf16[1024,128]{1,0:T(8,128)(2,1)S(1)}, bf16[1024,128]{1,0:T(8,128)(2,1)S(1)}, u32[]{:S(2)}, u32[]{:S(2)}) collective-permute-start(bf16[1024,128]{1,0:T(8,128)(2,1)S(1)} %fusion.36), channel_id=1, source_target_pairs={{0,2},{2,0},{1,3},{3,1},{4,6},{6,4},{5,7},{7,5},{8,10},{10,8},{9,1... | collective-permute-start | bytes 786440 | tf_op jit(solution)/shard_map/ppermute | solution.py:311
  533.1 309.9 %reduce-scatter.17.cloned.1.call-start = ((), (), s32[]{:S(2)}) async-start(), calls=%async_computation.22 | async-start | bytes 4718592 | tf_op jit(solution)/shard_map/reduce_scatter | solution.py:181
  537.6 343.9 %reduce-scatter.13.cloned.1.call-start = ((), (), s32[]{:S(2)}) async-start(), calls=%async_computation.18 | async-start | bytes 4718592 | tf_op jit(solution)/shard_map/reduce_scatter | solution.py:181
  545.8 113.5 %copy-start.17 = (f32[44,2048]{1,0:T(8,128)S(1)}, f32[44,2048]{1,0:T(8,128)}, u32[]{:S(2)}) copy-start(f32[44,2048]{1,0:T(8,128)} %param.34) | copy-start | bytes 1081348
  566.8 86.9 %all-to-all-start.3 = ((bf16[8,16,1536]{2,1,0:T(8,128)(2,1)}), bf16[8,16,1536]{2,1,0:T(8,128)(2,1)}, u32[]{:S(2)}, u32[]{:S(2)}) async-start(bf16[8,16,1536]{2,1,0:T(8,128)(2,1)} %bitcast.70), calls=%async_computation.10 | async-start | bytes 786432 | tf_op jit(solution)/shard_map/all_to_all | solution.py:321
  572.8 235.8 %copy-start.10 = (f32[16,11264]{1,0:T(8,128)S(1)}, f32[16,11264]{1,0:T(8,128)}, u32[]{:S(2)}) copy-start(f32[16,11264]{1,0:T(8,128)} %param.25) | copy-start | bytes 2162692
  643.9 15.4 %collective-permute-start.9 = (bf16[44,2048]{1,0:T(8,128)(2,1)}, bf16[44,2048]{1,0:T(8,128)(2,1)S(1)}, u32[]{:S(2)}, u32[]{:S(2)}) collective-permute-start(bf16[44,2048]{1,0:T(8,128)(2,1)} %bitcast.79), channel_id=1, source_target_pairs={{0,0},{2,1},{16,2},{18,3},{32,4},{34,5},{48,6},{50,7},{64,8},{66,9... | collective-permute-start | bytes 540680 | tf_op jit(solution)/shard_map/ppermute | solution.py:337
  653.7 6.8 collective-permute-start.8
  662.2 152.0 %copy-start.15 = (f32[16,2048]{1,0:T(8,128)S(1)}, f32[16,2048]{1,0:T(8,128)}, u32[]{:S(2)}) copy-start(f32[16,2048]{1,0:T(8,128)} %param.24) | copy-start | bytes 393220
  662.3 152.0 %copy-start.19 = (f32[16,2048]{1,0:T(8,128)S(1)}, f32[16,2048]{1,0:T(8,128)}, u32[]{:S(2)}) copy-start(f32[16,2048]{1,0:T(8,128)} %param.31) | copy-start | bytes 393220
  725.0 89.2 %collective-permute-start.7 = (bf16[16,2048]{1,0:T(8,128)(2,1)}, bf16[16,2048]{1,0:T(8,128)(2,1)}, u32[]{:S(2)}, u32[]{:S(2)}) collective-permute-start(bf16[16,2048]{1,0:T(8,128)(2,1)} %reduce-scatter.21.cloned.1.call-done), channel_id=1, source_target_pairs={{0,0},{2,1},{16,2},{18,3},{32,4},{34,5},{48,6},{50,7},{64,8},{66,9... | collective-permute-start | bytes 196616 | tf_op jit(solution)/shard_map/ppermute | solution.py:336
  801.5 12.1 %all-to-all-start.2 = ((bf16[8,16,384]{2,1,0:T(8,128)(2,1)}), bf16[8,16,384]{2,1,0:T(8,128)(2,1)S(1)}, u32[]{:S(2)}, u32[]{:S(2)}) async-start(bf16[8,16,384]{2,1,0:T(8,128)(2,1)} %bitcast.76), calls=%async_computation.7 | async-start | bytes 196608 | tf_op jit(solution)/shard_map/all_to_all | solution.py:321
  813.6 2.5 collective-permute-start.6
  (33 other events, 785.3 us)
Sparse Core Ops, SparseCore 0:
  28.0 42.0 all-gather.12
  72.4 34.0 all-gather.10
  109.2 39.9 all-gather.14
  153.8 45.5 reduce-scatter.10
  202.1 54.1 all-gather.24
  257.8 32.4 all-gather.20
  292.5 60.9 all-gather.18
  355.8 32.0 all-gather.16
  409.5 34.4 reduce-scatter.14
  447.9 34.4 all-gather.22
  485.7 81.0 reduce-scatter.22
  570.0 73.8 reduce-scatter.24
  647.1 77.8 reduce-scatter.20
  728.5 72.9 reduce-scatter.18
  803.8 39.1 reduce-scatter.16
  845.5 35.9 reduce-scatter.12

commit v2 on v1

--- a/solution.py
+++ b/solution.py
@@ -13,7 +13,6 @@
 REP = ("y", "zh", "zl")
 
 FF = 5632
-FT = 704
 FP = 768
 HD = 64
 STEP = 10
@@ -173,16 +172,53 @@
     )(q, do, o, k, kt, v, kp, lo, hi, lse)
 
 
+def shift(block, distance):
+    return lax.ppermute(block, "x", [(i, (i + distance) % 4) for i in range(4)])
+
+
+def swap(block):
+    return lax.ppermute(block, "c", [(0, 1), (1, 0)])
+
+
+ORDER = ((0, 0), (1, 0), (3, 0), (0, 1), (1, 1), (3, 1), (2, 0), (2, 1))
+NEAR = 768
+
+
 def gather_rows(block):
-    return lax.all_gather(block, TP, axis=0, tiled=True)
-
-
-def scatter_rows(partial):
-    return lax.psum_scatter(partial, TP, scatter_dimension=0, tiled=True).astype(F32)
+    right = shift(block, 1)
+    left = shift(block, -1)
+    near = jnp.concatenate([block, right, left], axis=0)
+    near = jnp.concatenate([near, swap(near)], axis=0)
+    far = jnp.concatenate([shift(right[:64], 1), shift(left[64:], -1)], axis=0)
+    far = jnp.concatenate([far, swap(far)], axis=0)
+    return near, far
+
+
+def scatter_rows(left_side, contract, weight):
+    near, far = left_side
+    far_part = contract(far, weight).astype(BF)
+    far_sum = (far_part[:128].astype(F32) + swap(far_part[128:]).astype(F32)).astype(BF)
+    by_left = shift(far_sum[:64], -1)
+    by_right = shift(far_sum[64:], 1)
+    other = swap(contract(near[384:], weight).astype(BF))
+    mine = contract(near[:384], weight) + other.astype(F32)
+    to_left = jnp.concatenate([mine[128:192] + by_left.astype(F32), mine[192:256]], axis=0)
+    to_right = jnp.concatenate([mine[256:320], mine[320:] + by_right.astype(F32)], axis=0)
+    from_right = shift(to_left.astype(BF), -1).astype(F32)
+    from_left = shift(to_right.astype(BF), 1).astype(F32)
+    return mine[:128] + from_right + from_left
+
+
+def whole(pair):
+    return jnp.concatenate(pair, axis=0)
 
 
 def row_positions(span_order, zl):
-    spans = lax.dynamic_index_in_dim(span_order.reshape(4, 2, 4), zl, axis=1, keepdims=False)
+    x = lax.axis_index("x")
+    c = lax.axis_index("c")
+    holders = jnp.stack([((x - dx) % 4 * 2 + zl) * 2 + (c + dc) % 2 for dx, dc in ORDER])
+    picked = (holders[:, None] == jnp.arange(16, dtype=jnp.int32)[None, :]).astype(jnp.int32)
+    spans = jnp.sum(picked[:, :, None] * span_order.reshape(1, 16, 2), axis=1)
     return (spans.reshape(16, 1) * 64 + jnp.arange(64, dtype=jnp.int32)[None, :]).reshape(ROWS)
 
 
@@ -228,22 +264,26 @@
     qkv_cols = jnp.concatenate(
         [scaled_qkv[:, :2048].reshape(16, 8, 256), kv_cols[:, 0], kv_cols[:, 1]], axis=2
     ).transpose(1, 0, 2)
-    gu_cols = (low_gu * gain_two).astype(BF).reshape(16, 2, 8, FT)
-    gu_cols = jnp.pad(gu_cols, ((0, 0), (0, 0), (0, 0), (0, FP - FT)))
-    gu_cols = gu_cols.transpose(2, 0, 1, 3).reshape(8, 16, 2 * FP)
+    gu_cols = (low_gu * gain_two).astype(BF).reshape(16, 2, 8, 16, 44)
+    gu_cols = jnp.pad(gu_cols, ((0, 0), (0, 0), (0, 0), (0, 0), (0, 4)))
+    gu_cols = gu_cols.transpose(2, 0, 1, 3, 4).reshape(8, 16, 2 * FP)
 
     def to_rank(cols):
         moved = lax.ppermute(cols, ALL, NATURAL)
         return lax.all_to_all(moved, TP, 0, 0, tiled=True).reshape(128, cols.shape[2])
 
-    qkv_part = to_rank(qkv_cols)
+    def spread_all(part):
+        copies = jnp.broadcast_to(part[None], (16, *part.shape))
+        moved = lax.all_to_all(copies, REP, 0, 0, tiled=True)
+        return moved.reshape(16 * part.shape[0], part.shape[1])
+
+    w_qkv = spread_all(to_rank(qkv_cols))
     gu_part = to_rank(gu_cols)
-    out_part = lax.ppermute(attn_out.astype(BF), ALL, SPREAD)
-    down_part = lax.ppermute(down_proj.astype(BF), ALL, SPREAD)
-    w_qkv = lax.all_gather(qkv_part, REP, axis=0, tiled=True)
-    w_out = lax.all_gather(out_part, REP, axis=0, tiled=True)
+    w_out = spread_all(lax.ppermute(attn_out.astype(BF), ALL, SPREAD))
+    down_rows = jnp.pad(down_proj.astype(BF), ((0, 4), (0, 0)))
+    down_part = lax.ppermute(down_rows, ALL, SPREAD)
     w_gu = lax.all_gather(gu_part, REP, axis=0, tiled=True)
-    w_down = lax.all_gather(down_part, REP, axis=0, tiled=False).reshape(FT, 2048)
+    w_down = lax.all_gather(down_part, REP, axis=0, tiled=True)
 
     own_pos = row_positions(span_order, zl)
     other_pos = row_positions(span_order, 1 - zl)
@@ -258,9 +298,9 @@
     inputs = tokens.astype(F32)
     scale_one = norm_scale(inputs)
     hat_one = inputs * scale_one
-    all_hat_one = gather_rows(hat_one.astype(BF))
-    all_grad = gather_rows(out_grad)
-    projected = dot_nn(all_hat_one, w_qkv).astype(BF)
+    hat_one_pair = gather_rows(hat_one.astype(BF))
+    grad_pair = gather_rows(out_grad)
+    projected = whole([dot_nn(part, w_qkv).astype(BF) for part in hat_one_pair])
     queries = projected[:, :256] * BF(HD**-0.5)
     own_kv = projected[:, 256:]
     other_kv = lax.ppermute(own_kv, "zl", [(0, 1), (1, 0)])
@@ -268,41 +308,39 @@
     keys = kv[:, :HD]
     values = kv[:, HD:]
     att, lse = attend(queries, keys, values.T, key_pos, low_pos, high_pos)
-    hidden = inputs + scatter_rows(dot_nn(att, w_out).astype(BF))
+    hidden = inputs + scatter_rows((att[:NEAR], att[NEAR:]), dot_nn, w_out)
 
     scale_two = norm_scale(hidden)
     hat_two = hidden * scale_two
-    all_hat_two = gather_rows(hat_two.astype(BF))
-    w_gate = w_gu[:, :FT]
-    w_up = w_gu[:, FP : FP + FT]
-    gate = dot_nn(all_hat_two, w_gate)
-    up = dot_nn(all_hat_two, w_up)
-    sig = jax.nn.sigmoid(gate)
-    silu = gate * sig
-    hid = (silu * up).astype(BF)
-    block_out = (hidden + scatter_rows(dot_nn(hid, w_down).astype(BF))).astype(BF)
-
-    grad_hid = dot_nt(all_grad, w_down)
-    grad_gate = (grad_hid * up * sig * (1.0 + gate * (1.0 - sig))).astype(BF)
-    grad_up = (grad_hid * silu).astype(BF)
-    grad_hat_two = scatter_rows((dot_nt(grad_gate, w_gate) + dot_nt(grad_up, w_up)).astype(BF))
-    sum_down = dot_tn(hid, all_grad).astype(BF)
-    grad_gu = jnp.concatenate(
-        [
-            jnp.pad(grad_gate, ((0, 0), (0, FP - FT))),
-            jnp.pad(grad_up, ((0, 0), (0, FP - FT))),
-        ],
-        axis=1,
-    )
-    sum_gu = dot_tn(all_hat_two, grad_gu).astype(BF)
+    hat_two_pair = gather_rows(hat_two.astype(BF))
+    hid_pair = []
+    grad_gu_pair = []
+    for hat_part, grad_part in zip(hat_two_pair, grad_pair):
+        gate_up_val = dot_nn(hat_part, w_gu)
+        gate = gate_up_val[:, :FP]
+        up = gate_up_val[:, FP:]
+        sig = jax.nn.sigmoid(gate)
+        silu = gate * sig
+        hid_pair.append((silu * up).astype(BF))
+        grad_hid = dot_nt(grad_part, w_down)
+        grad_gate = grad_hid * up * sig * (1.0 + gate * (1.0 - sig))
+        grad_up = grad_hid * silu
+        grad_gu_pair.append(jnp.concatenate([grad_gate.astype(BF), grad_up.astype(BF)], axis=1))
+    grad_hat_two = scatter_rows(grad_gu_pair, dot_nt, w_gu)
+    sum_gu = dot_tn(whole(hat_two_pair), whole(grad_gu_pair)).astype(BF)
     sum_gu = lax.psum_scatter(sum_gu, REP, scatter_dimension=0, tiled=True)
-    sum_down = lax.psum_scatter(sum_down.reshape(16, 44, 2048), REP, scatter_dimension=0, tiled=False)
-
+    sum_down = dot_tn(whole(hid_pair), whole(grad_pair)).astype(BF)
+
+    def sum_replicas(partial):
+        split = partial.reshape(16, partial.shape[0] // 16, partial.shape[1])
+        return jnp.sum(lax.all_to_all(split, REP, 0, 0, tiled=True).astype(F32), axis=0).astype(BF)
+
+    sum_down = sum_replicas(sum_down)
     grad_hidden = norm_back(grad_hat_two, hat_two, scale_two, out_grad.astype(F32))
-    all_grad_hidden = gather_rows(grad_hidden.astype(BF))
+    all_grad_hidden = whole(gather_rows(grad_hidden.astype(BF)))
+    block_out = (hidden + scatter_rows(hid_pair, dot_nn, w_down)).astype(BF)
     grad_att = dot_nt(all_grad_hidden, w_out).astype(BF)
-    sum_out = dot_tn(att, all_grad_hidden).astype(BF)
-    sum_out = lax.psum_scatter(sum_out, REP, scatter_dimension=0, tiled=True)
+    sum_out = sum_replicas(dot_tn(att, all_grad_hidden).astype(BF))
 
     grad_q, grad_k, grad_v = attend_back(
         queries, grad_att, att, keys, keys.T, values, key_pos, low_pos, high_pos, lse
@@ -312,17 +350,16 @@
     grad_mixed = jnp.concatenate(
         [grad_q, (grad_kv[:ROWS] + arrived.astype(F32)).astype(BF)], axis=1
     )
-    grad_hat_one = scatter_rows(dot_nt(grad_mixed, w_qkv).astype(BF))
+    sum_qkv = sum_replicas(dot_tn(whole(hat_one_pair), grad_mixed).astype(BF))
+    grad_hat_one = scatter_rows((grad_mixed[:NEAR], grad_mixed[NEAR:]), dot_nt, w_qkv)
     in_grad = norm_back(grad_hat_one, hat_one, scale_one, grad_hidden).astype(BF)
-    sum_qkv = dot_tn(all_hat_one, grad_mixed).astype(BF)
-    sum_qkv = lax.psum_scatter(sum_qkv, REP, scatter_dimension=0, tiled=True)
 
     def to_shard(rows):
         mixed = lax.all_to_all(rows.reshape(8, 16, rows.shape[1]), TP, 0, 0, tiled=True)
         return lax.ppermute(mixed, ALL, back(NATURAL)).astype(F32)
 
-    got_gu = to_shard(sum_gu).reshape(8, 16, 2, FP)[..., :FT]
-    got_gu = got_gu.transpose(1, 2, 0, 3).reshape(16, 2 * FF)
+    got_gu = to_shard(sum_gu).reshape(8, 16, 2, 16, 48)[..., :44]
+    got_gu = got_gu.transpose(1, 2, 0, 3, 4).reshape(16, 2 * FF)
     got_qkv = to_shard(sum_qkv).transpose(1, 0, 2)
     got_kv = got_qkv[:, :, 256:].reshape(16, 4, 2, 2, HD).sum(axis=2)
     got_qkv = jnp.concatenate(
@@ -334,7 +371,7 @@
         axis=1,
     )
     got_out = lax.ppermute(sum_out, ALL, back(SPREAD)).astype(F32)
-    got_down = lax.ppermute(sum_down, ALL, back(SPREAD)).astype(F32)
+    got_down = lax.ppermute(sum_down, ALL, back(SPREAD))[:44].astype(F32)
     gain_sums = jnp.stack(
         [jnp.sum(low_qkv * got_qkv, axis=1), jnp.sum(low_gu * got_gu, axis=1)], axis=0
     )

time: 905 us -> 588 us (0.65)
  the two profiles are of different devices: /device:TPU:17 before, /device:TPU:10 now
where the time goes in v2:
time: 588 us; the launch traced here: 578 us
  waiting for transfers between devices  162 us (28%)
  starting transfers between devices  140 us (24%)
  matrix products  85.3 us (15%)
  other arithmetic  56.8 us (10%)
  local copies, waits for them, and re-layouts  56.7 us (10%)
  Pallas kernels  46.4 us (8%)
  between operations  16.9 us (3%)
  blocking collectives  13.4 us (2%)
    ppermute x32, waiting for transfers between devices, shift(): return lax.ppermute(block, 'x', [(i, (i + distance) % 4) for i in range(4)])  67.4 us
    ppermute x32, starting transfers between devices, shift(): return lax.ppermute(block, 'x', [(i, (i + distance) % 4) for i in range(4)])  46.4 us
    all_to_all x3, starting transfers between devices, sum_replicas(): lax.all_to_all(split, REP, 0, 0, tiled=True).astype(F32)  32.1 us
    dot_general x10, matrix products, dot_nn(): lax.dot_general(a, b, (((1,), (0,)), ((), ())), preferred_element_type=F32)  29.9 us
    unnamed x176, local copies, waits for them, and re-layouts  28.2 us
    dot_general x9, matrix products, dot_nt(): lax.dot_general(a, b, (((1,), (1,)), ((), ())), preferred_element_type=F32)  28.1 us
    dot_general x4, matrix products, dot_tn(): lax.dot_general(a, b, (((0,), (0,)), ((), ())), preferred_element_type=F32)  27.3 us
    pallas_call x1, Pallas kernels, attend_back(): pl.pallas_call(attend_back_kernel, grid=(ROWS // QB,), in_specs=[block, b...  24.8 us
  transfers between devices with their start and end apart: 69, of which 27 were waited for; matrix products, arithmetic and copies ran while one was open for 30% of the time, Pallas kernels for 8%

profile of v2, /device:TPU:10, one launch (start us, length us, event | category | flops | bytes accessed | tf_op | source)
XLA Modules:
  0.0 578.2 jit_solution(4653030388823179209)
XLA Ops:
  18.4 10.2 %collective-permute-done.18 = bf16[8,16,1536]{2,1,0:T(8,128)(2,1)S(1)} collective-permute-done((bf16[8,16,1536]{2,1,0:T(8,128)(2,1)S(1)}, bf16[8,16,1536]{2,1,0:T(8,128)(2,1)S(1)}, u32[]{:S(2)}, u32[]{:S(2)}) %collective-permute-start.18) | collective-permute-done | bytes 393248 | tf_op jit(solution)/shard_map/ppermute | solution.py:272
  28.6 13.4 %all_to_all.45 = bf16[8,16,1536]{2,1,0:T(8,128)(2,1)} all-to-all(bf16[8,16,1536]{2,1,0:T(8,128)(2,1)S(1)} %collective-permute-done.18), channel_id=1, replica_groups=mesh['y'=4,'zh'=2,'x'=4,'zl'=2,'c'=2] {'x','c'}, dimensions={0} | all-to-all | bytes 786432 | tf_op jit(solution)/shard_map/all_to_all | solution.py:273
  48.7 12.6 %collective-permute-done.3 = bf16[8,16,384]{2,0,1:T(8,128)(2,1)S(1)} collective-permute-done((bf16[8,16,384]{2,0,1:T(8,128)(2,1)S(1)}, bf16[8,16,384]{2,0,1:T(8,128)(2,1)S(1)}, u32[]{:S(2)}, u32[]{:S(2)}) %collective-permute-start.3) | collective-permute-done | bytes 98336 | tf_op jit(solution)/shard_map/ppermute | solution.py:272
  71.2 9.4 %all-to-all-start.1 = ((bf16[16,128,384]{2,1,0:T(8,128)(2,1)}), bf16[16,128,384]{2,1,0:T(8,128)(2,1)S(1)}, u32[]{:S(2)}, u32[]{:S(2)}) async-start(bf16[16,128,384]{2,1,0:T(8,128)(2,1)} %broadcast_in_dim.25), calls=%async_computation.1 | async-start | bytes 3145728 | tf_op jit(solution)/shard_map/all_to_all | solution.py:277
  85.8 5.1 collective-permute-done.5
  98.7 19.8 %all-to-all-done.1 = bf16[16,128,384]{2,1,0:T(8,128)(2,1)S(1)} async-done(((bf16[16,128,384]{2,1,0:T(8,128)(2,1)}), bf16[16,128,384]{2,1,0:T(8,128)(2,1)S(1)}, u32[]{:S(2)}, u32[]{:S(2)}) %all-to-all-start.1) | async-done | bytes 1572896 | tf_op jit(solution)/shard_map/all_to_all | solution.py:277
  119.8 6.0 %all-to-all-start.2 = ((bf16[16,16,2048]{2,1,0:T(8,128)(2,1)}), bf16[16,16,2048]{2,1,0:T(8,128)(2,1)S(1)}, u32[]{:S(2)}, u32[]{:S(2)}) async-start(bf16[16,16,2048]{2,1,0:T(8,128)(2,1)} %broadcast_in_dim.29), calls=%async_computation.2 | async-start | bytes 2097152 | tf_op jit(solution)/shard_map/all_to_all | solution.py:277
  135.1 8.2 %collective-permute-done.7 = bf16[1024,128]{1,0:T(8,128)(2,1)S(1)} collective-permute-done((bf16[1024,128]{1,0:T(8,128)(2,1)S(1)}, bf16[1024,128]{1,0:T(8,128)(2,1)S(1)}, u32[]{:S(2)}, u32[]{:S(2)}) %collective-permute-start.7) | collective-permute-done | bytes 262176 | tf_op jit(solution)/shard_map/ppermute | solution.py:306
  145.0 21.6 %attend.1 = (bf16[1024,256]{1,0:T(8,128)(2,1)S(1)}, f32[4,1024]{1,0:T(4,128)S(1)}) custom-call(bf16[1024,256]{1,0:T(8,128)(2,1)S(1)} %fusion.83.q_ref, bf16[2048,64]{1,0:T(8,128)(2,1)S(1)} %get-tuple-element.83.k_ref, bf16[64,2048]{1,0:T(8,128)(2,1)S(1)} %copy.83.vt_ref, s32[2048,256]{1,0:T(8,128)S(1)} %broadcast_in_dim.26.kp_ref, ...), custom_call_target="tpu_custom_call" | custom-call | flops 2147483648 | bytes 8388608 | tf_op jit(solution)/shard_map/attend/pallas_call | solution.py:99
  174.2 4.4 collective-permute-start.30
  180.8 8.3 %collective-permute-start.11 = (bf16[64,2048]{1,0:T(8,128)(2,1)S(1)}, bf16[64,2048]{1,0:T(8,128)(2,1)S(1)}, u32[]{:S(2)}, u32[]{:S(2)}) collective-permute-start(bf16[64,2048]{1,0:T(8,128)(2,1)S(1)} %get-tuple-element.88), channel_id=1, source_target_pairs={{0,12},{4,0},{8,4},{12,8},{1,13},{5,1},{9,5},{13,9},{2,14},{6,2},{... | collective-permute-start | bytes 786440 | tf_op jit(solution)/shard_map/ppermute | solution.py:176
  192.4 12.0 %collective-permute-done.11 = bf16[64,2048]{1,0:T(8,128)(2,1)S(1)} collective-permute-done((bf16[64,2048]{1,0:T(8,128)(2,1)S(1)}, bf16[64,2048]{1,0:T(8,128)(2,1)S(1)}, u32[]{:S(2)}, u32[]{:S(2)}) %collective-permute-start.11) | collective-permute-done | bytes 262176 | tf_op jit(solution)/shard_map/ppermute | solution.py:176
  213.1 6.5 %collective-permute-done.14 = bf16[128,2048]{1,0:T(8,128)(2,1)S(1)} collective-permute-done((bf16[128,2048]{1,0:T(8,128)(2,1)S(1)}, bf16[128,2048]{1,0:T(8,128)(2,1)S(1)}, u32[]{:S(2)}, u32[]{:S(2)}) %collective-permute-start.14) | collective-permute-done | bytes 524320 | tf_op jit(solution)/shard_map/ppermute | solution.py:176
  226.8 8.7 %collective-permute-done.16 = bf16[128,2048]{1,0:T(8,128)(2,1)S(1)} collective-permute-done((bf16[128,2048]{1,0:T(8,128)(2,1)S(1)}, bf16[128,2048]{1,0:T(8,128)(2,1)S(1)}, u32[]{:S(2)}, u32[]{:S(2)}) %collective-permute-start.16) | collective-permute-done | bytes 524320 | tf_op jit(solution)/shard_map/ppermute | solution.py:176
  258.9 6.1 %fusion.61 = f32[256,1536]{1,0:T(8,128)} fusion(bf16[2048,1536]{1,0:T(8,128)(2,1)} %all-gather.3.cloned.1.call-done, bf16[128,2048]{1,0:T(8,128)(2,1)} %copy-done.50, bf16[64,2048]{1,0:T(8,128)(2,1)} %copy-done.45, bf16[64,2048]{1,0:T(8,128)(2,1)} %copy-done.46), kind=kOutput, calls=%fused_computation.100 | convolution fusion | flops 1613758464 | bytes 8912896 | tf_op jit(solution)/shard_map/dot_general | solution.py:64
  273.2 8.1 %fusion.8 = f32[768,1536]{1,0:T(8,128)} fusion(bf16[2048,1536]{1,0:T(8,128)(2,1)S(1)} %copy-done.73, bf16[384,2048]{1,0:T(8,128)(2,1)} %collective-permute-done.17, bf16[128,2048]{1,0:T(8,128)(2,1)S(1)} %copy-done.21, bf16[128,2048]{1,0:T(8,128)(2,1)S(1)} %copy-done.23, bf16[128,2048]{1,0:T(8,128)(2,1)S(1)} %copy-done.30), kind=kOutput, calls=%fused_computation.10 | convolution fusion | flops 4844421120 | bytes 14155776 | tf_op jit(solution)/shard_map/dot_general | solution.py:64
  281.3 6.5 %multiply_convert_fusion.1 = (bf16[768,768]{1,0:T(8,128)(2,1)S(1)}, bf16[768,768]{1,0:T(8,128)(2,1)S(1)}, bf16[768,768]{1,0:T(8,128)(2,1)S(1)}) fusion(f32[768,1536]{1,0:T(8,128)} %fusion.8, bf16[768,2048]{1,0:T(8,128)(2,1)S(1)} %copy-done.24, bf16[384,2048]{1,0:T(8,128)(2,1)} %collective-permute-done.31, bf16[128,2048]{1,0:T(8,128)(2,1)S(1)} %copy-done.19, ...), kind=kOutput, calls=%fused_computation.50 | convolution fusion | flops 2437349376 | bytes 14548992 | tf_op jit(solution)/shard_map/dot_general | solution.py:68
  300.9 6.4 %collective-permute-done.25 = bf16[64,2048]{1,0:T(8,128)(2,1)S(1)} collective-permute-done((bf16[64,2048]{1,0:T(8,128)(2,1)S(1)}, bf16[64,2048]{1,0:T(8,128)(2,1)S(1)}, u32[]{:S(2)}, u32[]{:S(2)}) %collective-permute-start.25) | collective-permute-done | bytes 262176 | tf_op jit(solution)/shard_map/ppermute | solution.py:176
  323.8 16.5 %convolution_convert_fusion = bf16[2048,1536]{1,0:T(8,128)(2,1)} fusion(bf16[1024,2048]{1,0:T(8,128)(2,1)S(1)} %copy-done.57, bf16[256,768]{1,0:T(8,128)(2,1)S(1)} %get-tuple-element.65, bf16[256,768]{1,0:T(8,128)(2,1)S(1)} %get-tuple-element.64, bf16[768,768]{1,0:T(8,128)(2,1)S(1)} %get-tuple-element.54, bf16[768,768]{1,0:T(8,128)(2,1)S(1)} %get-tuple-element.53), kind=kOutput, calls=%fused_computation | convolution fusion | flops 6458179584 | bytes 13631488 | tf_op jit(solution)/shard_map/dot_general | solution.py:72
  353.9 6.5 %collective-permute-done.42 = bf16[128,2048]{1,0:T(8,128)(2,1)S(1)} collective-permute-done((bf16[128,2048]{1,0:T(8,128)(2,1)S(1)}, bf16[128,2048]{1,0:T(8,128)(2,1)S(1)}, u32[]{:S(2)}, u32[]{:S(2)}) %collective-permute-start.42) | collective-permute-done | bytes 524320 | tf_op jit(solution)/shard_map/ppermute | solution.py:176
  365.4 4.9 convolution_convert_fusion.1
  370.3 10.3 %all-to-all-start.8 = ((bf16[16,48,2048]{2,1,0:T(8,128)(2,1)}), bf16[16,48,2048]{2,1,0:T(8,128)(2,1)}, u32[]{:S(2)}, u32[]{:S(2)}) async-start(bf16[16,48,2048]{2,1,0:T(8,128)(2,1)} %bitcast.100), calls=%async_computation.9 | async-start | bytes 6291456 | tf_op jit(solution)/shard_map/all_to_all | solution.py:336
  384.5 4.7 collective-permute-done.45
  399.5 24.8 %attend_back.1 = (bf16[1024,256]{1,0:T(8,128)(2,1)S(1)}, f32[2048,64]{1,0:T(8,128)S(1)}, f32[2048,64]{1,0:T(8,128)S(1)}) custom-call(bf16[1024,256]{1,0:T(8,128)(2,1)S(1)} %copy-done.2, bf16[1024,256]{1,0:T(8,128)(2,1)S(1)} %convolution_convert_fusion.12.do_ref, bf16[1024,256]{1,0:T(8,128)(2,1)S(1)} %copy-done.5, ...), custom_call_target="tpu_custom_call" | custom-call | flops 5368709120 | bytes 8388608 | tf_op jit(solution)/shard_map/attend_back/pallas_call | solution.py:146
  430.3 16.2 %all-to-all-start.6 = ((bf16[16,16,2048]{2,1,0:T(8,128)(2,1)}), bf16[16,16,2048]{2,1,0:T(8,128)(2,1)}, u32[]{:S(2)}, u32[]{:S(2)}) async-start(bf16[16,16,2048]{2,1,0:T(8,128)(2,1)} %bitcast.103), calls=%async_computation.6 | async-start | bytes 2097152 | tf_op jit(solution)/shard_map/all_to_all | solution.py:336
  453.2 13.5 %all-to-all-done.6 = bf16[16,16,2048]{2,1,0:T(8,128)(2,1)} async-done(((bf16[16,16,2048]{2,1,0:T(8,128)(2,1)}), bf16[16,16,2048]{2,1,0:T(8,128)(2,1)}, u32[]{:S(2)}, u32[]{:S(2)}) %all-to-all-start.6) | async-done | bytes 1048608 | tf_op jit(solution)/shard_map/all_to_all | solution.py:336
  466.6 5.6 all-to-all-start.4
  497.7 10.2 %all-to-all-start.5 = ((bf16[8,16,384]{2,1,0:T(8,128)(2,1)}), bf16[8,16,384]{2,1,0:T(8,128)(2,1)S(1)}, u32[]{:S(2)}, u32[]{:S(2)}) async-start(bf16[8,16,384]{2,1,0:T(8,128)(2,1)} %bitcast.32), calls=%async_computation.5 | async-start | bytes 196608 | tf_op jit(solution)/shard_map/all_to_all | solution.py:358
  530.5 5.2 all-to-all-start.7
  538.5 4.8 all-to-all-done.7
  543.3 4.7 collective-permute-start.56
  550.5 14.0 %collective-permute-done.56 = bf16[8,16,1536]{2,1,0:T(8,128)(2,1)S(1)} collective-permute-done((bf16[8,16,1536]{2,1,0:T(8,128)(2,1)}, bf16[8,16,1536]{2,1,0:T(8,128)(2,1)S(1)}, u32[]{:S(2)}, u32[]{:S(2)}) %collective-permute-start.56) | collective-permute-done | bytes 393248 | tf_op jit(solution)/shard_map/ppermute | solution.py:359
  (441 shorter events, 245.8 us)
Async XLA Ops:
  7.2 251.7 %all-gather.3.cloned.1.call-start = ((), (), s32[]{:S(2)}) async-start(), calls=%async_computation.10 | async-start | bytes 6684672 | tf_op jit(solution)/shard_map/all_gather | solution.py:285
  43.2 37.4 %collective-permute-start.1 = (bf16[128,2048]{1,0:T(8,128)(2,1)S(1)}, bf16[128,2048]{1,0:T(8,128)(2,1)S(1)}, u32[]{:S(2)}, u32[]{:S(2)}) collective-permute-start(bf16[128,2048]{1,0:T(8,128)(2,1)S(1)} %get-tuple-element.47), channel_id=1, source_target_pairs={{0,12},{4,0},{8,4},{12,8},{1,13},{5,1},{9,5},{13,9},{2,14},{6,2},{... | collective-permute-start | bytes 1572872 | tf_op jit(solution)/shard_map/ppermute | solution.py:176
  44.7 36.0 %collective-permute-start = (bf16[128,2048]{1,0:T(8,128)(2,1)S(1)}, bf16[128,2048]{1,0:T(8,128)(2,1)S(1)}, u32[]{:S(2)}, u32[]{:S(2)}) collective-permute-start(bf16[128,2048]{1,0:T(8,128)(2,1)S(1)} %get-tuple-element.47), channel_id=1, source_target_pairs={{0,4},{4,8},{8,12},{12,0},{1,5},{5,9},{9,13},{13,1},{2,6},{6,10},{... | collective-permute-start | bytes 1572872 | tf_op jit(solution)/shard_map/ppermute | solution.py:176
  47.8 50.9 %collective-permute-start.8 = (bf16[16,2048]{1,0:T(8,128)(2,1)S(1)}, bf16[16,2048]{1,0:T(8,128)(2,1)S(1)}, u32[]{:S(2)}, u32[]{:S(2)}) collective-permute-start(bf16[16,2048]{1,0:T(8,128)(2,1)S(1)} %convert_element_type.268), channel_id=1, source_target_pairs={{0,0},{1,2},{2,16},{3,18},{4,32},{5,34},{6,48},{7,50},{8,64},{9,66... | collective-permute-start | bytes 196616 | tf_op jit(solution)/shard_map/ppermute | solution.py:282
  71.2 47.3 %all-to-all-start.1 = ((bf16[16,128,384]{2,1,0:T(8,128)(2,1)}), bf16[16,128,384]{2,1,0:T(8,128)(2,1)S(1)}, u32[]{:S(2)}, u32[]{:S(2)}) async-start(bf16[16,128,384]{2,1,0:T(8,128)(2,1)} %broadcast_in_dim.25), calls=%async_computation.1 | async-start | bytes 3145728 | tf_op jit(solution)/shard_map/all_to_all | solution.py:277
  82.0 45.8 %collective-permute-start.2 = (bf16[384,2048]{1,0:T(8,128)(2,1)}, bf16[384,2048]{1,0:T(8,128)(2,1)}, u32[]{:S(2)}, u32[]{:S(2)}) collective-permute-start(bf16[384,2048]{1,0:T(8,128)(2,1)} %pad_maximum_fusion), channel_id=1, source_target_pairs={{0,1},{1,0},{2,3},{3,2},{4,5},{5,4},{6,7},{7,6},{8,9},{9,8},{10,11... | collective-permute-start | bytes 4718600 | tf_op jit(solution)/shard_map/ppermute | solution.py:180
  93.9 32.0 %collective-permute-start.6 = (bf16[128,2048]{1,0:T(8,128)(2,1)}, bf16[128,2048]{1,0:T(8,128)(2,1)}, u32[]{:S(2)}, u32[]{:S(2)}) collective-permute-start(bf16[128,2048]{1,0:T(8,128)(2,1)} %pad_maximum_fusion.10), channel_id=1, source_target_pairs={{0,1},{1,0},{2,3},{3,2},{4,5},{5,4},{6,7},{7,6},{8,9},{9,8},{10,11... | collective-permute-start | bytes 1572872 | tf_op jit(solution)/shard_map/ppermute | solution.py:180
  119.8 48.1 %all-to-all-start.2 = ((bf16[16,16,2048]{2,1,0:T(8,128)(2,1)}), bf16[16,16,2048]{2,1,0:T(8,128)(2,1)S(1)}, u32[]{:S(2)}, u32[]{:S(2)}) async-start(bf16[16,16,2048]{2,1,0:T(8,128)(2,1)} %broadcast_in_dim.29), calls=%async_computation.2 | async-start | bytes 2097152 | tf_op jit(solution)/shard_map/all_to_all | solution.py:277
  125.8 139.2 %all-gather.5.cloned.1.call-start = ((), (), s32[]{:S(2)}) async-start(), calls=%async_computation.11 | async-start | bytes 3342336 | tf_op jit(solution)/shard_map/all_gather | solution.py:286
  174.2 32.6 %collective-permute-start.30 = (bf16[128,2048]{1,0:T(8,128)(2,1)}, bf16[128,2048]{1,0:T(8,128)(2,1)S(1)}, u32[]{:S(2)}, u32[]{:S(2)}) collective-permute-start(bf16[128,2048]{1,0:T(8,128)(2,1)} %param.20), channel_id=1, source_target_pairs={{0,12},{4,0},{8,4},{12,8},{1,13},{5,1},{9,5},{13,9},{2,14},{6,2},{... | collective-permute-start | bytes 1572872 | tf_op jit(solution)/shard_map/ppermute | solution.py:176
  178.7 28.4 %collective-permute-start.29 = (bf16[128,2048]{1,0:T(8,128)(2,1)}, bf16[128,2048]{1,0:T(8,128)(2,1)}, u32[]{:S(2)}, u32[]{:S(2)}) collective-permute-start(bf16[128,2048]{1,0:T(8,128)(2,1)} %param.20), channel_id=1, source_target_pairs={{0,4},{4,8},{8,12},{12,0},{1,5},{5,9},{9,13},{13,1},{2,6},{6,10},{... | collective-permute-start | bytes 1572872 | tf_op jit(solution)/shard_map/ppermute | solution.py:176
  179.3 351.1 %reduce-scatter.2.cloned.1.call-start = ((), (), s32[]{:S(2)}) async-start(), calls=%async_computation.12 | async-start | bytes 6684672 | tf_op jit(solution)/shard_map/reduce_scatter | solution.py:331
  180.8 23.6 %collective-permute-start.11 = (bf16[64,2048]{1,0:T(8,128)(2,1)S(1)}, bf16[64,2048]{1,0:T(8,128)(2,1)S(1)}, u32[]{:S(2)}, u32[]{:S(2)}) collective-permute-start(bf16[64,2048]{1,0:T(8,128)(2,1)S(1)} %get-tuple-element.88), channel_id=1, source_target_pairs={{0,12},{4,0},{8,4},{12,8},{1,13},{5,1},{9,5},{13,9},{2,14},{6,2},{... | collective-permute-start | bytes 786440 | tf_op jit(solution)/shard_map/ppermute | solution.py:176
  212.5 68.8 %collective-permute-start.31 = (bf16[384,2048]{1,0:T(8,128)(2,1)}, bf16[384,2048]{1,0:T(8,128)(2,1)}, u32[]{:S(2)}, u32[]{:S(2)}) collective-permute-start(bf16[384,2048]{1,0:T(8,128)(2,1)} %pad_maximum_fusion.2), channel_id=1, source_target_pairs={{0,1},{1,0},{2,3},{3,2},{4,5},{5,4},{6,7},{7,6},{8,9},{9,8},{10,11... | collective-permute-start | bytes 4718600 | tf_op jit(solution)/shard_map/ppermute | solution.py:180
  226.8 38.3 %collective-permute-start.35 = (bf16[128,2048]{1,0:T(8,128)(2,1)}, bf16[128,2048]{1,0:T(8,128)(2,1)}, u32[]{:S(2)}, u32[]{:S(2)}) collective-permute-start(bf16[128,2048]{1,0:T(8,128)(2,1)} %pad_maximum_fusion.16), channel_id=1, source_target_pairs={{0,1},{1,0},{2,3},{3,2},{4,5},{5,4},{6,7},{7,6},{8,9},{9,8},{10,11... | collective-permute-start | bytes 1572872 | tf_op jit(solution)/shard_map/ppermute | solution.py:180
  271.3 21.3 %collective-permute-start.36 = (bf16[128,2048]{1,0:T(8,128)(2,1)S(1)}, bf16[128,2048]{1,0:T(8,128)(2,1)S(1)}, u32[]{:S(2)}, u32[]{:S(2)}) collective-permute-start(bf16[128,2048]{1,0:T(8,128)(2,1)S(1)} %slice.374), channel_id=1, source_target_pairs={{0,1},{1,0},{2,3},{3,2},{4,5},{5,4},{6,7},{7,6},{8,9},{9,8},{10,11... | collective-permute-start | bytes 1572872 | tf_op jit(solution)/shard_map/ppermute | solution.py:180
  272.9 22.6 %collective-permute-start.24 = (bf16[128,2048]{1,0:T(8,128)(2,1)S(1)}, bf16[128,2048]{1,0:T(8,128)(2,1)S(1)}, u32[]{:S(2)}, u32[]{:S(2)}) collective-permute-start(bf16[128,2048]{1,0:T(8,128)(2,1)S(1)} %slice.361), channel_id=1, source_target_pairs={{0,1},{1,0},{2,3},{3,2},{4,5},{5,4},{6,7},{7,6},{8,9},{9,8},{10,11... | collective-permute-start | bytes 1572872 | tf_op jit(solution)/shard_map/ppermute | solution.py:180
  292.5 22.3 %collective-permute-start.32 = (bf16[384,2048]{1,0:T(8,128)(2,1)S(1)}, bf16[384,2048]{1,0:T(8,128)(2,1)S(1)}, u32[]{:S(2)}, u32[]{:S(2)}) collective-permute-start(bf16[384,2048]{1,0:T(8,128)(2,1)S(1)} %convolution_convert_fusion.5), channel_id=1, source_target_pairs={{0,1},{1,0},{2,3},{3,2},{4,5},{5,4},{6,7},{7,6},{8,9},{9,8},{10,11... | collective-permute-start | bytes 4718600 | tf_op jit(solution)/shard_map/ppermute | solution.py:180
  292.8 24.7 %collective-permute-start.37 = (bf16[64,2048]{1,0:T(8,128)(2,1)S(1)}, bf16[64,2048]{1,0:T(8,128)(2,1)S(1)}, u32[]{:S(2)}, u32[]{:S(2)}) collective-permute-start(bf16[64,2048]{1,0:T(8,128)(2,1)S(1)} %get-tuple-element.84), channel_id=1, source_target_pairs={{0,12},{4,0},{8,4},{12,8},{1,13},{5,1},{9,5},{13,9},{2,14},{6,2},{... | collective-permute-start | bytes 786440 | tf_op jit(solution)/shard_map/ppermute | solution.py:176
  295.6 21.9 %collective-permute-start.39 = (bf16[64,2048]{1,0:T(8,128)(2,1)S(1)}, bf16[64,2048]{1,0:T(8,128)(2,1)S(1)}, u32[]{:S(2)}, u32[]{:S(2)}) collective-permute-start(bf16[64,2048]{1,0:T(8,128)(2,1)S(1)} %get-tuple-element.85), channel_id=1, source_target_pairs={{0,4},{4,8},{8,12},{12,0},{1,5},{5,9},{9,13},{13,1},{2,6},{6,10},{... | collective-permute-start | bytes 786440 | tf_op jit(solution)/shard_map/ppermute | solution.py:176
  311.7 28.6 %collective-permute-start.28 = (bf16[128,2048]{1,0:T(8,128)(2,1)}, bf16[128,2048]{1,0:T(8,128)(2,1)}, u32[]{:S(2)}, u32[]{:S(2)}) collective-permute-start(bf16[128,2048]{1,0:T(8,128)(2,1)} %pad_maximum_fusion.15), channel_id=1, source_target_pairs={{0,4},{4,8},{8,12},{12,0},{1,5},{5,9},{9,13},{13,1},{2,6},{6,10},{... | collective-permute-start | bytes 1572872 | tf_op jit(solution)/shard_map/ppermute | solution.py:176
  312.8 27.5 %collective-permute-start.26 = (bf16[128,2048]{1,0:T(8,128)(2,1)}, bf16[128,2048]{1,0:T(8,128)(2,1)}, u32[]{:S(2)}, u32[]{:S(2)}) collective-permute-start(bf16[128,2048]{1,0:T(8,128)(2,1)} %pad_maximum_fusion.14), channel_id=1, source_target_pairs={{0,12},{4,0},{8,4},{12,8},{1,13},{5,1},{9,5},{13,9},{2,14},{6,2},{... | collective-permute-start | bytes 1572872 | tf_op jit(solution)/shard_map/ppermute | solution.py:176
  364.3 26.3 %collective-permute-start.43 = (bf16[384,2048]{1,0:T(8,128)(2,1)}, bf16[384,2048]{1,0:T(8,128)(2,1)}, u32[]{:S(2)}, u32[]{:S(2)}) collective-permute-start(bf16[384,2048]{1,0:T(8,128)(2,1)} %pad_maximum_fusion.3), channel_id=1, source_target_pairs={{0,1},{1,0},{2,3},{3,2},{4,5},{5,4},{6,7},{7,6},{8,9},{9,8},{10,11... | collective-permute-start | bytes 4718600 | tf_op jit(solution)/shard_map/ppermute | solution.py:180
  370.3 60.1 %all-to-all-start.8 = ((bf16[16,48,2048]{2,1,0:T(8,128)(2,1)}), bf16[16,48,2048]{2,1,0:T(8,128)(2,1)}, u32[]{:S(2)}, u32[]{:S(2)}) async-start(bf16[16,48,2048]{2,1,0:T(8,128)(2,1)} %bitcast.100), calls=%async_computation.9 | async-start | bytes 6291456 | tf_op jit(solution)/shard_map/all_to_all | solution.py:336
  424.4 22.2 %collective-permute-start.47 = (bf16[1024,128]{1,0:T(8,128)(2,1)S(1)}, bf16[1024,128]{1,0:T(8,128)(2,1)S(1)}, u32[]{:S(2)}, u32[]{:S(2)}) collective-permute-start(bf16[1024,128]{1,0:T(8,128)(2,1)S(1)} %fusion.89), channel_id=1, source_target_pairs={{0,2},{2,0},{1,3},{3,1},{4,6},{6,4},{5,7},{7,5},{8,10},{10,8},{9,1... | collective-permute-start | bytes 786440 | tf_op jit(solution)/shard_map/ppermute | solution.py:349
  430.3 36.3 %all-to-all-start.6 = ((bf16[16,16,2048]{2,1,0:T(8,128)(2,1)}), bf16[16,16,2048]{2,1,0:T(8,128)(2,1)}, u32[]{:S(2)}, u32[]{:S(2)}) async-start(bf16[16,16,2048]{2,1,0:T(8,128)(2,1)} %bitcast.103), calls=%async_computation.6 | async-start | bytes 2097152 | tf_op jit(solution)/shard_map/all_to_all | solution.py:336
  449.5 24.9 %collective-permute-start.49 = (bf16[128,2048]{1,0:T(8,128)(2,1)}, bf16[128,2048]{1,0:T(8,128)(2,1)}, u32[]{:S(2)}, u32[]{:S(2)}) collective-permute-start(bf16[128,2048]{1,0:T(8,128)(2,1)} %slice.393), channel_id=1, source_target_pairs={{0,1},{1,0},{2,3},{3,2},{4,5},{5,4},{6,7},{7,6},{8,9},{9,8},{10,11... | collective-permute-start | bytes 1572872 | tf_op jit(solution)/shard_map/ppermute | solution.py:180
  466.6 28.8 %all-to-all-start.4 = ((bf16[16,128,384]{2,1,0:T(8,128)(2,1)}), bf16[16,128,384]{2,1,0:T(8,128)(2,1)}, u32[]{:S(2)}, u32[]{:S(2)}) async-start(bf16[16,128,384]{2,1,0:T(8,128)(2,1)} %bitcast.101), calls=%async_computation.4 | async-start | bytes 3145728 | tf_op jit(solution)/shard_map/all_to_all | solution.py:336
  474.4 41.9 %collective-permute-start.48 = (bf16[384,2048]{1,0:T(8,128)(2,1)}, bf16[384,2048]{1,0:T(8,128)(2,1)}, u32[]{:S(2)}, u32[]{:S(2)}) collective-permute-start(bf16[384,2048]{1,0:T(8,128)(2,1)} %convolution_convert_fusion.3), channel_id=1, source_target_pairs={{0,1},{1,0},{2,3},{3,2},{4,5},{5,4},{6,7},{7,6},{8,9},{9,8},{10,11... | collective-permute-start | bytes 4718600 | tf_op jit(solution)/shard_map/ppermute | solution.py:180
  483.6 36.9 %collective-permute-start.50 = (bf16[64,2048]{1,0:T(8,128)(2,1)}, bf16[64,2048]{1,0:T(8,128)(2,1)S(1)}, u32[]{:S(2)}, u32[]{:S(2)}) collective-permute-start(bf16[64,2048]{1,0:T(8,128)(2,1)} %get-tuple-element.79), channel_id=1, source_target_pairs={{0,12},{4,0},{8,4},{12,8},{1,13},{5,1},{9,5},{13,9},{2,14},{6,2},{... | collective-permute-start | bytes 786440 | tf_op jit(solution)/shard_map/ppermute | solution.py:176
  484.2 36.4 %collective-permute-start.52 = (bf16[64,2048]{1,0:T(8,128)(2,1)}, bf16[64,2048]{1,0:T(8,128)(2,1)S(1)}, u32[]{:S(2)}, u32[]{:S(2)}) collective-permute-start(bf16[64,2048]{1,0:T(8,128)(2,1)} %get-tuple-element.80), channel_id=1, source_target_pairs={{0,4},{4,8},{8,12},{12,0},{1,5},{5,9},{9,13},{13,1},{2,6},{6,10},{... | collective-permute-start | bytes 786440 | tf_op jit(solution)/shard_map/ppermute | solution.py:176
  543.3 21.2 %collective-permute-start.56 = (bf16[8,16,1536]{2,1,0:T(8,128)(2,1)}, bf16[8,16,1536]{2,1,0:T(8,128)(2,1)S(1)}, u32[]{:S(2)}, u32[]{:S(2)}) collective-permute-start(bf16[8,16,1536]{2,1,0:T(8,128)(2,1)} %all-to-all-done.7), channel_id=1, source_target_pairs={{0,0},{1,1},{4,2},{5,3},{8,4},{9,5},{12,6},{13,7},{2,8},{3,9},{6,1... | collective-permute-start | bytes 1179656 | tf_op jit(solution)/shard_map/ppermute | solution.py:359
  (113 other events, 1387.9 us)
Sparse Core Ops, SparseCore 0:
  42.2 80.6 all-gather.2
  179.5 59.2 all-gather.4
  340.4 128.4 reduce-scatter.1

commit v3 on v1

v3 whole, which is shorter than its diff:
```python
import functools

import jax
import jax.numpy as jnp
from jax import lax
from jax.experimental import pallas as pl
from jax.experimental.pallas import tpu as pltpu
from jax.sharding import Mesh
from jax.sharding import PartitionSpec as P

BF = jnp.bfloat16
F32 = jnp.float32
ALL = ("y", "zh", "x", "zl", "c")
TP = ("x", "c")
REP = ("y", "zh", "zl")

FF = 5632
FP = 768
HD = 64
STEP = 10
ROWS = 1024
KEYS = 2048

norm_eps = 1e-05
beta_one = 0.9
beta_two = 0.95
adam_eps = 1e-08
big_negative = -1e30
step_rates = (0.15, 0.3, 0.06, 0.04, 2.0)
decay_rates = (0.1, 0.1, 0.1, 0.1, 0.0)


def flat_index(f, x, zl, c):
    return ((f * 4 + x) * 2 + zl) * 2 + c


SPREAD = [
    (t * 16 + k, flat_index(k // 2, t // 2, k % 2, t % 2)) for t in range(8) for k in range(16)
]


def back(route):
    return [(b, a) for a, b in route]


def adam_update(master, grad_sum, first_old, second_old, step_rate, decay_rate):
    first_new = beta_one * first_old + (1.0 - beta_one) * grad_sum
    second_new = beta_two * second_old + (1.0 - beta_two) * grad_sum * grad_sum
    first_fix = first_new / (1.0 - beta_one**STEP)
    second_fix = second_new / (1.0 - beta_two**STEP)
    master_new = master - step_rate * (
        first_fix / (jnp.sqrt(second_fix) + adam_eps) + decay_rate * master
    )
    return (first_new, second_new, master_new)


def dot_nn(a, b):
    return lax.dot_general(a, b, (((1,), (0,)), ((), ())), preferred_element_type=F32)


def dot_nt(a, b):
    return lax.dot_general(a, b, (((1,), (1,)), ((), ())), preferred_element_type=F32)


def dot_tn(a, b):
    return lax.dot_general(a, b, (((0,), (0,)), ((), ())), preferred_element_type=F32)


QB = 256


def takes(microseconds):
    return pl.CostEstimate(
        flops=int(microseconds * 1.15e9), bytes_accessed=1 << 20, transcendentals=0
    )


WHOLE = pl.BlockSpec(memory_space=pltpu.VMEM)
ANYWHERE = pl.BlockSpec(memory_space=pl.ANY)


def fixed(shape):
    return pl.BlockSpec(shape, lambda i: (0,) * len(shape), pipeline_mode=pl.Buffered(1))


def params(mib):
    return pltpu.CompilerParams(vmem_limit_bytes=mib * 1024 * 1024)


def attend_kernel(first, q_ref, kv_ref, kp_ref, lo_ref, hi_ref, *rest):
    turned = rest[-1]

    @pl.when(pl.program_id(0) == 0)
    def _():
        turned[...] = kv_ref[...].T

    key_pos = kp_ref[...]
    high = hi_ref[...]
    allowed = (key_pos >= lo_ref[...]) & (key_pos <= high)
    keys = kv_ref[:, :HD]
    for h in range(4):
        cols = slice(h * HD, (h + 1) * HD)
        row = slice(h, h + 1)
        s = jnp.where(allowed, dot_nt(keys, q_ref[:, cols]), big_negative)
        peak = jnp.max(s, axis=0, keepdims=True)
        if not first:
            out_before, peak_before, total_before = rest[:3]
            peak = jnp.maximum(peak, peak_before[row, :])
        p = jnp.exp(s - peak)
        total = jnp.sum(p, axis=0, keepdims=True)
        out = dot_nn(turned[HD:, :], p.astype(BF))
        if first:
            out_ref, peak_ref, total_ref = rest[-4:-1]
            out_ref[cols, :] = out
            peak_ref[row, :] = peak
            total_ref[row, :] = total
        else:
            o_ref, lse_ref = rest[-3:-1]
            fade = jnp.exp(peak_before[row, :] - peak)
            total = total + fade * total_before[row, :]
            out = out + fade * out_before[cols, :]
            out = out * jnp.where(high >= 0, 1.0 / total, 0.0)
            o_ref[:, cols] = out.T.astype(BF)
            lse_ref[row, :] = peak + jnp.log(total)


def attend(q, kv, kp, lo, hi, before, *earlier):
    first = before is None
    count = kv.shape[0]
    row = pl.BlockSpec((1, QB), lambda i: (0, i))
    rows = pl.BlockSpec((4, QB), lambda i: (0, i))
    flat = pl.BlockSpec((256, QB), lambda i: (0, i))
    block = pl.BlockSpec((QB, 256), lambda i: (i, 0))
    stat = jax.ShapeDtypeStruct((4, ROWS), F32)
    carried = [] if first else list(before)
    return pl.pallas_call(
        functools.partial(attend_kernel, first),
        grid=(ROWS // QB,),
        in_specs=[block, fixed((count, 2 * HD)), fixed((count, QB)), row, row]
        + [flat, rows, rows][: len(carried)]
        + [ANYWHERE] * len(earlier),
        out_specs=[flat, rows, rows] if first else [block, rows],
        out_shape=[jax.ShapeDtypeStruct((256, ROWS), F32), stat, stat]
        if first
        else [jax.ShapeDtypeStruct((ROWS, 256), BF), stat],
        scratch_shapes=[pltpu.VMEM((2 * HD, count), BF)],
        compiler_params=params(40),
        cost_estimate=takes(11),
        name="attend",
    )(q, kv, kp, lo, hi, *carried, *earlier)


def attend_back_kernel(first, q_ref, do_ref, o_ref, kv_ref, kp_ref, lo_ref, hi_ref, lse_ref, *rest):
    dq_ref, dkv_ref, turned, values = rest[-4:]

    @pl.when(pl.program_id(0) == 0)
    def _():
        dkv_ref[...] = jnp.zeros_like(dkv_ref)
        turned[...] = kv_ref[...].T
        values[...] = kv_ref[:, HD:]

    key_pos = kp_ref[...]
    allowed = (key_pos >= lo_ref[...]) & (key_pos <= hi_ref[...])
    keys = kv_ref[:, :HD]
    delta_all = (do_ref[...].astype(F32) * o_ref[...].astype(F32)).T
    for h in range(4):
        cols = slice(h * HD, (h + 1) * HD)
        qh = q_ref[:, cols]
        doh = do_ref[:, cols]
        delta = jnp.sum(delta_all[cols], axis=0, keepdims=True)
        s = dot_nt(keys, qh)
        p = jnp.where(allowed, jnp.exp(s - lse_ref[h : h + 1, :]), 0.0)
        ds = (p * (dot_nt(values[...], doh) - delta)).astype(BF)
        dkv_ref[:, :HD] += dot_nn(ds, qh)
        dkv_ref[:, HD:] += dot_nn(p.astype(BF), doh)
        dq = dot_nn(turned[:HD, :], ds) * HD**-0.5
        if first:
            dq_ref[cols, :] = dq
        else:
            dq_ref[:, cols] = (dq + rest[0][cols, :]).T.astype(BF)


def attend_back(q, do, o, kv, kp, lo, hi, lse, earlier_dq, *earlier):
    first = earlier_dq is None
    count = kv.shape[0]
    row = pl.BlockSpec((1, QB), lambda i: (0, i))
    block = pl.BlockSpec((QB, 256), lambda i: (i, 0))
    flat = pl.BlockSpec((256, QB), lambda i: (0, i))
    carried = [] if first else [earlier_dq]
    return pl.pallas_call(
        functools.partial(attend_back_kernel, first),
        grid=(ROWS // QB,),
        in_specs=[block, block, block, fixed((count, 2 * HD)), fixed((count, QB)), row, row]
        + [pl.BlockSpec((4, QB), lambda i: (0, i))]
        + [flat] * len(carried)
        + [ANYWHERE] * len(earlier),
        out_specs=[
            flat if first else block,
            pl.BlockSpec((count, 2 * HD), lambda i: (0, 0)),
        ],
        out_shape=[
            jax.ShapeDtypeStruct((256, ROWS), F32)
            if first
            else jax.ShapeDtypeStruct((ROWS, 256), BF),
            jax.ShapeDtypeStruct((count, 2 * HD), F32),
        ],
        scratch_shapes=[pltpu.VMEM((2 * HD, count), BF), pltpu.VMEM((count, HD), BF)],
        compiler_params=params(40),
        cost_estimate=takes(12.5),
        name="attend_back",
    )(q, do, o, kv, kp, lo, hi, lse, *carried, *earlier)


def project_kernel(*refs):
    pieces = refs[:8]
    raw_ref = refs[8]
    q_ref, kv_ref, w_ref = refs[-4:-1]
    hat = refs[-1]
    for f in range(8):
        for zl in range(2):
            for x in range(4):
                row = 256 * f + 64 * x + 32 * zl
                w_ref[row : row + 32, :] = raw_ref[2 * f + zl, 32 * x : 32 * x + 32, :]
    for k in range(8):
        hat[128 * k : 128 * k + 128, :] = pieces[k][...]
    for k in range(2):
        rows = slice(512 * k, 512 * k + 512)
        product = dot_nn(hat[rows, :], w_ref[...]).astype(BF)
        q_ref[rows, :] = product[:, :256] * BF(HD**-0.5)
        kv_ref[rows, :] = product[:, 256:]


def project(pieces, raw, *earlier):
    shape = lambda *dims: jax.ShapeDtypeStruct(dims, BF)
    return pl.pallas_call(
        project_kernel,
        in_specs=[WHOLE] * 9 + [ANYWHERE] * len(earlier),
        out_specs=[WHOLE] * 3,
        out_shape=[shape(ROWS, 256), shape(ROWS, 128), shape(2048, 384)],
        scratch_shapes=[pltpu.VMEM((ROWS, 2048), BF)],
        compiler_params=params(40),
        cost_estimate=takes(5),
        name="project",
    )(*pieces, raw, *earlier)


def hidden_products_kernel(*refs):
    pieces = refs[:8]
    att_ref, w_ref = refs[8:10]
    grad_att_ref, sum_ref, grad = refs[-3:]
    for k in range(8):
        grad[128 * k : 128 * k + 128, :] = pieces[k][...]
    grad_att_ref[...] = dot_nt(grad[...], w_ref[...]).astype(BF)
    for k in range(4):
        cols = slice(512 * k, 512 * k + 512)
        sum_ref[:, cols] = dot_tn(att_ref[...], grad[:, cols]).astype(BF)


def hidden_products(pieces, att, w_out, *earlier):
    return pl.pallas_call(
        hidden_products_kernel,
        in_specs=[WHOLE] * 10 + [ANYWHERE] * len(earlier),
        out_specs=[WHOLE] * 2,
        out_shape=[jax.ShapeDtypeStruct((ROWS, 256), BF), jax.ShapeDtypeStruct((256, 2048), BF)],
        scratch_shapes=[pltpu.VMEM((ROWS, 2048), BF)],
        compiler_params=params(40),
        cost_estimate=takes(6),
        name="hidden_products",
    )(*pieces, att, w_out, *earlier)


def feed_forward_kernel(*refs):
    hat_pieces, grad_pieces, ff_ref = refs[:8], refs[8:16], refs[16]
    hid_ref, grad_gu_ref, back_mine, back_other, ahead_mine, ahead_other = refs[17:23]
    w_gu, w_down, hat, grad = refs[23:]
    step = pl.program_id(0)

    @pl.when(step == 0)
    def _():
        for f in range(8):
            for zl in range(2):
                r = 2 * f + zl
                for x in range(4):
                    row = 256 * f + 64 * x + 32 * zl
                    w_gu[row : row + 32, :] = ff_ref[192 * r + 32 * x : 192 * r + 32 * x + 32, :]
                w_down[48 * r : 48 * r + 48, :1536] = ff_ref[192 * r + 128 : 192 * r + 176, :]
                for part in range(3):
                    w_down[48 * r + 16 * part : 48 * r + 16 * part + 16, 1536:] = ff_ref[
                        192 * r + 176 : 192 * r + 192, 512 * part : 512 * part + 512
                    ]

    for k in range(4):

        @pl.when(step == k)
        def _():
            for half in range(2):
                piece = (2 * k + 4) % 8 + half
                rows = slice(128 * half, 128 * half + 128)
                hat[rows, :] = hat_pieces[piece][...]
                grad[rows, :] = grad_pieces[piece][...]

    gate_up_val = dot_nn(hat[...], w_gu[...])
    gate = gate_up_val[:, :FP]
    up = gate_up_val[:, FP:]
    sig = jax.nn.sigmoid(gate)
    silu = gate * sig
    hid_ref[...] = (silu * up).astype(BF)
    grad_hid = dot_nt(grad[...], w_down[...])
    grad_gu_ref[:, :FP] = (grad_hid * up * sig * (1.0 + gate * (1.0 - sig))).astype(BF)
    grad_gu_ref[:, FP:] = (grad_hid * silu).astype(BF)
    back = dot_nt(grad_gu_ref[...], w_gu[...]).astype(BF)
    ahead = dot_nn(hid_ref[...], w_down[...]).astype(BF)

    @pl.when(step < 2)
    def _():
        back_other[...] = back
        ahead_other[...] = ahead

    @pl.when(step >= 2)
    def _():
        back_mine[...] = back
        ahead_mine[...] = ahead


def feed_forward(hat_pieces, grad_pieces, ff_all):
    piece = fixed((128, 2048))
    block = lambda cols: pl.BlockSpec((256, cols), lambda i: ((i + 2) % 4, 0))
    mine = pl.BlockSpec((256, 2048), lambda i: (jnp.maximum(i - 2, 0), 0))
    other = pl.BlockSpec((256, 2048), lambda i: (jnp.minimum(i, 1), 0))
    shape = lambda rows, cols: jax.ShapeDtypeStruct((rows, cols), BF)
    half = shape(ROWS // 2, 2048)
    return pl.pallas_call(
        feed_forward_kernel,
        grid=(4,),
        in_specs=[piece] * 16 + [fixed((3072, 1536))],
        out_specs=[block(FP), block(2 * FP), mine, other, mine, other],
        out_shape=[shape(ROWS, FP), shape(ROWS, 2 * FP), half, half, half, half],
        scratch_shapes=[
            pltpu.VMEM((2048, 2 * FP), BF),
            pltpu.VMEM((FP, 2048), BF),
            pltpu.VMEM((256, 2048), BF),
            pltpu.VMEM((256, 2048), BF),
        ],
        compiler_params=params(58),
        cost_estimate=takes(28),
        name="feed_forward",
    )(*hat_pieces, *grad_pieces, ff_all)


def weight_grads_kernel(*refs):
    hat_pieces, grad_pieces = refs[:8], refs[8:16]
    grad_gu_ref, hid_ref = refs[16:18]
    out_ref, hid_t, grad, hat = refs[-4:]

    @pl.when(pl.program_id(0) == 0)
    def _():
        hid_t[...] = hid_ref[...].T
        for k in range(8):
            grad[128 * k : 128 * k + 128, :] = grad_pieces[k][...]

    for k in range(8):
        hat[128 * k : 128 * k + 128, :] = hat_pieces[k][...]
    for half in range(2):
        total = dot_tn(hat[:, 256 * half : 256 * half + 256], grad_gu_ref[...])
        total = total.astype(BF).reshape(4, 2, 32, 2 * FP)
        for zl in range(2):
            out_ref[2 * half + zl, :128, :] = total[:, zl].reshape(128, 2 * FP)
    rows = pl.ds(pl.multiple_of(pl.program_id(0) * 192, 64), 192)
    total = dot_nn(hid_t[rows, :], grad[...]).astype(BF).reshape(4, 48, 2048)
    out_ref[:, 128:176, :] = total[:, :, :1536]
    for part in range(3):
        out_ref[:, 176:192, 512 * part : 512 * part + 512] = total[:, 16 * part : 16 * part + 16, 1536:]


def weight_grads(hat_pieces, grad_pieces, grad_gu, hid, *earlier):
    return pl.pallas_call(
        weight_grads_kernel,
        grid=(4,),
        in_specs=[pl.BlockSpec((128, 512), lambda j: (0, j))] * 8
        + [fixed((128, 2048))] * 8
        + [fixed((ROWS, 2 * FP)), fixed((ROWS, FP))]
        + [ANYWHERE] * len(earlier),
        out_specs=pl.BlockSpec((4, 192, 1536), lambda j: (j, 0, 0)),
        out_shape=jax.ShapeDtypeStruct((16, 192, 1536), BF),
        scratch_shapes=[
            pltpu.VMEM((FP, ROWS), BF),
            pltpu.VMEM((ROWS, 2048), BF),
            pltpu.VMEM((ROWS, 512), BF),
        ],
        compiler_params=params(56),
        cost_estimate=takes(16.5),
        name="weight_grads",
    )(*hat_pieces, *grad_pieces, grad_gu, hid, *earlier)


def ff_columns():
    for f in range(8):
        for x in range(4):
            for zl in range(2):
                for c in range(2):
                    for g in range(2):
                        yield (
                            x * 2 + c,
                            g * FP + (f * 2 + zl) * 48,
                            g * FF + flat_index(f, x, zl, c) * 44,
                        )


def pack_kernel(qkv_ref, gate_up_ref, gains_ref, out_ref, scaled_qkv, scaled, packed):
    gains = gains_ref[...]
    scaled_qkv[...] = qkv_ref[...].astype(BF).astype(F32) * gains[:, 0:1]
    scaled[...] = gate_up_ref[...].astype(BF).astype(F32) * gains[:, 1:2]
    packed[...] = jnp.zeros_like(packed)
    for rank in range(8):
        head = 2048 + rank // 2 * HD
        packed[rank, :, :256] = scaled_qkv[:, rank * 256 : rank * 256 + 256]
        packed[rank, :, 256:320] = scaled_qkv[:, head : head + HD]
        packed[rank, :, 320:384] = scaled_qkv[:, head + 256 : head + 256 + HD]
    for rank, there, here in ff_columns():
        packed[rank, :, 384 + there : 384 + there + 44] = scaled[:, here : here + 44]
    out_ref[...] = packed[...].astype(BF)


def pack(qkv, gate_up, gains):
    return pl.pallas_call(
        pack_kernel,
        in_specs=[WHOLE] * 3,
        out_specs=WHOLE,
        out_shape=jax.ShapeDtypeStruct((8, 16, 1920), BF),
        scratch_shapes=[
            pltpu.VMEM((16, 2560), F32),
            pltpu.VMEM((16, 2 * FF), F32),
            pltpu.VMEM((8, 16, 1920), F32),
        ],
        compiler_params=params(24),
        cost_estimate=takes(3),
        name="pack",
    )(qkv, gate_up, gains)


def update_kernel(
    got_ref, master_ref, gain_ref, first_ref, second_ref, new_first, new_second, new_master, gain_sum, packed, sums
):
    packed[...] = got_ref[...].astype(F32)
    for rank, there, here in ff_columns():
        sums[:, here : here + 44] = packed[rank, :, 384 + there : 384 + there + 44]
    master = master_ref[...]
    gain_sum[...] = jnp.sum(
        master.astype(BF).astype(F32) * sums[...], axis=1, keepdims=True
    )
    new_first[...], new_second[...], new_master[...] = adam_update(
        master,
        sums[...] * gain_ref[...],
        first_ref[...],
        second_ref[...],
        step_rates[2],
        decay_rates[2],
    )


def update_gate_up(got, master, gain, first, second):
    shape = jax.ShapeDtypeStruct((16, 2 * FF), F32)
    return pl.pallas_call(
        update_kernel,
        in_specs=[WHOLE] * 5,
        out_specs=[WHOLE] * 4,
        out_shape=[shape, shape, shape, jax.ShapeDtypeStruct((16, 1), F32)],
        scratch_shapes=[pltpu.VMEM((8, 16, 1920), F32), pltpu.VMEM((16, 2 * FF), F32)],
        compiler_params=params(32),
        cost_estimate=takes(4),
        name="update_gate_up",
    )(got, master, gain, first, second)


def shift(block, distance):
    return lax.ppermute(block, "x", [(i, (i + distance) % 4) for i in range(4)])


def swap(block):
    return lax.ppermute(block, "c", [(0, 1), (1, 0)])


ORDER = ((0, 0), (1, 0), (3, 0), (2, 0), (0, 1), (1, 1), (3, 1), (2, 1))


def tie_kernel(*refs):
    pass


def tie(value, *earlier):
    anywhere = pl.BlockSpec(memory_space=pl.ANY)
    return pl.pallas_call(
        tie_kernel,
        in_specs=[anywhere] * (1 + len(earlier)),
        out_specs=anywhere,
        out_shape=jax.ShapeDtypeStruct(value.shape, value.dtype),
        input_output_aliases={0: 0},
        cost_estimate=pl.CostEstimate(flops=0, bytes_accessed=0, transcendentals=0),
        name="tie",
    )(value, *earlier)


def gather_pieces(block):
    mine = [block, shift(block, 1), shift(block, -1), shift(block, 2)]
    return mine + [swap(piece) for piece in mine]


def scatter_first(mine, other):
    return mine.astype(F32) + swap(other).astype(F32)


def scatter_second(mine):
    far = mine[384:].astype(BF)
    by_left = shift(far[:64], -1)
    by_right = shift(far[64:], 1)
    to_left = jnp.concatenate([mine[128:192] + by_left.astype(F32), mine[192:256]], axis=0)
    to_right = jnp.concatenate([mine[256:320], mine[320:384] + by_right.astype(F32)], axis=0)
    return to_left.astype(BF), to_right.astype(BF), mine[:128]


def scatter_third(to_left, to_right):
    return shift(to_left, -1), shift(to_right, 1)


def total(parts):
    first, second, third = parts
    return first.astype(F32) + second.astype(F32) + third.astype(F32)


def last_products_kernel(place_ref, mixed_ref, w_ref, out_ref, rows):
    for k in range(4):
        first = pl.multiple_of(place_ref[pl.program_id(0) * 4 + k] * 128, 128)
        rows[128 * k : 128 * k + 128, :] = mixed_ref[pl.ds(first, 128), :]
    out_ref[...] = dot_nt(rows[...], w_ref[...]).astype(BF)


def last_products(grad_mixed, w_qkv):
    owner = jnp.arange(8, dtype=jnp.int32)
    dx = (lax.axis_index("x") - owner // 2) % 4
    dc = (lax.axis_index("c") + owner) % 2
    place = 4 * dc + jnp.where(dx < 2, dx, 5 - dx)
    return pl.pallas_call(
        last_products_kernel,
        grid_spec=pltpu.PrefetchScalarGridSpec(
            num_scalar_prefetch=1,
            grid=(2,),
            in_specs=[
                pl.BlockSpec((ROWS, 384), lambda j, place: (0, 0)),
                pl.BlockSpec((2048, 384), lambda j, place: (0, 0)),
            ],
            out_specs=pl.BlockSpec((512, 2048), lambda j, place: (j, 0)),
            scratch_shapes=[pltpu.VMEM((512, 384), BF)],
        ),
        out_shape=jax.ShapeDtypeStruct((ROWS, 2048), BF),
        compiler_params=pltpu.CompilerParams(vmem_limit_bytes=32 * 1024 * 1024),
        cost_estimate=takes(5),
        name="last_products",
    )(place, grad_mixed, w_qkv)


def attn_grads_kernel(*refs):
    pieces = refs[:8]
    mixed_ref, out_grad_ref, sum_ref, hat = refs[8:]
    for k in range(8):
        hat[128 * k : 128 * k + 128, :] = pieces[k][...]
    total = dot_tn(hat[...], mixed_ref[...]).astype(BF).reshape(4, 2, 32, 384)
    for zl in range(2):
        sum_ref[zl, :, :384] = total[:, zl].reshape(128, 384)
        for k in range(8):
            sum_ref[zl, 16 * k : 16 * k + 16, 384:] = out_grad_ref[
                16 * zl : 16 * zl + 16, 256 * k : 256 * k + 256
            ]


def attn_grads(pieces, grad_mixed, sum_out):
    return pl.pallas_call(
        attn_grads_kernel,
        grid=(8,),
        in_specs=[pl.BlockSpec((128, 256), lambda f: (0, f))] * 8
        + [fixed((ROWS, 384)), pl.BlockSpec((32, 2048), lambda f: (f, 0))],
        out_specs=pl.BlockSpec((2, 128, 640), lambda f: (f, 0, 0)),
        out_shape=jax.ShapeDtypeStruct((16, 128, 640), BF),
        scratch_shapes=[pltpu.VMEM((ROWS, 256), BF)],
        compiler_params=params(40),
        cost_estimate=takes(4),
        name="attn_grads",
    )(*pieces, grad_mixed, sum_out)


def row_positions(span_order, zl):
    x = lax.axis_index("x")
    c = lax.axis_index("c")
    holders = jnp.stack([((x - dx) % 4 * 2 + zl) * 2 + (c + dc) % 2 for dx, dc in ORDER])
    picked = (holders[:, None] == jnp.arange(16, dtype=jnp.int32)[None, :]).astype(jnp.int32)
    spans = jnp.sum(picked[:, :, None] * span_order.reshape(1, 16, 2), axis=1)
    return (spans.reshape(16, 1) * 64 + jnp.arange(64, dtype=jnp.int32)[None, :]).reshape(ROWS)


def norm_scale(rows):
    return lax.rsqrt(jnp.mean(rows * rows, axis=-1, keepdims=True) + norm_eps)


def norm_back(grad_hat, hat, scale, rest):
    return rest + scale * (grad_hat - hat * jnp.mean(grad_hat * hat, axis=-1, keepdims=True))


def body(
    tokens,
    out_grad,
    seq_lengths,
    span_order,
    attn_in,
    attn_out,
    gate_up,
    down_proj,
    norm_gains,
    first_attn_in,
    second_attn_in,
    first_attn_out,
    second_attn_out,
    first_gate_up,
    second_gate_up,
    first_down_proj,
    second_down_proj,
    first_norm_gains,
    second_norm_gains,
):
    zl = lax.axis_index("zl")
    gains = norm_gains.astype(BF).astype(F32)
    gain_one = gains[0][:, None]
    gain_two = gains[1][:, None]
    low_qkv = attn_in.astype(BF).astype(F32)

    inputs = tokens.astype(F32)
    scale_one = norm_scale(inputs)
    hat_one = inputs * scale_one
    packed = pack(attn_in, gate_up, gains.T)
    ranked = lax.all_to_all(packed, TP, 0, 0, tiled=True).reshape(128, 1920)
    hat_pieces = gather_pieces(tie(hat_one.astype(BF), ranked))
    qkv_copies = jnp.broadcast_to(ranked[None, :, :384], (16, 128, 384))
    qkv_all = lax.all_to_all(qkv_copies, REP, 0, 0, tiled=True)
    out_part = lax.ppermute(tie(attn_out.astype(BF), ranked), ALL, SPREAD)
    down_rows = jnp.pad(down_proj.astype(BF), ((0, 4), (0, 0)))
    down_tail = [down_rows[16 * part : 16 * part + 16, 1536:] for part in range(3)]
    ff_part = jnp.concatenate(
        [ranked[:, 384:], down_rows[:, :1536], jnp.concatenate(down_tail, axis=1)], axis=0
    )
    ff_all = lax.all_gather(ff_part, REP, axis=0, tiled=True)
    grad_pieces = gather_pieces(tie(out_grad, *hat_pieces[1:4]))

    own_pos = row_positions(span_order, zl)
    other_pos = row_positions(span_order, 1 - zl)
    lengths = seq_lengths[0]
    bound_one = lengths[0]
    bound_two = lengths[0] + lengths[1]
    low_pos = jnp.where(own_pos < bound_one, 0, bound_one)[None, :]
    high_pos = jnp.where(own_pos < bound_two, own_pos, -1)[None, :]
    key_pos = jnp.concatenate([own_pos, other_pos])
    key_pos = jnp.broadcast_to(key_pos[:, None], (KEYS, QB))

    queries, own_kv, w_qkv = project(hat_pieces, qkv_all)
    other_kv = lax.ppermute(own_kv, "zl", [(0, 1), (1, 0)])
    out_copies = jnp.broadcast_to(tie(out_part, own_kv)[None], (16, 16, 2048))
    w_out = lax.all_to_all(out_copies, REP, 0, 0, tiled=True).reshape(256, 2048)
    before = attend(queries, own_kv, key_pos[:ROWS], low_pos, high_pos, None)
    att, lse = attend(
        queries, other_kv, key_pos[ROWS:], low_pos, high_pos, before, *grad_pieces[1:4]
    )
    att_other = dot_nn(att[512:], w_out).astype(BF)
    att_mine = dot_nn(att[:512], w_out)
    to_left, to_right, stays = scatter_second(scatter_first(att_mine, att_other))
    hidden = inputs + total((stays, *scatter_third(to_left, to_right)))

    scale_two = norm_scale(hidden)
    hat_two = hidden * scale_two
    hat_two_pieces = gather_pieces(hat_two.astype(BF))
    hid, grad_gu, back_mine, back_other, ahead_mine, ahead_other = feed_forward(
        hat_two_pieces, grad_pieces, ff_all
    )
    to_left, to_right, stays = scatter_second(scatter_first(back_mine, back_other))
    grad_hat_two = total((stays, *scatter_third(to_left, to_right)))
    grad_hidden = norm_back(grad_hat_two, hat_two, scale_two, out_grad.astype(F32))
    grad_hidden_low = grad_hidden.astype(BF)
    hidden_pieces = gather_pieces(grad_hidden_low)
    sum_ff = weight_grads(hat_two_pieces, grad_pieces, grad_gu, hid, grad_hidden_low)
    all_sum_ff = sum_ff.reshape(16 * 192, 1536)
    sum_ff = lax.psum_scatter(all_sum_ff, REP, scatter_dimension=0, tiled=True)
    grad_att, sum_out = hidden_products(hidden_pieces, att, w_out, all_sum_ff)
    ahead = scatter_first(ahead_mine, tie(ahead_other, hidden_pieces[3]))

    grad_q, grad_kv = attend_back(
        queries, grad_att, att, other_kv, key_pos[ROWS:], low_pos, high_pos, lse, None, ahead
    )
    arrived = lax.ppermute(grad_kv.astype(BF), "zl", [(0, 1), (1, 0)])
    ahead_left, ahead_right, ahead_stays = scatter_second(ahead)
    grad_q, grad_kv = attend_back(
        queries,
        grad_att,
        att,
        own_kv,
        key_pos[:ROWS],
        low_pos,
        high_pos,
        lse,
        grad_q,
        ahead_left,
        ahead_right,
    )
    ahead = scatter_third(ahead_left, ahead_right)
    block_out = (hidden + total((ahead_stays, *ahead))).astype(BF)
    grad_mixed = jnp.concatenate([grad_q, (grad_kv + arrived.astype(F32)).astype(BF)], axis=1)
    grad_mixed = tie(grad_mixed, *ahead)
    attn_sums = attn_grads(hat_pieces, grad_mixed, sum_out)
    attn_sums = lax.all_to_all(attn_sums, REP, 0, 0, tiled=True)
    grad_hat_one = lax.psum_scatter(
        last_products(tie(grad_mixed, sum_ff), w_qkv), TP, scatter_dimension=0, tiled=True
    ).astype(F32)
    attn_sums = jnp.sum(attn_sums.astype(F32), axis=0).astype(BF)
    in_grad = norm_back(grad_hat_one, hat_one, scale_one, grad_hidden).astype(BF)

    got = jnp.concatenate([attn_sums[:, :384], sum_ff[:128]], axis=1).reshape(8, 16, 1920)
    got = lax.all_to_all(got, TP, 0, 0, tiled=True)
    got_qkv = got[:, :, :384].transpose(1, 0, 2).astype(F32)
    got_kv = got_qkv[:, :, 256:].reshape(16, 4, 2, 2, HD).sum(axis=2)
    got_qkv = jnp.concatenate(
        [
            got_qkv[:, :, :256].reshape(16, 2048),
            got_kv[:, :, 0].reshape(16, 256),
            got_kv[:, :, 1].reshape(16, 256),
        ],
        axis=1,
    )
    sum_out = attn_sums[:, 384:].reshape(8, 16, 256).transpose(1, 0, 2).reshape(16, 2048)
    got_out = lax.ppermute(sum_out, ALL, back(SPREAD)).astype(F32)
    tail = [sum_ff[176:192, 512 * part : 512 * part + 512] for part in range(3)]
    got_down = jnp.concatenate([sum_ff[128:176], jnp.concatenate(tail, axis=0)], axis=1)
    got_down = got_down[:44].astype(F32)
    gu_new = update_gate_up(got, gate_up, gain_two, first_gate_up, second_gate_up)
    gain_sums = jnp.stack([jnp.sum(low_qkv * got_qkv, axis=1), gu_new[3][:, 0]], axis=0)
    qkv_new = adam_update(
        attn_in, got_qkv * gain_one, first_attn_in, second_attn_in, step_rates[0], decay_rates[0]
    )
    out_new = adam_update(
        attn_out, got_out, first_attn_out, second_attn_out, step_rates[1], decay_rates[1]
    )
    down_new = adam_update(
        down_proj, got_down, first_down_proj, second_down_proj, step_rates[3], decay_rates[3]
    )
    gains_new = adam_update(
        norm_gains, gain_sums, first_norm_gains, second_norm_gains, step_rates[4], decay_rates[4]
    )
    return (block_out, in_grad, *qkv_new, *out_new, *gu_new[:3], *down_new, *gains_new)


def solution(mesh):
    split = Mesh(mesh.devices.reshape(4, 2, 4, 2, 2), ALL)
    rows = P(ALL, None)
    cols = P(None, ALL)
    group = P(("y", "zh"), None)
    in_specs = (rows, rows, group, P()) + (rows,) * 4 + (cols,) + (rows,) * 8 + (cols,) * 2
    out_specs = (rows,) * 14 + (cols,) * 3
    return jax.shard_map(body, mesh=split, in_specs=in_specs, out_specs=out_specs, check_vma=False)
```

time: 905 us -> 470 us (0.52)
  waiting for transfers between devices: 596 us -> 147 us
  matrix products: 80 us -> 1.46 us
  Pallas kernels: 47.1 us -> 124 us
  starting transfers between devices: 55.5 us -> 112 us
  blocking collectives: 47.9 us -> 0 us
  local copies, waits for them, and re-layouts: 19.3 us -> 31.8 us
    reduce_scatter x7 -> x2, waiting for transfers between devices: 246 us -> 0.61 us  [the longest x1 0.61 us: body(): sum_ff = lax.psum_scatter(all_sum_ff, REP, scatter_dimension=0, tiled=True)]
    all_gather x8 -> x1, waiting for transfers between devices: 244 us -> 0.01 us  [body(): ff_all = lax.all_gather(ff_part, REP, axis=0, tiled=True)]
    pallas_call x2 -> x19, Pallas kernels: 47.1 us -> 124 us  [the longest x1 32.8 us: feed_forward(): pl.pallas_call(feed_forward_kernel, grid=(4,), in_specs=[piece] * 16 + [f...]
    unnamed x17 -> x3, waiting for transfers between devices: 71.9 us -> 0.05 us
    ppermute x8 -> x45, waiting for transfers between devices: 28.1 us -> 99.9 us  [the longest x24 88.1 us: shift(): return lax.ppermute(block, 'x', [(i, (i + distance) % 4) for i in range(4)])]
    dot_general x9 -> x0, matrix products: 51.7 us -> none  [the longest x4 27 us: dot_tn(): lax.dot_general(a, b, (((0,), (0,)), ((), ())), preferred_element_type=F32)]
    all_to_all x2 -> x0, blocking collectives: 47.9 us -> none  [to_rank(): lax.all_to_all(moved, TP, 0, 0, tiled=True).reshape(128, cols.shape[2])]
    all_to_all x2 -> x5, waiting for transfers between devices: 1.14 us -> 46.4 us  [the longest x1 30.9 us: body(): attn_sums = lax.all_to_all(attn_sums, REP, 0, 0, tiled=True)]
  transfers between devices with their start and end apart: 28 -> 55, of which waited for: 21 -> 25; matrix products, arithmetic and copies ran while one was open for 10% -> 6% of each run, Pallas kernels for 5% -> 15%
where the time goes in v3:
time: 470 us; the launch traced here: 461 us
  waiting for transfers between devices  147 us (31%)
  Pallas kernels  124 us (26%)
  starting transfers between devices  112 us (24%)
  local copies, waits for them, and re-layouts  31.8 us (7%)
  other arithmetic  28.1 us (6%)
  between operations  16.8 us (4%)
    ppermute x24, waiting for transfers between devices, shift(): return lax.ppermute(block, 'x', [(i, (i + distance) % 4) for i in range(4)])  88.1 us
    pallas_call x1, Pallas kernels, feed_forward(): pl.pallas_call(feed_forward_kernel, grid=(4,), in_specs=[piece] * 16 + [f...  32.8 us
    all_to_all x1, waiting for transfers between devices, body(): attn_sums = lax.all_to_all(attn_sums, REP, 0, 0, tiled=True)  30.9 us
    ppermute x19, starting transfers between devices, swap(): return lax.ppermute(block, 'c', [(0, 1), (1, 0)])  29.4 us
    ppermute x24, starting transfers between devices, shift(): return lax.ppermute(block, 'x', [(i, (i + distance) % 4) for i in range(4)])  26.5 us
    pallas_call x2, Pallas kernels, attend_back(): pl.pallas_call(functools.partial(attend_back_kernel, first), grid=(ROWS /...  26 us
    unnamed x154, local copies, waits for them, and re-layouts  25.6 us
    pallas_call x2, Pallas kernels, attend(): pl.pallas_call(functools.partial(attend_kernel, first), grid=(ROWS // QB,...  25.6 us
  transfers between devices with their start and end apart: 55, of which 25 were waited for; matrix products, arithmetic and copies ran while one was open for 6% of the time, Pallas kernels for 15%

profile of v3, /device:TPU:17, one launch (start us, length us, event | category | flops | bytes accessed | tf_op | source)
XLA Modules:
  0.0 460.9 jit_solution(11594309174767625951)
XLA Ops:
  12.3 5.0 %all-to-all-start = ((bf16[8,16,1920]{2,1,0:T(8,128)(2,1)}), bf16[8,16,1920]{2,1,0:T(8,128)(2,1)S(1)}, u32[]{:S(2)}, u32[]{:S(2)}) async-start(bf16[8,16,1920]{2,1,0:T(8,128)(2,1)} %pack.1), calls=%async_computation | async-start | bytes 983040 | tf_op jit(solution)/shard_map/all_to_all | solution.py:638
  17.4 9.0 %all-to-all-done = bf16[8,16,1920]{2,1,0:T(8,128)(2,1)S(1)} async-done(((bf16[8,16,1920]{2,1,0:T(8,128)(2,1)}), bf16[8,16,1920]{2,1,0:T(8,128)(2,1)S(1)}, u32[]{:S(2)}, u32[]{:S(2)}) %all-to-all-start) | async-done | bytes 491552 | tf_op jit(solution)/shard_map/all_to_all | solution.py:638
  29.7 7.7 %all-to-all-start.1 = ((bf16[16,128,384]{2,1,0:T(8,128)(2,1)}), bf16[16,128,384]{2,1,0:T(8,128)(2,1)S(1)}, u32[]{:S(2)}, u32[]{:S(2)}) async-start(bf16[16,128,384]{2,1,0:T(8,128)(2,1)} %broadcast_in_dim.17), calls=%async_computation.1 | async-start | bytes 3145728 | tf_op jit(solution)/shard_map/all_to_all | solution.py:641
  43.8 8.3 %collective-permute-done.2.refs_3_ = bf16[128,2048]{1,0:T(8,128)(2,1)S(1)} collective-permute-done((bf16[128,2048]{1,0:T(8,128)(2,1)}, bf16[128,2048]{1,0:T(8,128)(2,1)S(1)}, u32[]{:S(2)}, u32[]{:S(2)}) %collective-permute-start.2) | collective-permute-done | bytes 524320 | tf_op jit(solution)/shard_map/ppermute | solution.py:476
  52.1 4.3 collective-permute-start.6
  56.4 6.3 %collective-permute-done.1.refs_2_ = bf16[128,2048]{1,0:T(8,128)(2,1)S(1)} collective-permute-done((bf16[128,2048]{1,0:T(8,128)(2,1)}, bf16[128,2048]{1,0:T(8,128)(2,1)S(1)}, u32[]{:S(2)}, u32[]{:S(2)}) %collective-permute-start.1) | collective-permute-done | bytes 524320 | tf_op jit(solution)/shard_map/ppermute | solution.py:476
  71.1 4.0 collective-permute-start.11
  79.4 4.8 %project.1 = (bf16[1024,256]{1,0:T(8,128)(2,1)S(1)}, bf16[1024,128]{1,0:T(8,128)(2,1)}, bf16[2048,384]{1,0:T(8,128)(2,1)S(1)}) custom-call(bf16[128,2048]{1,0:T(8,128)(2,1)S(1)} %copy-done.4, bf16[128,2048]{1,0:T(8,128)(2,1)} %collective-permute-done.refs_1_, bf16[128,2048]{1,0:T(8,128)(2,1)S(1)} %copy-done.11, bf16[128,2048]{1,0:T(8,128)(2,1)S(1)} %copy-done.8, ...), custom_call_target="tpu_custom_call" | custom-call | flops 5750000128 | bytes 1048576 | tf_op jit(solution)/shard_map/project/pallas_call | solution.py:235
  90.7 12.8 %all-to-all-start.2 = ((bf16[16,16,2048]{2,1,0:T(8,128)(2,1)}), bf16[16,16,2048]{2,1,0:T(8,128)(2,1)S(1)}, u32[]{:S(2)}, u32[]{:S(2)}) async-start(bf16[16,16,2048]{2,1,0:T(8,128)(2,1)} %broadcast_in_dim.23), calls=%async_computation.2 | async-start | bytes 2097152 | tf_op jit(solution)/shard_map/all_to_all | solution.py:664
  105.4 12.9 %attend.2 = (f32[256,1024]{1,0:T(8,128)S(1)}, f32[4,1024]{1,0:T(4,128)S(1)}, f32[4,1024]{1,0:T(4,128)S(1)}) custom-call(bf16[1024,256]{1,0:T(8,128)(2,1)S(1)} %copy-done.33, bf16[1024,128]{1,0:T(8,128)(2,1)} %get-tuple-element.42.kv_ref.refs_1_, s32[1024,256]{1,0:T(8,128)S(1)} %broadcast_in_dim.22.kp_ref, s32[1,1024]{1,0:T(1,128)S(1)} %get-tuple-element.119.lo_ref, ...), custom_call_target="tpu_custom_call" | custom-call | flops 12650000384 | bytes 1048576 | tf_op jit(solution)/shard_map/attend/pallas_call | solution.py:136
  120.2 12.6 %attend.3 = (bf16[1024,256]{1,0:T(8,128)(2,1)S(1)}, f32[4,1024]{1,0:T(4,128)S(1)}) custom-call(bf16[1024,256]{1,0:T(8,128)(2,1)S(1)} %copy-done.34, bf16[1024,128]{1,0:T(8,128)(2,1)S(1)} %collective-permute-done.7.kv_ref, s32[1024,256]{1,0:T(8,128)S(1)} %broadcast_in_dim.18.kp_ref, s32[1,1024]{1,0:T(1,128)S(1)} %get-tuple-element.119.lo_ref, ...), custom_call_target="tpu_custom_call" | custom-call | flops 12650000384 | bytes 1048576 | tf_op jit(solution)/shard_map/attend/pallas_call | solution.py:136
  136.5 3.8 collective-permute-done.12
  142.7 6.1 %collective-permute-done.13 = bf16[64,2048]{1,0:T(8,128)(2,1)S(1)} collective-permute-done((bf16[64,2048]{1,0:T(8,128)(2,1)S(1)}, bf16[64,2048]{1,0:T(8,128)(2,1)S(1)}, u32[]{:S(2)}, u32[]{:S(2)}) %collective-permute-start.13) | collective-permute-done | bytes 262176 | tf_op jit(solution)/shard_map/ppermute | solution.py:476
  155.4 8.4 %collective-permute-done.16 = bf16[128,2048]{1,0:T(8,128)(2,1)S(1)} collective-permute-done((bf16[128,2048]{1,0:T(8,128)(2,1)S(1)}, bf16[128,2048]{1,0:T(8,128)(2,1)S(1)}, u32[]{:S(2)}, u32[]{:S(2)}) %collective-permute-start.16) | collective-permute-done | bytes 524320 | tf_op jit(solution)/shard_map/ppermute | solution.py:476
  170.7 6.6 %collective-permute-done.19.refs_3_ = bf16[128,2048]{1,0:T(8,128)(2,1)S(1)} collective-permute-done((bf16[128,2048]{1,0:T(8,128)(2,1)S(1)}, bf16[128,2048]{1,0:T(8,128)(2,1)S(1)}, u32[]{:S(2)}, u32[]{:S(2)}) %collective-permute-start.19) | collective-permute-done | bytes 524320 | tf_op jit(solution)/shard_map/ppermute | solution.py:476
  177.2 5.7 %collective-permute-start.23 = (bf16[128,2048]{1,0:T(8,128)(2,1)S(1)}, bf16[128,2048]{1,0:T(8,128)(2,1)S(1)}, u32[]{:S(2)}, u32[]{:S(2)}) collective-permute-start(bf16[128,2048]{1,0:T(8,128)(2,1)S(1)} %collective-permute-done.19.refs_3_), channel_id=1, source_target_pairs={{0,1},{1,0},{2,3},{3,2},{4,5},{5,4},{6,7},{7,6},{8,9},{9,8},{10,11... | collective-permute-start | bytes 1572872 | tf_op jit(solution)/shard_map/ppermute | solution.py:480
  182.9 6.7 %collective-permute-done.18.refs_2_ = bf16[128,2048]{1,0:T(8,128)(2,1)S(1)} collective-permute-done((bf16[128,2048]{1,0:T(8,128)(2,1)S(1)}, bf16[128,2048]{1,0:T(8,128)(2,1)S(1)}, u32[]{:S(2)}, u32[]{:S(2)}) %collective-permute-start.18) | collective-permute-done | bytes 524320 | tf_op jit(solution)/shard_map/ppermute | solution.py:476
  194.2 32.8 %feed_forward.1 = (bf16[1024,768]{1,0:T(8,128)(2,1)}, bf16[1024,1536]{1,0:T(8,128)(2,1)}, bf16[512,2048]{1,0:T(8,128)(2,1)}, bf16[512,2048]{1,0:T(8,128)(2,1)}, ...) custom-call(bf16[128,2048]{1,0:T(8,128)(2,1)} %copy-done.51, bf16[128,2048]{1,0:T(8,128)(2,1)} %copy-done.70, ...), custom_call_target="tpu_custom_call" | custom-call | flops 32199999488 | bytes 1048576 | tf_op jit(solution)/shard_map/feed_forward/pallas_call | solution.py:332
  227.4 4.0 collective-permute-done.28
  236.3 5.4 %collective-permute-done.29 = bf16[64,2048]{1,0:T(8,128)(2,1)S(1)} collective-permute-done((bf16[64,2048]{1,0:T(8,128)(2,1)S(1)}, bf16[64,2048]{1,0:T(8,128)(2,1)S(1)}, u32[]{:S(2)}, u32[]{:S(2)}) %collective-permute-start.29) | collective-permute-done | bytes 262176 | tf_op jit(solution)/shard_map/ppermute | solution.py:476
  247.9 10.1 %collective-permute-done.32 = bf16[128,2048]{1,0:T(8,128)(2,1)S(1)} collective-permute-done((bf16[128,2048]{1,0:T(8,128)(2,1)S(1)}, bf16[128,2048]{1,0:T(8,128)(2,1)S(1)}, u32[]{:S(2)}, u32[]{:S(2)}) %collective-permute-start.32) | collective-permute-done | bytes 524320 | tf_op jit(solution)/shard_map/ppermute | solution.py:476
  260.1 17.0 %weight_grads.1 = bf16[16,192,1536]{2,1,0:T(8,128)(2,1)} custom-call(bf16[128,2048]{1,0:T(8,128)(2,1)} %copy-done.51, bf16[128,2048]{1,0:T(8,128)(2,1)} %copy-done.70, bf16[128,2048]{1,0:T(8,128)(2,1)} %copy-done.69, bf16[128,2048]{1,0:T(8,128)(2,1)} %copy-done.68, bf16[128,2048]{1,0:T(8,128)(2,1)} %copy-done.72, ...), custom_call_target="tpu_custom_call" | custom-call | flops 18975000576 | bytes 1048576 | tf_op jit(solution)/shard_map/weight_grads/pallas_call | solution.py:376
  278.8 11.2 %collective-permute-done.33.refs_1_.refs_3_ = bf16[128,2048]{1,0:T(8,128)(2,1)S(1)} collective-permute-done((bf16[128,2048]{1,0:T(8,128)(2,1)}, bf16[128,2048]{1,0:T(8,128)(2,1)S(1)}, u32[]{:S(2)}, u32[]{:S(2)}) %collective-permute-start.33) | collective-permute-done | bytes 524320 | tf_op jit(solution)/shard_map/ppermute | solution.py:476
  297.1 11.4 %collective-permute-done.40.refs_2_ = bf16[128,2048]{1,0:T(8,128)(2,1)S(1)} collective-permute-done((bf16[128,2048]{1,0:T(8,128)(2,1)}, bf16[128,2048]{1,0:T(8,128)(2,1)S(1)}, u32[]{:S(2)}, u32[]{:S(2)}) %collective-permute-start.40) | collective-permute-done | bytes 524320 | tf_op jit(solution)/shard_map/ppermute | solution.py:476
  325.8 12.2 %attend_back.2 = (f32[256,1024]{1,0:T(8,128)S(1)}, f32[1024,128]{1,0:T(8,128)S(1)}) custom-call(bf16[1024,256]{1,0:T(8,128)(2,1)S(1)} %copy-done.35, bf16[1024,256]{1,0:T(8,128)(2,1)S(1)} %get-tuple-element.53.do_ref, bf16[1024,256]{1,0:T(8,128)(2,1)S(1)} %copy-done.17, bf16[1024,128]{1,0:T(8,128)(2,1)S(1)} %collective-permute-done.7.kv_ref, ...), custom_call_target="tpu_custom_call" | custom-call | flops 14375000064 | bytes 1048576 | tf_op jit(solution)/shard_map/attend_back/pallas_call | solution.py:190
  342.4 13.8 %attend_back.3 = (bf16[1024,256]{1,0:T(8,128)(2,1)S(1)}, f32[1024,128]{1,0:T(8,128)S(1)}) custom-call(bf16[1024,256]{1,0:T(8,128)(2,1)S(1)} %copy-done.35, bf16[1024,256]{1,0:T(8,128)(2,1)S(1)} %get-tuple-element.53.do_ref, bf16[1024,256]{1,0:T(8,128)(2,1)S(1)} %copy-done.17, bf16[1024,128]{1,0:T(8,128)(2,1)} %get-tuple-element.42.kv_ref.refs_1_, ...), custom_call_target="tpu_custom_call" | custom-call | flops 14375000064 | bytes 1048576 | tf_op jit(solution)/shard_map/attend_back/pallas_call | solution.py:190
  359.2 7.6 %attn_grads.1 = bf16[16,128,640]{2,1,0:T(8,128)(2,1)} custom-call(bf16[128,2048]{1,0:T(8,128)(2,1)S(1)} %copy-done.4, bf16[128,2048]{1,0:T(8,128)(2,1)} %collective-permute-done.refs_1_, bf16[128,2048]{1,0:T(8,128)(2,1)S(1)} %copy-done.12, bf16[128,2048]{1,0:T(8,128)(2,1)S(1)} %copy-done.9, bf16[128,2048]{1,0:T(8,128)(2,1)} %collective-permute-done.3.refs_4_, ...), custom_call_target="tpu_custom_call" | custom-call | flops 4600000000 | bytes 1048576 | tf_op jit(solution)/shard_map/attn_grads/pallas_call | solution.py:576
  374.6 6.4 %all-to-all-start.3 = ((bf16[16,128,640]{2,1,0:T(8,128)(2,1)}), bf16[16,128,640]{2,1,0:T(8,128)(2,1)}, u32[]{:S(2)}, u32[]{:S(2)}) async-start(bf16[16,128,640]{2,1,0:T(8,128)(2,1)} %attn_grads.1), calls=%async_computation.5 | async-start | bytes 5242880 | tf_op jit(solution)/shard_map/all_to_all | solution.py:714
  381.2 30.9 %all-to-all-done.3 = bf16[16,128,640]{2,1,0:T(8,128)(2,1)} async-done(((bf16[16,128,640]{2,1,0:T(8,128)(2,1)}), bf16[16,128,640]{2,1,0:T(8,128)(2,1)}, u32[]{:S(2)}, u32[]{:S(2)}) %all-to-all-start.3) | async-done | bytes 2621472 | tf_op jit(solution)/shard_map/all_to_all | solution.py:714
  414.3 8.6 %collective-permute-start.46 = (bf16[16,2048]{1,0:T(8,128)(2,1)S(1)}, bf16[16,2048]{1,0:T(8,128)(2,1)S(1)}, u32[]{:S(2)}, u32[]{:S(2)}) collective-permute-start(bf16[16,2048]{1,0:T(8,128)(2,1)S(1)} %bitcast.57), channel_id=1, source_target_pairs={{0,0},{2,1},{16,2},{18,3},{32,4},{34,5},{48,6},{50,7},{64,8},{66,9... | collective-permute-start | bytes 196616 | tf_op jit(solution)/shard_map/ppermute | solution.py:734
  427.2 7.6 %all-to-all-start.4 = ((bf16[8,16,1920]{2,1,0:T(8,128)(2,1)}), bf16[8,16,1920]{2,1,0:T(8,128)(2,1)S(1)}, u32[]{:S(2)}, u32[]{:S(2)}) async-start(bf16[8,16,1920]{2,1,0:T(8,128)(2,1)} %bitcast.22), calls=%async_computation.6 | async-start | bytes 983040 | tf_op jit(solution)/shard_map/all_to_all | solution.py:722
  437.5 6.5 %all-to-all-done.4.got_ref = bf16[8,16,1920]{2,1,0:T(8,128)(2,1)S(1)} async-done(((bf16[8,16,1920]{2,1,0:T(8,128)(2,1)}), bf16[8,16,1920]{2,1,0:T(8,128)(2,1)S(1)}, u32[]{:S(2)}, u32[]{:S(2)}) %all-to-all-start.4) | async-done | bytes 491552 | tf_op jit(solution)/shard_map/all_to_all | solution.py:722
  (347 shorter events, 133.6 us)
Async XLA Ops:
  17.3 176.9 %all-gather.2.cloned.1.call-start = ((), (), s32[]{:S(2)}) async-start(), calls=%async_computation.7 | async-start | bytes 10027008 | tf_op jit(solution)/shard_map/all_gather | solution.py:648
  29.7 47.7 %all-to-all-start.1 = ((bf16[16,128,384]{2,1,0:T(8,128)(2,1)}), bf16[16,128,384]{2,1,0:T(8,128)(2,1)S(1)}, u32[]{:S(2)}, u32[]{:S(2)}) async-start(bf16[16,128,384]{2,1,0:T(8,128)(2,1)} %broadcast_in_dim.17), calls=%async_computation.1 | async-start | bytes 3145728 | tf_op jit(solution)/shard_map/all_to_all | solution.py:641
  38.8 24.0 %collective-permute-start.1 = (bf16[128,2048]{1,0:T(8,128)(2,1)}, bf16[128,2048]{1,0:T(8,128)(2,1)S(1)}, u32[]{:S(2)}, u32[]{:S(2)}) collective-permute-start(bf16[128,2048]{1,0:T(8,128)(2,1)} %tie.7.refs_0_), channel_id=1, source_target_pairs={{0,12},{4,0},{8,4},{12,8},{1,13},{5,1},{9,5},{13,9},{2,14},{6,2},{... | collective-permute-start | bytes 1572872 | tf_op jit(solution)/shard_map/ppermute | solution.py:476
  41.1 24.2 %collective-permute-start = (bf16[128,2048]{1,0:T(8,128)(2,1)}, bf16[128,2048]{1,0:T(8,128)(2,1)}, u32[]{:S(2)}, u32[]{:S(2)}) collective-permute-start(bf16[128,2048]{1,0:T(8,128)(2,1)} %tie.7.refs_0_), channel_id=1, source_target_pairs={{0,4},{4,8},{8,12},{12,0},{1,5},{5,9},{9,13},{13,1},{2,6},{6,10},{... | collective-permute-start | bytes 1572872 | tf_op jit(solution)/shard_map/ppermute | solution.py:476
  41.8 33.4 %collective-permute-start.3 = (bf16[128,2048]{1,0:T(8,128)(2,1)}, bf16[128,2048]{1,0:T(8,128)(2,1)}, u32[]{:S(2)}, u32[]{:S(2)}) collective-permute-start(bf16[128,2048]{1,0:T(8,128)(2,1)} %tie.7.refs_0_), channel_id=1, source_target_pairs={{0,1},{1,0},{2,3},{3,2},{4,5},{5,4},{6,7},{7,6},{8,9},{9,8},{10,11... | collective-permute-start | bytes 1572872 | tf_op jit(solution)/shard_map/ppermute | solution.py:480
  52.1 23.4 %collective-permute-start.6 = (bf16[128,2048]{1,0:T(8,128)(2,1)S(1)}, bf16[128,2048]{1,0:T(8,128)(2,1)}, u32[]{:S(2)}, u32[]{:S(2)}) collective-permute-start(bf16[128,2048]{1,0:T(8,128)(2,1)S(1)} %collective-permute-done.2.refs_3_), channel_id=1, source_target_pairs={{0,1},{1,0},{2,3},{3,2},{4,5},{5,4},{6,7},{7,6},{8,9},{9,8},{10,11... | collective-permute-start | bytes 1572872 | tf_op jit(solution)/shard_map/ppermute | solution.py:480
  62.8 14.5 %collective-permute-start.5 = (bf16[128,2048]{1,0:T(8,128)(2,1)S(1)}, bf16[128,2048]{1,0:T(8,128)(2,1)}, u32[]{:S(2)}, u32[]{:S(2)}) collective-permute-start(bf16[128,2048]{1,0:T(8,128)(2,1)S(1)} %collective-permute-done.1.refs_2_), channel_id=1, source_target_pairs={{0,1},{1,0},{2,3},{3,2},{4,5},{5,4},{6,7},{7,6},{8,9},{9,8},{10,11... | collective-permute-start | bytes 1572872 | tf_op jit(solution)/shard_map/ppermute | solution.py:480
  71.1 17.0 %collective-permute-start.11 = (bf16[16,2048]{1,0:T(8,128)(2,1)}, bf16[16,2048]{1,0:T(8,128)(2,1)S(1)}, u32[]{:S(2)}, u32[]{:S(2)}) collective-permute-start(bf16[16,2048]{1,0:T(8,128)(2,1)} %tie.9), channel_id=1, source_target_pairs={{0,0},{1,2},{2,16},{3,18},{4,32},{5,34},{6,48},{7,50},{8,64},{9,66... | collective-permute-start | bytes 196616 | tf_op jit(solution)/shard_map/ppermute | solution.py:642
  75.2 43.2 %collective-permute-start.10 = (bf16[128,2048]{1,0:T(8,128)(2,1)}, bf16[128,2048]{1,0:T(8,128)(2,1)}, u32[]{:S(2)}, u32[]{:S(2)}) collective-permute-start(bf16[128,2048]{1,0:T(8,128)(2,1)} %tie.8.refs_8_), channel_id=1, source_target_pairs={{0,8},{4,12},{8,0},{12,4},{1,9},{5,13},{9,1},{13,5},{2,10},{6,14},... | collective-permute-start | bytes 1572872 | tf_op jit(solution)/shard_map/ppermute | solution.py:476
  75.5 42.8 %collective-permute-start.9 = (bf16[128,2048]{1,0:T(8,128)(2,1)}, bf16[128,2048]{1,0:T(8,128)(2,1)S(1)}, u32[]{:S(2)}, u32[]{:S(2)}) collective-permute-start(bf16[128,2048]{1,0:T(8,128)(2,1)} %tie.8.refs_8_), channel_id=1, source_target_pairs={{0,12},{4,0},{8,4},{12,8},{1,13},{5,1},{9,5},{13,9},{2,14},{6,2},{... | collective-permute-start | bytes 1572872 | tf_op jit(solution)/shard_map/ppermute | solution.py:476
  77.3 41.0 %collective-permute-start.8 = (bf16[128,2048]{1,0:T(8,128)(2,1)}, bf16[128,2048]{1,0:T(8,128)(2,1)}, u32[]{:S(2)}, u32[]{:S(2)}) collective-permute-start(bf16[128,2048]{1,0:T(8,128)(2,1)} %tie.8.refs_8_), channel_id=1, source_target_pairs={{0,4},{4,8},{8,12},{12,0},{1,5},{5,9},{9,13},{13,1},{2,6},{6,10},{... | collective-permute-start | bytes 1572872 | tf_op jit(solution)/shard_map/ppermute | solution.py:476
  86.2 32.2 %collective-permute-start.7 = (bf16[1024,128]{1,0:T(8,128)(2,1)}, bf16[1024,128]{1,0:T(8,128)(2,1)S(1)}, u32[]{:S(2)}, u32[]{:S(2)}) collective-permute-start(bf16[1024,128]{1,0:T(8,128)(2,1)} %get-tuple-element.42.kv_ref.refs_1_), channel_id=1, source_target_pairs={{0,2},{2,0},{1,3},{3,1},{4,6},{6,4},{5,7},{7,5},{8,10},{10,8},{9,1... | collective-permute-start | bytes 786440 | tf_op jit(solution)/shard_map/ppermute | solution.py:662
  90.7 43.1 %all-to-all-start.2 = ((bf16[16,16,2048]{2,1,0:T(8,128)(2,1)}), bf16[16,16,2048]{2,1,0:T(8,128)(2,1)S(1)}, u32[]{:S(2)}, u32[]{:S(2)}) async-start(bf16[16,16,2048]{2,1,0:T(8,128)(2,1)} %broadcast_in_dim.23), calls=%async_computation.2 | async-start | bytes 2097152 | tf_op jit(solution)/shard_map/all_to_all | solution.py:664
  103.6 263.9 %reduce-scatter.3.cloned.1.call-start = ((), (), s32[]{:S(2)}) async-start(), calls=%async_computation.8 | async-start | bytes 10027008 | tf_op jit(solution)/shard_map/reduce_scatter | solution.py:687
  154.9 15.7 %collective-permute-start.26 = (bf16[128,2048]{1,0:T(8,128)(2,1)S(1)}, bf16[128,2048]{1,0:T(8,128)(2,1)S(1)}, u32[]{:S(2)}, u32[]{:S(2)}) collective-permute-start(bf16[128,2048]{1,0:T(8,128)(2,1)S(1)} %copy-done.27), channel_id=1, source_target_pairs={{0,1},{1,0},{2,3},{3,2},{4,5},{5,4},{6,7},{7,6},{8,9},{9,8},{10,11... | collective-permute-start | bytes 1572872 | tf_op jit(solution)/shard_map/ppermute | solution.py:480
  165.7 24.0 %collective-permute-start.18 = (bf16[128,2048]{1,0:T(8,128)(2,1)S(1)}, bf16[128,2048]{1,0:T(8,128)(2,1)S(1)}, u32[]{:S(2)}, u32[]{:S(2)}) collective-permute-start(bf16[128,2048]{1,0:T(8,128)(2,1)S(1)} %multiply_convert_fusion.refs_0_), channel_id=1, source_target_pairs={{0,12},{4,0},{8,4},{12,8},{1,13},{5,1},{9,5},{13,9},{2,14},{6,2},{... | collective-permute-start | bytes 1572872 | tf_op jit(solution)/shard_map/ppermute | solution.py:476
  167.0 24.8 %collective-permute-start.17 = (bf16[128,2048]{1,0:T(8,128)(2,1)S(1)}, bf16[128,2048]{1,0:T(8,128)(2,1)S(1)}, u32[]{:S(2)}, u32[]{:S(2)}) collective-permute-start(bf16[128,2048]{1,0:T(8,128)(2,1)S(1)} %multiply_convert_fusion.refs_0_), channel_id=1, source_target_pairs={{0,4},{4,8},{8,12},{12,0},{1,5},{5,9},{9,13},{13,1},{2,6},{6,10},{... | collective-permute-start | bytes 1572872 | tf_op jit(solution)/shard_map/ppermute | solution.py:476
  167.6 24.3 %collective-permute-start.25 = (bf16[128,2048]{1,0:T(8,128)(2,1)}, bf16[128,2048]{1,0:T(8,128)(2,1)S(1)}, u32[]{:S(2)}, u32[]{:S(2)}) collective-permute-start(bf16[128,2048]{1,0:T(8,128)(2,1)} %collective-permute-done.8.rest_3_.refs_9_), channel_id=1, source_target_pairs={{0,1},{1,0},{2,3},{3,2},{4,5},{5,4},{6,7},{7,6},{8,9},{9,8},{10,11... | collective-permute-start | bytes 1572872 | tf_op jit(solution)/shard_map/ppermute | solution.py:480
  170.5 21.4 %collective-permute-start.20 = (bf16[128,2048]{1,0:T(8,128)(2,1)S(1)}, bf16[128,2048]{1,0:T(8,128)(2,1)S(1)}, u32[]{:S(2)}, u32[]{:S(2)}) collective-permute-start(bf16[128,2048]{1,0:T(8,128)(2,1)S(1)} %multiply_convert_fusion.refs_0_), channel_id=1, source_target_pairs={{0,1},{1,0},{2,3},{3,2},{4,5},{5,4},{6,7},{7,6},{8,9},{9,8},{10,11... | collective-permute-start | bytes 1572872 | tf_op jit(solution)/shard_map/ppermute | solution.py:480
  177.2 14.7 %collective-permute-start.23 = (bf16[128,2048]{1,0:T(8,128)(2,1)S(1)}, bf16[128,2048]{1,0:T(8,128)(2,1)S(1)}, u32[]{:S(2)}, u32[]{:S(2)}) collective-permute-start(bf16[128,2048]{1,0:T(8,128)(2,1)S(1)} %collective-permute-done.19.refs_3_), channel_id=1, source_target_pairs={{0,1},{1,0},{2,3},{3,2},{4,5},{5,4},{6,7},{7,6},{8,9},{9,8},{10,11... | collective-permute-start | bytes 1572872 | tf_op jit(solution)/shard_map/ppermute | solution.py:480
  277.1 173.2 %reduce-scatter.5.cloned.1.call-start = ((), (), s32[]{:S(2)}) async-start(), calls=%async_computation.9 | async-start | bytes 4718592 | tf_op jit(solution)/shard_map/reduce_scatter | solution.py:715
  290.7 31.0 %collective-permute-start.34 = (bf16[512,2048]{1,0:T(8,128)(2,1)}, bf16[512,2048]{1,0:T(8,128)(2,1)S(1)}, u32[]{:S(2)}, u32[]{:S(2)}) collective-permute-start(bf16[512,2048]{1,0:T(8,128)(2,1)} %tie.11), channel_id=1, source_target_pairs={{0,1},{1,0},{2,3},{3,2},{4,5},{5,4},{6,7},{7,6},{8,9},{9,8},{10,11... | collective-permute-start | bytes 6291464 | tf_op jit(solution)/shard_map/ppermute | solution.py:480
  294.1 14.4 %collective-permute-start.40 = (bf16[128,2048]{1,0:T(8,128)(2,1)}, bf16[128,2048]{1,0:T(8,128)(2,1)S(1)}, u32[]{:S(2)}, u32[]{:S(2)}) collective-permute-start(bf16[128,2048]{1,0:T(8,128)(2,1)} %get-tuple-element.79.refs_18_.refs_0_), channel_id=1, source_target_pairs={{0,12},{4,0},{8,4},{12,8},{1,13},{5,1},{9,5},{13,9},{2,14},{6,2},{... | collective-permute-start | bytes 1572872 | tf_op jit(solution)/shard_map/ppermute | solution.py:476
  296.8 14.8 %collective-permute-start.39 = (bf16[128,2048]{1,0:T(8,128)(2,1)}, bf16[128,2048]{1,0:T(8,128)(2,1)S(1)}, u32[]{:S(2)}, u32[]{:S(2)}) collective-permute-start(bf16[128,2048]{1,0:T(8,128)(2,1)} %get-tuple-element.79.refs_18_.refs_0_), channel_id=1, source_target_pairs={{0,4},{4,8},{8,12},{12,0},{1,5},{5,9},{9,13},{13,1},{2,6},{6,10},{... | collective-permute-start | bytes 1572872 | tf_op jit(solution)/shard_map/ppermute | solution.py:476
  296.8 15.8 %collective-permute-start.41 = (bf16[128,2048]{1,0:T(8,128)(2,1)}, bf16[128,2048]{1,0:T(8,128)(2,1)S(1)}, u32[]{:S(2)}, u32[]{:S(2)}) collective-permute-start(bf16[128,2048]{1,0:T(8,128)(2,1)} %get-tuple-element.79.refs_18_.refs_0_), channel_id=1, source_target_pairs={{0,1},{1,0},{2,3},{3,2},{4,5},{5,4},{6,7},{7,6},{8,9},{9,8},{10,11... | collective-permute-start | bytes 1572872 | tf_op jit(solution)/shard_map/ppermute | solution.py:480
  322.8 16.6 %collective-permute-start.35 = (bf16[64,2048]{1,0:T(8,128)(2,1)S(1)}, bf16[64,2048]{1,0:T(8,128)(2,1)S(1)}, u32[]{:S(2)}, u32[]{:S(2)}) collective-permute-start(bf16[64,2048]{1,0:T(8,128)(2,1)S(1)} %get-tuple-element.93), channel_id=1, source_target_pairs={{0,12},{4,0},{8,4},{12,8},{1,13},{5,1},{9,5},{13,9},{2,14},{6,2},{... | collective-permute-start | bytes 786440 | tf_op jit(solution)/shard_map/ppermute | solution.py:476
  323.7 15.7 %collective-permute-start.37 = (bf16[64,2048]{1,0:T(8,128)(2,1)S(1)}, bf16[64,2048]{1,0:T(8,128)(2,1)S(1)}, u32[]{:S(2)}, u32[]{:S(2)}) collective-permute-start(bf16[64,2048]{1,0:T(8,128)(2,1)S(1)} %get-tuple-element.94), channel_id=1, source_target_pairs={{0,4},{4,8},{8,12},{12,0},{1,5},{5,9},{9,13},{13,1},{2,6},{6,10},{... | collective-permute-start | bytes 786440 | tf_op jit(solution)/shard_map/ppermute | solution.py:476
  338.1 18.1 %collective-permute-start.45 = (bf16[1024,128]{1,0:T(8,128)(2,1)S(1)}, bf16[1024,128]{1,0:T(8,128)(2,1)S(1)}, u32[]{:S(2)}, u32[]{:S(2)}) collective-permute-start(bf16[1024,128]{1,0:T(8,128)(2,1)S(1)} %convert_element_type.174), channel_id=1, source_target_pairs={{0,2},{2,0},{1,3},{3,1},{4,6},{6,4},{5,7},{7,5},{8,10},{10,8},{9,1... | collective-permute-start | bytes 786440 | tf_op jit(solution)/shard_map/ppermute | solution.py:694
  339.5 17.7 %collective-permute-start.38 = (bf16[128,2048]{1,0:T(8,128)(2,1)S(1)}, bf16[128,2048]{1,0:T(8,128)(2,1)S(1)}, u32[]{:S(2)}, u32[]{:S(2)}) collective-permute-start(bf16[128,2048]{1,0:T(8,128)(2,1)S(1)} %pad_maximum_fusion.6.rest_2_), channel_id=1, source_target_pairs={{0,4},{4,8},{8,12},{12,0},{1,5},{5,9},{9,13},{13,1},{2,6},{6,10},{... | collective-permute-start | bytes 1572872 | tf_op jit(solution)/shard_map/ppermute | solution.py:476
  339.6 17.6 %collective-permute-start.36 = (bf16[128,2048]{1,0:T(8,128)(2,1)S(1)}, bf16[128,2048]{1,0:T(8,128)(2,1)}, u32[]{:S(2)}, u32[]{:S(2)}) collective-permute-start(bf16[128,2048]{1,0:T(8,128)(2,1)S(1)} %pad_maximum_fusion.5.rest_1_), channel_id=1, source_target_pairs={{0,12},{4,0},{8,4},{12,8},{1,13},{5,1},{9,5},{13,9},{2,14},{6,2},{... | collective-permute-start | bytes 1572872 | tf_op jit(solution)/shard_map/ppermute | solution.py:476
  374.6 37.4 %all-to-all-start.3 = ((bf16[16,128,640]{2,1,0:T(8,128)(2,1)}), bf16[16,128,640]{2,1,0:T(8,128)(2,1)}, u32[]{:S(2)}, u32[]{:S(2)}) async-start(bf16[16,128,640]{2,1,0:T(8,128)(2,1)} %attn_grads.1), calls=%async_computation.5 | async-start | bytes 5242880 | tf_op jit(solution)/shard_map/all_to_all | solution.py:714
  427.2 16.8 %all-to-all-start.4 = ((bf16[8,16,1920]{2,1,0:T(8,128)(2,1)}), bf16[8,16,1920]{2,1,0:T(8,128)(2,1)S(1)}, u32[]{:S(2)}, u32[]{:S(2)}) async-start(bf16[8,16,1920]{2,1,0:T(8,128)(2,1)} %bitcast.22), calls=%async_computation.6 | async-start | bytes 983040 | tf_op jit(solution)/shard_map/all_to_all | solution.py:722
  (100 other events, 816.5 us)
Sparse Core Ops, SparseCore 0:
  27.5 104.4 all-gather.1
  277.3 90.1 reduce-scatter.2
  374.8 35.4 reduce-scatter.4

commit v4 on v3

--- a/solution.py
+++ b/solution.py
@@ -211,18 +211,35 @@
     )(q, do, o, kv, kp, lo, hi, lse, *carried, *earlier)
 
 
+def fetch(pieces, rows, sems):
+    copies = [
+        pltpu.make_async_copy(piece, rows.at[pl.ds(128 * k, 128), :], sems.at[k])
+        for k, piece in enumerate(pieces)
+    ]
+    for copy in copies:
+        copy.start()
+    return copies
+
+
 def project_kernel(*refs):
-    pieces = refs[:8]
-    raw_ref = refs[8]
-    q_ref, kv_ref, w_ref = refs[-4:-1]
-    hat = refs[-1]
+    pieces, raw_hbm = refs[:8], refs[8]
+    q_ref, kv_ref, w_ref, w_out_ref, hat, raw_ref, sems, raw_sem = refs[9:]
+    raw_copy = pltpu.make_async_copy(raw_hbm, raw_ref, raw_sem)
+    raw_copy.start()
+    copies = fetch(pieces, hat, sems)
+    raw_copy.wait()
     for f in range(8):
         for zl in range(2):
+            r = 2 * f + zl
             for x in range(4):
                 row = 256 * f + 64 * x + 32 * zl
-                w_ref[row : row + 32, :] = raw_ref[2 * f + zl, 32 * x : 32 * x + 32, :]
-    for k in range(8):
-        hat[128 * k : 128 * k + 128, :] = pieces[k][...]
+                w_ref[row : row + 32, :] = raw_ref[128 * r + 32 * x : 128 * r + 32 * x + 32, :384]
+            for k in range(8):
+                w_out_ref[16 * r : 16 * r + 16, 256 * k : 256 * k + 256] = raw_ref[
+                    128 * r + 16 * k : 128 * r + 16 * k + 16, 384:
+                ]
+    for copy in copies:
+        copy.wait()
     for k in range(2):
         rows = slice(512 * k, 512 * k + 512)
         product = dot_nn(hat[rows, :], w_ref[...]).astype(BF)
@@ -230,26 +247,31 @@
         kv_ref[rows, :] = product[:, 256:]
 
 
-def project(pieces, raw, *earlier):
+def project(pieces, raw):
     shape = lambda *dims: jax.ShapeDtypeStruct(dims, BF)
     return pl.pallas_call(
         project_kernel,
-        in_specs=[WHOLE] * 9 + [ANYWHERE] * len(earlier),
-        out_specs=[WHOLE] * 3,
-        out_shape=[shape(ROWS, 256), shape(ROWS, 128), shape(2048, 384)],
-        scratch_shapes=[pltpu.VMEM((ROWS, 2048), BF)],
-        compiler_params=params(40),
+        in_specs=[ANYWHERE] * 9,
+        out_specs=[WHOLE] * 4,
+        out_shape=[shape(ROWS, 256), shape(ROWS, 128), shape(2048, 384), shape(256, 2048)],
+        scratch_shapes=[
+            pltpu.VMEM((ROWS, 2048), BF),
+            pltpu.VMEM((2048, 640), BF),
+            pltpu.SemaphoreType.DMA((8,)),
+            pltpu.SemaphoreType.DMA,
+        ],
+        compiler_params=params(60),
         cost_estimate=takes(5),
         name="project",
-    )(*pieces, raw, *earlier)
+    )(*pieces, raw)
 
 
 def hidden_products_kernel(*refs):
     pieces = refs[:8]
     att_ref, w_ref = refs[8:10]
-    grad_att_ref, sum_ref, grad = refs[-3:]
-    for k in range(8):
-        grad[128 * k : 128 * k + 128, :] = pieces[k][...]
+    grad_att_ref, sum_ref, grad, sems = refs[-4:]
+    for copy in fetch(pieces, grad, sems):
+        copy.wait()
     grad_att_ref[...] = dot_nt(grad[...], w_ref[...]).astype(BF)
     for k in range(4):
         cols = slice(512 * k, 512 * k + 512)
@@ -259,11 +281,11 @@
 def hidden_products(pieces, att, w_out, *earlier):
     return pl.pallas_call(
         hidden_products_kernel,
-        in_specs=[WHOLE] * 10 + [ANYWHERE] * len(earlier),
+        in_specs=[ANYWHERE] * 8 + [WHOLE] * 2 + [ANYWHERE] * len(earlier),
         out_specs=[WHOLE] * 2,
         out_shape=[jax.ShapeDtypeStruct((ROWS, 256), BF), jax.ShapeDtypeStruct((256, 2048), BF)],
-        scratch_shapes=[pltpu.VMEM((ROWS, 2048), BF)],
-        compiler_params=params(40),
+        scratch_shapes=[pltpu.VMEM((ROWS, 2048), BF), pltpu.SemaphoreType.DMA((8,))],
+        compiler_params=params(60),
         cost_estimate=takes(6),
         name="hidden_products",
     )(*pieces, att, w_out, *earlier)
@@ -272,79 +294,117 @@
 def feed_forward_kernel(*refs):
     hat_pieces, grad_pieces, ff_ref = refs[:8], refs[8:16], refs[16]
     hid_ref, grad_gu_ref, back_mine, back_other, ahead_mine, ahead_other = refs[17:23]
-    w_gu, w_down, hat, grad = refs[23:]
+    w_gu_ref, w_down_ref, hat, grad, w_sems, hat_sems, grad_sems = refs[23:]
     step = pl.program_id(0)
+
+    def copies(first, count):
+        return (
+            [
+                pltpu.make_async_copy(
+                    hat_pieces[k], hat.at[pl.ds(128 * k, 128), :], hat_sems.at[k]
+                )
+                for k in range(first, first + count)
+            ],
+            [
+                pltpu.make_async_copy(
+                    grad_pieces[k], grad.at[pl.ds(128 * k, 128), :], grad_sems.at[k]
+                )
+                for k in range(first, first + count)
+            ],
+        )
+
+    gu_copies = [
+        pltpu.make_async_copy(
+            ff_ref.at[:, zl, pl.ds(0, 4)], w_gu_ref.at[:, :, zl], w_sems.at[zl]
+        )
+        for zl in range(2)
+    ]
+    down_copies = [
+        pltpu.make_async_copy(
+            ff_ref.at[:, :, 4], w_down_ref.at[:, :, pl.ds(0, 32), pl.ds(0, 1536)], w_sems.at[2]
+        ),
+        pltpu.make_async_copy(
+            ff_ref.at[:, :, 5, pl.ds(0, 16)],
+            w_down_ref.at[:, :, pl.ds(32, 16), pl.ds(0, 1536)],
+            w_sems.at[3],
+        ),
+    ] + [
+        pltpu.make_async_copy(
+            ff_ref.at[:, :, 5, pl.ds(16, 16), pl.ds(512 * part, 512)],
+            w_down_ref.at[:, :, pl.ds(16 * part, 16), pl.ds(1536, 512)],
+            w_sems.at[4 + part],
+        )
+        for part in range(3)
+    ]
+    mine_hat, mine_grad = copies(0, 4)
+    other_hat, other_grad = copies(4, 4)
 
     @pl.when(step == 0)
     def _():
-        for f in range(8):
-            for zl in range(2):
-                r = 2 * f + zl
-                for x in range(4):
-                    row = 256 * f + 64 * x + 32 * zl
-                    w_gu[row : row + 32, :] = ff_ref[192 * r + 32 * x : 192 * r + 32 * x + 32, :]
-                w_down[48 * r : 48 * r + 48, :1536] = ff_ref[192 * r + 128 : 192 * r + 176, :]
-                for part in range(3):
-                    w_down[48 * r + 16 * part : 48 * r + 16 * part + 16, 1536:] = ff_ref[
-                        192 * r + 176 : 192 * r + 192, 512 * part : 512 * part + 512
-                    ]
-
-    for k in range(4):
-
-        @pl.when(step == k)
-        def _():
-            for half in range(2):
-                piece = (2 * k + 4) % 8 + half
-                rows = slice(128 * half, 128 * half + 128)
-                hat[rows, :] = hat_pieces[piece][...]
-                grad[rows, :] = grad_pieces[piece][...]
-
-    gate_up_val = dot_nn(hat[...], w_gu[...])
+        for copy in gu_copies + other_hat + down_copies + other_grad + mine_hat + mine_grad:
+            copy.start()
+        for copy in gu_copies + other_hat:
+            copy.wait()
+
+    @pl.when(step == 1)
+    def _():
+        for copy in mine_hat + mine_grad:
+            copy.wait()
+
+    rows = pl.ds(pl.multiple_of((1 - step) * 512, 512), 512)
+    w_gu = w_gu_ref[...].reshape(2048, 2 * FP)
+    gate_up_val = dot_nn(hat[rows, :], w_gu)
     gate = gate_up_val[:, :FP]
     up = gate_up_val[:, FP:]
     sig = jax.nn.sigmoid(gate)
     silu = gate * sig
     hid_ref[...] = (silu * up).astype(BF)
-    grad_hid = dot_nt(grad[...], w_down[...])
+
+    @pl.when(step == 0)
+    def _():
+        for copy in down_copies + other_grad:
+            copy.wait()
+
+    w_down = w_down_ref[...].reshape(FP, 2048)
+    grad_hid = dot_nt(grad[rows, :], w_down)
     grad_gu_ref[:, :FP] = (grad_hid * up * sig * (1.0 + gate * (1.0 - sig))).astype(BF)
     grad_gu_ref[:, FP:] = (grad_hid * silu).astype(BF)
-    back = dot_nt(grad_gu_ref[...], w_gu[...]).astype(BF)
-    ahead = dot_nn(hid_ref[...], w_down[...]).astype(BF)
-
-    @pl.when(step < 2)
-    def _():
-        back_other[...] = back
-        ahead_other[...] = ahead
-
-    @pl.when(step >= 2)
-    def _():
-        back_mine[...] = back
-        ahead_mine[...] = ahead
+    for back_ref, ahead_ref, now in ((back_other, ahead_other, 0), (back_mine, ahead_mine, 1)):
+
+        @pl.when(step == now)
+        def _():
+            for k in range(2):
+                cols = slice(1024 * k, 1024 * k + 1024)
+                w_cols = w_gu_ref[4 * k : 4 * k + 4].reshape(1024, 2 * FP)
+                back_ref[:, cols] = dot_nt(grad_gu_ref[...], w_cols).astype(BF)
+                w_cols = w_down_ref[:, :, :, cols].reshape(FP, 1024)
+                ahead_ref[:, cols] = dot_nn(hid_ref[...], w_cols).astype(BF)
 
 
 def feed_forward(hat_pieces, grad_pieces, ff_all):
-    piece = fixed((128, 2048))
-    block = lambda cols: pl.BlockSpec((256, cols), lambda i: ((i + 2) % 4, 0))
-    mine = pl.BlockSpec((256, 2048), lambda i: (jnp.maximum(i - 2, 0), 0))
-    other = pl.BlockSpec((256, 2048), lambda i: (jnp.minimum(i, 1), 0))
+    block = lambda cols: pl.BlockSpec((512, cols), lambda i: (1 - i, 0))
+    held = pl.BlockSpec((512, 2048), lambda i: (0, 0))
     shape = lambda rows, cols: jax.ShapeDtypeStruct((rows, cols), BF)
     half = shape(ROWS // 2, 2048)
     return pl.pallas_call(
         feed_forward_kernel,
-        grid=(4,),
-        in_specs=[piece] * 16 + [fixed((3072, 1536))],
-        out_specs=[block(FP), block(2 * FP), mine, other, mine, other],
-        out_shape=[shape(ROWS, FP), shape(ROWS, 2 * FP), half, half, half, half],
+        grid=(2,),
+        in_specs=[ANYWHERE] * 17,
+        out_specs=[block(FP), block(2 * FP)] + [held] * 4,
+        out_shape=[shape(ROWS, FP), shape(ROWS, 2 * FP)] + [half] * 4,
         scratch_shapes=[
-            pltpu.VMEM((2048, 2 * FP), BF),
-            pltpu.VMEM((FP, 2048), BF),
-            pltpu.VMEM((256, 2048), BF),
-            pltpu.VMEM((256, 2048), BF),
+            pltpu.VMEM((8, 4, 2, 32, 2 * FP), BF),
+            pltpu.VMEM((8, 2, 48, 2048), BF),
+            pltpu.VMEM((ROWS, 2048), BF),
+            pltpu.VMEM((ROWS, 2048), BF),
+            pltpu.SemaphoreType.DMA((7,)),
+            pltpu.SemaphoreType.DMA((8,)),
+            pltpu.SemaphoreType.DMA((8,)),
         ],
-        compiler_params=params(58),
+        compiler_params=params(60),
         cost_estimate=takes(28),
         name="feed_forward",
-    )(*hat_pieces, *grad_pieces, ff_all)
+    )(*hat_pieces, *grad_pieces, ff_all.reshape(8, 2, 6, 32, 1536))
 
 
 def weight_grads_kernel(*refs):
@@ -527,61 +587,32 @@
     return first.astype(F32) + second.astype(F32) + third.astype(F32)
 
 
-def last_products_kernel(place_ref, mixed_ref, w_ref, out_ref, rows):
-    for k in range(4):
-        first = pl.multiple_of(place_ref[pl.program_id(0) * 4 + k] * 128, 128)
-        rows[128 * k : 128 * k + 128, :] = mixed_ref[pl.ds(first, 128), :]
-    out_ref[...] = dot_nt(rows[...], w_ref[...]).astype(BF)
-
-
-def last_products(grad_mixed, w_qkv):
-    owner = jnp.arange(8, dtype=jnp.int32)
-    dx = (lax.axis_index("x") - owner // 2) % 4
-    dc = (lax.axis_index("c") + owner) % 2
-    place = 4 * dc + jnp.where(dx < 2, dx, 5 - dx)
-    return pl.pallas_call(
-        last_products_kernel,
-        grid_spec=pltpu.PrefetchScalarGridSpec(
-            num_scalar_prefetch=1,
-            grid=(2,),
-            in_specs=[
-                pl.BlockSpec((ROWS, 384), lambda j, place: (0, 0)),
-                pl.BlockSpec((2048, 384), lambda j, place: (0, 0)),
-            ],
-            out_specs=pl.BlockSpec((512, 2048), lambda j, place: (j, 0)),
-            scratch_shapes=[pltpu.VMEM((512, 384), BF)],
-        ),
-        out_shape=jax.ShapeDtypeStruct((ROWS, 2048), BF),
-        compiler_params=pltpu.CompilerParams(vmem_limit_bytes=32 * 1024 * 1024),
-        cost_estimate=takes(5),
-        name="last_products",
-    )(place, grad_mixed, w_qkv)
-
-
 def attn_grads_kernel(*refs):
     pieces = refs[:8]
-    mixed_ref, out_grad_ref, sum_ref, hat = refs[8:]
-    for k in range(8):
-        hat[128 * k : 128 * k + 128, :] = pieces[k][...]
-    total = dot_tn(hat[...], mixed_ref[...]).astype(BF).reshape(4, 2, 32, 384)
-    for zl in range(2):
-        sum_ref[zl, :, :384] = total[:, zl].reshape(128, 384)
+    mixed_ref, out_grad_ref, sum_ref, hat, sems = refs[8:]
+    copies = fetch(pieces, hat, sems)
+    for r in range(16):
         for k in range(8):
-            sum_ref[zl, 16 * k : 16 * k + 16, 384:] = out_grad_ref[
-                16 * zl : 16 * zl + 16, 256 * k : 256 * k + 256
+            sum_ref[r, 16 * k : 16 * k + 16, 384:] = out_grad_ref[
+                16 * r : 16 * r + 16, 256 * k : 256 * k + 256
             ]
+    for copy in copies:
+        copy.wait()
+    for f in range(8):
+        total = dot_tn(hat[:, 256 * f : 256 * f + 256], mixed_ref[...])
+        total = total.astype(BF).reshape(4, 2, 32, 384)
+        for zl in range(2):
+            sum_ref[2 * f + zl, :, :384] = total[:, zl].reshape(128, 384)
 
 
 def attn_grads(pieces, grad_mixed, sum_out):
     return pl.pallas_call(
         attn_grads_kernel,
-        grid=(8,),
-        in_specs=[pl.BlockSpec((128, 256), lambda f: (0, f))] * 8
-        + [fixed((ROWS, 384)), pl.BlockSpec((32, 2048), lambda f: (f, 0))],
-        out_specs=pl.BlockSpec((2, 128, 640), lambda f: (f, 0, 0)),
+        in_specs=[ANYWHERE] * 8 + [WHOLE] * 2,
+        out_specs=WHOLE,
         out_shape=jax.ShapeDtypeStruct((16, 128, 640), BF),
-        scratch_shapes=[pltpu.VMEM((ROWS, 256), BF)],
-        compiler_params=params(40),
+        scratch_shapes=[pltpu.VMEM((ROWS, 2048), BF), pltpu.SemaphoreType.DMA((8,))],
+        compiler_params=params(60),
         cost_estimate=takes(4),
         name="attn_grads",
     )(*pieces, grad_mixed, sum_out)
@@ -637,16 +668,19 @@
     packed = pack(attn_in, gate_up, gains.T)
     ranked = lax.all_to_all(packed, TP, 0, 0, tiled=True).reshape(128, 1920)
     hat_pieces = gather_pieces(tie(hat_one.astype(BF), ranked))
-    qkv_copies = jnp.broadcast_to(ranked[None, :, :384], (16, 128, 384))
-    qkv_all = lax.all_to_all(qkv_copies, REP, 0, 0, tiled=True)
-    out_part = lax.ppermute(tie(attn_out.astype(BF), ranked), ALL, SPREAD)
+    out_part = lax.ppermute(attn_out.astype(BF), ALL, SPREAD)
+    out_part = out_part.reshape(16, 8, 256).transpose(1, 0, 2).reshape(128, 256)
+    attn_part = jnp.concatenate([ranked[:, :384], out_part], axis=1)
+    attn_all = lax.all_gather(attn_part, REP, axis=0, tiled=True)
     down_rows = jnp.pad(down_proj.astype(BF), ((0, 4), (0, 0)))
     down_tail = [down_rows[16 * part : 16 * part + 16, 1536:] for part in range(3)]
     ff_part = jnp.concatenate(
         [ranked[:, 384:], down_rows[:, :1536], jnp.concatenate(down_tail, axis=1)], axis=0
     )
-    ff_all = lax.all_gather(ff_part, REP, axis=0, tiled=True)
     grad_pieces = gather_pieces(tie(out_grad, *hat_pieces[1:4]))
+    ff_all = lax.all_gather(
+        tie(ff_part, attn_all, *hat_pieces[1:]), REP, axis=0, tiled=True
+    )
 
     own_pos = row_positions(span_order, zl)
     other_pos = row_positions(span_order, 1 - zl)
@@ -658,10 +692,8 @@
     key_pos = jnp.concatenate([own_pos, other_pos])
     key_pos = jnp.broadcast_to(key_pos[:, None], (KEYS, QB))
 
-    queries, own_kv, w_qkv = project(hat_pieces, qkv_all)
+    queries, own_kv, w_qkv, w_out = project(hat_pieces, attn_all)
     other_kv = lax.ppermute(own_kv, "zl", [(0, 1), (1, 0)])
-    out_copies = jnp.broadcast_to(tie(out_part, own_kv)[None], (16, 16, 2048))
-    w_out = lax.all_to_all(out_copies, REP, 0, 0, tiled=True).reshape(256, 2048)
     before = attend(queries, own_kv, key_pos[:ROWS], low_pos, high_pos, None)
     att, lse = attend(
         queries, other_kv, key_pos[ROWS:], low_pos, high_pos, before, *grad_pieces[1:4]
@@ -680,13 +712,13 @@
     to_left, to_right, stays = scatter_second(scatter_first(back_mine, back_other))
     grad_hat_two = total((stays, *scatter_third(to_left, to_right)))
     grad_hidden = norm_back(grad_hat_two, hat_two, scale_two, out_grad.astype(F32))
-    grad_hidden_low = grad_hidden.astype(BF)
+    sums = weight_grads(hat_two_pieces, grad_pieces, grad_gu, hid, to_left, to_right)
+    sums = sums.reshape(16 * 192, 1536)
+    grad_hidden_low = tie(grad_hidden.astype(BF), sums)
     hidden_pieces = gather_pieces(grad_hidden_low)
-    sum_ff = weight_grads(hat_two_pieces, grad_pieces, grad_gu, hid, grad_hidden_low)
-    all_sum_ff = sum_ff.reshape(16 * 192, 1536)
-    sum_ff = lax.psum_scatter(all_sum_ff, REP, scatter_dimension=0, tiled=True)
-    grad_att, sum_out = hidden_products(hidden_pieces, att, w_out, all_sum_ff)
-    ahead = scatter_first(ahead_mine, tie(ahead_other, hidden_pieces[3]))
+    sums = lax.psum_scatter(tie(sums, grad_hidden_low), REP, scatter_dimension=0, tiled=True)
+    ahead = scatter_first(ahead_mine, tie(ahead_other, hidden_pieces[0]))
+    grad_att, sum_out = hidden_products(hidden_pieces, att, w_out, ahead)
 
     grad_q, grad_kv = attend_back(
         queries, grad_att, att, other_kv, key_pos[ROWS:], low_pos, high_pos, lse, None, ahead
@@ -710,15 +742,17 @@
     block_out = (hidden + total((ahead_stays, *ahead))).astype(BF)
     grad_mixed = jnp.concatenate([grad_q, (grad_kv + arrived.astype(F32)).astype(BF)], axis=1)
     grad_mixed = tie(grad_mixed, *ahead)
-    attn_sums = attn_grads(hat_pieces, grad_mixed, sum_out)
-    attn_sums = lax.all_to_all(attn_sums, REP, 0, 0, tiled=True)
-    grad_hat_one = lax.psum_scatter(
-        last_products(tie(grad_mixed, sum_ff), w_qkv), TP, scatter_dimension=0, tiled=True
-    ).astype(F32)
+    attn_parts = attn_grads(hat_pieces, grad_mixed, sum_out)
+    attn_sums = lax.all_to_all(attn_parts, REP, 0, 0, tiled=True)
     attn_sums = jnp.sum(attn_sums.astype(F32), axis=0).astype(BF)
+    last_rows = tie(grad_mixed, attn_parts)
+    last_other = dot_nt(last_rows[512:], w_qkv).astype(BF)
+    last_mine = dot_nt(last_rows[:512], w_qkv)
+    to_left, to_right, stays = scatter_second(scatter_first(last_mine, last_other))
+    grad_hat_one = total((stays, *scatter_third(to_left, to_right)))
     in_grad = norm_back(grad_hat_one, hat_one, scale_one, grad_hidden).astype(BF)
 
-    got = jnp.concatenate([attn_sums[:, :384], sum_ff[:128]], axis=1).reshape(8, 16, 1920)
+    got = jnp.concatenate([attn_sums[:, :384], sums[:128]], axis=1).reshape(8, 16, 1920)
     got = lax.all_to_all(got, TP, 0, 0, tiled=True)
     got_qkv = got[:, :, :384].transpose(1, 0, 2).astype(F32)
     got_kv = got_qkv[:, :, 256:].reshape(16, 4, 2, 2, HD).sum(axis=2)
@@ -731,9 +765,9 @@
         axis=1,
     )
     sum_out = attn_sums[:, 384:].reshape(8, 16, 256).transpose(1, 0, 2).reshape(16, 2048)
-    got_out = lax.ppermute(sum_out, ALL, back(SPREAD)).astype(F32)
-    tail = [sum_ff[176:192, 512 * part : 512 * part + 512] for part in range(3)]
-    got_down = jnp.concatenate([sum_ff[128:176], jnp.concatenate(tail, axis=0)], axis=1)
+    got_out = lax.ppermute(tie(sum_out, got), ALL, back(SPREAD)).astype(F32)
+    tail = [sums[176:192, 512 * part : 512 * part + 512] for part in range(3)]
+    got_down = jnp.concatenate([sums[128:176], jnp.concatenate(tail, axis=0)], axis=1)
     got_down = got_down[:44].astype(F32)
     gu_new = update_gate_up(got, gate_up, gain_two, first_gate_up, second_gate_up)
     gain_sums = jnp.stack([jnp.sum(low_qkv * got_qkv, axis=1), gu_new[3][:, 0]], axis=0)

time: 470 us -> 446 us (0.949)
  waiting for transfers between devices: 147 us -> 121 us
  local copies, waits for them, and re-layouts: 31.8 us -> 24.7 us
  other arithmetic: 28.1 us -> 35.1 us
  matrix products: 1.46 us -> 8.39 us
  starting transfers between devices: 112 us -> 107 us
    all_to_all x3 -> x1, starting transfers between devices: 27 us -> 6.5 us  [body(): attn_sums = lax.all_to_all(attn_parts, REP, 0, 0, tiled=True)]
    ppermute x24 -> x28, waiting for transfers between devices: 88.1 us -> 70 us  [shift(): return lax.ppermute(block, 'x', [(i, (i + distance) % 4) for i in range(4)])]
    all_to_all x3 -> x1, waiting for transfers between devices: 30.9 us -> 13.5 us  [body(): attn_sums = lax.all_to_all(attn_parts, REP, 0, 0, tiled=True)]
    all_gather x1 -> x2, waiting for transfers between devices: 0.01 us -> 14.8 us  [the longest x1 14.8 us: body(): attn_all = lax.all_gather(attn_part, REP, axis=0, tiled=True)]
    ppermute x19 -> x20, starting transfers between devices: 29.4 us -> 41.9 us  [swap(): return lax.ppermute(block, 'c', [(0, 1), (1, 0)])]
    all_to_all x1, waiting for transfers between devices: 9.01 us -> 0.01 us  [body(): ranked = lax.all_to_all(packed, TP, 0, 0, tiled=True).reshape(128, 1920)]
    ppermute x2, waiting for transfers between devices: 0.22 us -> 7.57 us  [the longest x1 7.56 us: body(): out_part = lax.ppermute(attn_out.astype(BF), ALL, SPREAD)]
    dot_general x0 -> x2, matrix products: none -> 6.96 us  [dot_nt(): lax.dot_general(a, b, (((1,), (1,)), ((), ())), preferred_element_type=F32)]
  transfers between devices with their start and end apart: 55 -> 58, of which waited for: 25 -> 19; matrix products, arithmetic and copies ran while one was open for 6% -> 9% of each run, Pallas kernels for 15% -> 21%
where the time goes in v4:
time: 446 us; the launch traced here: 437 us
  Pallas kernels  124 us (28%)
  waiting for transfers between devices  121 us (27%)
  starting transfers between devices  107 us (24%)
  other arithmetic  35.1 us (8%)
  local copies, waits for them, and re-layouts  24.7 us (6%)
  between operations  16.9 us (4%)
  matrix products  8.39 us (2%)
    ppermute x28, waiting for transfers between devices, shift(): return lax.ppermute(block, 'x', [(i, (i + distance) % 4) for i in range(4)])  70 us
    ppermute x20, starting transfers between devices, swap(): return lax.ppermute(block, 'c', [(0, 1), (1, 0)])  41.9 us
    ppermute x28, starting transfers between devices, shift(): return lax.ppermute(block, 'x', [(i, (i + distance) % 4) for i in range(4)])  33.4 us
    pallas_call x1, Pallas kernels, feed_forward(): pl.pallas_call(feed_forward_kernel, grid=(2,), in_specs=[ANYWHERE] * 17,...  30.8 us
    pallas_call x2, Pallas kernels, attend_back(): pl.pallas_call(functools.partial(attend_back_kernel, first), grid=(ROWS /...  25.4 us
    pallas_call x2, Pallas kernels, attend(): pl.pallas_call(functools.partial(attend_kernel, first), grid=(ROWS // QB,...  24.5 us
    unnamed x173, local copies, waits for them, and re-layouts  18.7 us
    pallas_call x1, Pallas kernels, weight_grads(): pl.pallas_call(weight_grads_kernel, grid=(4,), in_specs=[pl.BlockSpec((12...  17.1 us
  transfers between devices with their start and end apart: 58, of which 19 were waited for; matrix products, arithmetic and copies ran while one was open for 9% of the time, Pallas kernels for 21%

profile of v4, /device:TPU:17, one launch (start us, length us, event | category | flops | bytes accessed | tf_op | source)
XLA Modules:
  0.0 437.2 jit_solution(11868607177334939322)
XLA Ops:
  12.3 5.1 %all-to-all-start = ((bf16[8,16,1920]{2,1,0:T(8,128)(2,1)}), bf16[8,16,1920]{2,1,0:T(8,128)(2,1)S(1)}, u32[]{:S(2)}, u32[]{:S(2)}) async-start(bf16[8,16,1920]{2,1,0:T(8,128)(2,1)} %pack.1), calls=%async_computation | async-start | bytes 983040 | tf_op jit(solution)/shard_map/all_to_all | solution.py:669
  17.5 6.3 %collective-permute-start.7 = (bf16[16,2048]{1,0:T(8,128)(2,1)S(1)}, bf16[16,2048]{1,0:T(8,128)(2,1)S(1)}, u32[]{:S(2)}, u32[]{:S(2)}) collective-permute-start(bf16[16,2048]{1,0:T(8,128)(2,1)S(1)} %convert_element_type.166), channel_id=1, source_target_pairs={{0,0},{1,2},{2,16},{3,18},{4,32},{5,34},{6,48},{7,50},{8,64},{9,66... | collective-permute-start | bytes 196616 | tf_op jit(solution)/shard_map/ppermute | solution.py:671
  23.8 7.6 %collective-permute-done.7 = bf16[16,2048]{1,0:T(8,128)(2,1)S(1)} collective-permute-done((bf16[16,2048]{1,0:T(8,128)(2,1)S(1)}, bf16[16,2048]{1,0:T(8,128)(2,1)S(1)}, u32[]{:S(2)}, u32[]{:S(2)}) %collective-permute-start.7) | collective-permute-done | bytes 65568 | tf_op jit(solution)/shard_map/ppermute | solution.py:671
  36.4 10.6 %collective-permute-done.refs_1_.refs_2_ = bf16[128,2048]{1,0:T(8,128)(2,1)S(1)} collective-permute-done((bf16[128,2048]{1,0:T(8,128)(2,1)}, bf16[128,2048]{1,0:T(8,128)(2,1)S(1)}, u32[]{:S(2)}, u32[]{:S(2)}) %collective-permute-start) | collective-permute-done | bytes 524320 | tf_op jit(solution)/shard_map/ppermute | solution.py:536
  48.8 9.1 %collective-permute-done.2.refs_3_.refs_4_ = bf16[128,2048]{1,0:T(8,128)(2,1)S(1)} collective-permute-done((bf16[128,2048]{1,0:T(8,128)(2,1)}, bf16[128,2048]{1,0:T(8,128)(2,1)S(1)}, u32[]{:S(2)}, u32[]{:S(2)}) %collective-permute-start.2) | collective-permute-done | bytes 524320 | tf_op jit(solution)/shard_map/ppermute | solution.py:536
  60.8 14.8 %all-gather.3.cloned.1.call-done.refs_8_.refs_1_ = bf16[2048,640]{1,0:T(8,128)(2,1)} async-done(((bf16[128,640]{1,0:T(8,128)(2,1)}), bf16[2048,640]{1,0:T(8,128)(2,1)}) %all-gather.3.cloned.1.call-update) | async-done | bytes 2621456 | tf_op jit(solution)/shard_map/all_gather | solution.py:674
  84.8 6.9 %project.1 = (bf16[1024,256]{1,0:T(8,128)(2,1)}, bf16[1024,128]{1,0:T(8,128)(2,1)}, bf16[2048,384]{1,0:T(8,128)(2,1)}, bf16[256,2048]{1,0:T(8,128)(2,1)}) custom-call(bf16[128,2048]{1,0:T(8,128)(2,1)} %tie.9.refs_0_, bf16[128,2048]{1,0:T(8,128)(2,1)} %copy-done.35, bf16[128,2048]{1,0:T(8,128)(2,1)} %copy-done.36, bf16[128,2048]{1,0:T(8,128)(2,1)} %copy-done.37, ...), custom_call_target="tpu_custom_call" | custom-call | flops 5750000128 | bytes 1048576 | tf_op jit(solution)/shard_map/project/pallas_call | solution.py:252
  94.7 11.9 %attend.2 = (f32[256,1024]{1,0:T(8,128)S(1)}, f32[4,1024]{1,0:T(4,128)S(1)}, f32[4,1024]{1,0:T(4,128)S(1)}) custom-call(bf16[1024,256]{1,0:T(8,128)(2,1)S(1)} %copy-done.17, bf16[1024,128]{1,0:T(8,128)(2,1)S(1)} %copy-done.15, s32[1024,256]{1,0:T(8,128)S(1)} %broadcast_in_dim.17.kp_ref, s32[1,1024]{1,0:T(1,128)S(1)} %get-tuple-element.127.lo_ref, ...), custom_call_target="tpu_custom_call" | custom-call | flops 12650000384 | bytes 1048576 | tf_op jit(solution)/shard_map/attend/pallas_call | solution.py:136
  108.9 12.6 %attend.3 = (bf16[1024,256]{1,0:T(8,128)(2,1)S(1)}, f32[4,1024]{1,0:T(4,128)S(1)}) custom-call(bf16[1024,256]{1,0:T(8,128)(2,1)S(1)} %copy-done.18, bf16[1024,128]{1,0:T(8,128)(2,1)S(1)} %collective-permute-done.8.kv_ref, s32[1024,256]{1,0:T(8,128)S(1)} %broadcast_in_dim.13.kp_ref, s32[1,1024]{1,0:T(1,128)S(1)} %get-tuple-element.127.lo_ref, ...), custom_call_target="tpu_custom_call" | custom-call | flops 12650000384 | bytes 1048576 | tf_op jit(solution)/shard_map/attend/pallas_call | solution.py:136
  124.8 3.8 collective-permute-done.12
  131.0 6.2 %collective-permute-done.13 = bf16[64,2048]{1,0:T(8,128)(2,1)S(1)} collective-permute-done((bf16[64,2048]{1,0:T(8,128)(2,1)S(1)}, bf16[64,2048]{1,0:T(8,128)(2,1)S(1)}, u32[]{:S(2)}, u32[]{:S(2)}) %collective-permute-start.13) | collective-permute-done | bytes 262176 | tf_op jit(solution)/shard_map/ppermute | solution.py:536
  144.6 8.0 %collective-permute-done.16 = bf16[128,2048]{1,0:T(8,128)(2,1)S(1)} collective-permute-done((bf16[128,2048]{1,0:T(8,128)(2,1)S(1)}, bf16[128,2048]{1,0:T(8,128)(2,1)S(1)}, u32[]{:S(2)}, u32[]{:S(2)}) %collective-permute-start.16) | collective-permute-done | bytes 524320 | tf_op jit(solution)/shard_map/ppermute | solution.py:536
  160.2 5.4 %collective-permute-done.17.refs_1_ = bf16[128,2048]{1,0:T(8,128)(2,1)S(1)} collective-permute-done((bf16[128,2048]{1,0:T(8,128)(2,1)S(1)}, bf16[128,2048]{1,0:T(8,128)(2,1)S(1)}, u32[]{:S(2)}, u32[]{:S(2)}) %collective-permute-start.17) | collective-permute-done | bytes 524320 | tf_op jit(solution)/shard_map/ppermute | solution.py:536
  165.6 5.2 %collective-permute-start.21 = (bf16[128,2048]{1,0:T(8,128)(2,1)S(1)}, bf16[128,2048]{1,0:T(8,128)(2,1)S(1)}, u32[]{:S(2)}, u32[]{:S(2)}) collective-permute-start(bf16[128,2048]{1,0:T(8,128)(2,1)S(1)} %collective-permute-done.17.refs_1_), channel_id=1, source_target_pairs={{0,1},{1,0},{2,3},{3,2},{4,5},{5,4},{6,7},{7,6},{8,9},{9,8},{10,11... | collective-permute-start | bytes 1572872 | tf_op jit(solution)/shard_map/ppermute | solution.py:540
  170.8 8.9 %collective-permute-start.22 = (bf16[128,2048]{1,0:T(8,128)(2,1)S(1)}, bf16[128,2048]{1,0:T(8,128)(2,1)S(1)}, u32[]{:S(2)}, u32[]{:S(2)}) collective-permute-start(bf16[128,2048]{1,0:T(8,128)(2,1)S(1)} %collective-permute-done.18.refs_2_), channel_id=1, source_target_pairs={{0,1},{1,0},{2,3},{3,2},{4,5},{5,4},{6,7},{7,6},{8,9},{9,8},{10,11... | collective-permute-start | bytes 1572872 | tf_op jit(solution)/shard_map/ppermute | solution.py:540
  182.9 30.8 %feed_forward.1 = (bf16[1024,768]{1,0:T(8,128)(2,1)}, bf16[1024,1536]{1,0:T(8,128)(2,1)}, bf16[512,2048]{1,0:T(8,128)(2,1)}, bf16[512,2048]{1,0:T(8,128)(2,1)}, ...) custom-call(bf16[128,2048]{1,0:T(8,128)(2,1)} %copy-done.50, bf16[128,2048]{1,0:T(8,128)(2,1)} %copy-done.70, ...), custom_call_target="tpu_custom_call" | custom-call | flops 32199999488 | bytes 1048576 | tf_op jit(solution)/shard_map/feed_forward/pallas_call | solution.py:389
  214.2 4.1 collective-permute-done.28
  223.8 5.3 %collective-permute-done.29 = bf16[64,2048]{1,0:T(8,128)(2,1)S(1)} collective-permute-done((bf16[64,2048]{1,0:T(8,128)(2,1)S(1)}, bf16[64,2048]{1,0:T(8,128)(2,1)S(1)}, u32[]{:S(2)}, u32[]{:S(2)}) %collective-permute-start.29) | collective-permute-done | bytes 262176 | tf_op jit(solution)/shard_map/ppermute | solution.py:536
  235.3 17.1 %weight_grads.1 = bf16[16,192,1536]{2,1,0:T(8,128)(2,1)} custom-call(bf16[128,2048]{1,0:T(8,128)(2,1)} %copy-done.50, bf16[128,2048]{1,0:T(8,128)(2,1)} %copy-done.70, bf16[128,2048]{1,0:T(8,128)(2,1)} %copy-done.71, bf16[128,2048]{1,0:T(8,128)(2,1)} %copy-done.72, bf16[128,2048]{1,0:T(8,128)(2,1)} %copy-done.74, bf16[128,2048]{1,0:T(8,128)(2,1)} %copy-done.75, ...), custom_call_target="tpu_custom_call" | custom-call | flops 18975000576 | bytes 1048576 | tf_op jit(solution)/shard_map/weight_grads/pallas_call | solution.py:436
  263.2 10.7 %collective-permute-done.38.refs_1_ = bf16[128,2048]{1,0:T(8,128)(2,1)S(1)} collective-permute-done((bf16[128,2048]{1,0:T(8,128)(2,1)S(1)}, bf16[128,2048]{1,0:T(8,128)(2,1)S(1)}, u32[]{:S(2)}, u32[]{:S(2)}) %collective-permute-start.38) | collective-permute-done | bytes 524320 | tf_op jit(solution)/shard_map/ppermute | solution.py:536
  273.9 11.9 %collective-permute-start.42 = (bf16[128,2048]{1,0:T(8,128)(2,1)S(1)}, bf16[128,2048]{1,0:T(8,128)(2,1)S(1)}, u32[]{:S(2)}, u32[]{:S(2)}) collective-permute-start(bf16[128,2048]{1,0:T(8,128)(2,1)S(1)} %collective-permute-done.38.refs_1_), channel_id=1, source_target_pairs={{0,1},{1,0},{2,3},{3,2},{4,5},{5,4},{6,7},{7,6},{8,9},{9,8},{10,11... | collective-permute-start | bytes 1572872 | tf_op jit(solution)/shard_map/ppermute | solution.py:540
  286.4 4.6 %fusion.36 = (bf16[512,2048]{1,0:T(8,128)(2,1)S(1)}, f32[512,2048]{1,0:T(8,128)}) fusion(bf16[512,2048]{1,0:T(8,128)(2,1)S(1)} %collective-permute-done.33, bf16[512,2048]{1,0:T(8,128)(2,1)} %get-tuple-element.49), kind=kLoop, calls=%fused_computation.116 | loop fusion | flops 4194304 | bytes 10485760 | tf_op jit(solution)/shard_map/convert.15
  296.1 7.4 %hidden_products.1 = (bf16[1024,256]{1,0:T(8,128)(2,1)}, bf16[256,2048]{1,0:T(8,128)(2,1)}) custom-call(bf16[128,2048]{1,0:T(8,128)(2,1)} %tie.12.refs_1_.refs_0_, bf16[128,2048]{1,0:T(8,128)(2,1)} %copy-done.77, bf16[128,2048]{1,0:T(8,128)(2,1)} %copy-done.78, bf16[128,2048]{1,0:T(8,128)(2,1)} %copy-done.79, bf16[128,2048]{1,0:T(8,128)(2,1)} %copy-done.80, ...), custom_call_target="tpu_custom_call" | custom-call | flops 6899999744 | bytes 1048576 | tf_op jit(solution)/shard_map/hidden_products/pallas_call | solution.py:282
  306.9 12.4 %attend_back.2 = (f32[256,1024]{1,0:T(8,128)S(1)}, f32[1024,128]{1,0:T(8,128)S(1)}) custom-call(bf16[1024,256]{1,0:T(8,128)(2,1)S(1)} %copy-done.19, bf16[1024,256]{1,0:T(8,128)(2,1)S(1)} %copy-done.20, bf16[1024,256]{1,0:T(8,128)(2,1)S(1)} %copy-done.4, bf16[1024,128]{1,0:T(8,128)(2,1)S(1)} %collective-permute-done.8.kv_ref, ...), custom_call_target="tpu_custom_call" | custom-call | flops 14375000064 | bytes 1048576 | tf_op jit(solution)/shard_map/attend_back/pallas_call | solution.py:190
  324.0 13.0 %attend_back.3 = (bf16[1024,256]{1,0:T(8,128)(2,1)S(1)}, f32[1024,128]{1,0:T(8,128)S(1)}) custom-call(bf16[1024,256]{1,0:T(8,128)(2,1)S(1)} %copy-done.19, bf16[1024,256]{1,0:T(8,128)(2,1)S(1)} %copy-done.20, bf16[1024,256]{1,0:T(8,128)(2,1)S(1)} %copy-done.4, bf16[1024,128]{1,0:T(8,128)(2,1)S(1)} %copy-done.16, s32[1024,256]{1,0:T(8,128)S(1)} %broadcast_in_dim.17.kp_ref, ...), custom_call_target="tpu_custom_call" | custom-call | flops 14375000064 | bytes 1048576 | tf_op jit(solution)/shard_map/attend_back/pallas_call | solution.py:190
  338.9 7.7 %attn_grads.1.refs_1_ = bf16[16,128,640]{2,1,0:T(8,128)(2,1)} custom-call(bf16[128,2048]{1,0:T(8,128)(2,1)} %tie.9.refs_0_, bf16[128,2048]{1,0:T(8,128)(2,1)} %copy-done.35, bf16[128,2048]{1,0:T(8,128)(2,1)} %copy-done.36, bf16[128,2048]{1,0:T(8,128)(2,1)} %copy-done.37, bf16[128,2048]{1,0:T(8,128)(2,1)} %copy-done.47, bf16[128,2048]{1,0:T(8,128)(2,1)} %copy-done.48, ...), custom_call_target="tpu_custom_call" | custom-call | flops 4600000000 | bytes 1048576 | tf_op jit(solution)/shard_map/attn_grads/pallas_call | solution.py:609
  353.2 6.5 %all-to-all-start.1 = ((bf16[16,128,640]{2,1,0:T(8,128)(2,1)}), bf16[16,128,640]{2,1,0:T(8,128)(2,1)S(1)}, u32[]{:S(2)}, u32[]{:S(2)}) async-start(bf16[16,128,640]{2,1,0:T(8,128)(2,1)} %attn_grads.1.refs_1_), calls=%async_computation.1 | async-start | bytes 5242880 | tf_op jit(solution)/shard_map/all_to_all | solution.py:746
  364.9 5.4 %collective-permute-done.47 = bf16[64,2048]{1,0:T(8,128)(2,1)S(1)} collective-permute-done((bf16[64,2048]{1,0:T(8,128)(2,1)S(1)}, bf16[64,2048]{1,0:T(8,128)(2,1)S(1)}, u32[]{:S(2)}, u32[]{:S(2)}) %collective-permute-start.47) | collective-permute-done | bytes 262176 | tf_op jit(solution)/shard_map/ppermute | solution.py:536
  379.8 13.5 %all-to-all-done.1 = bf16[16,128,640]{2,1,0:T(8,128)(2,1)S(1)} async-done(((bf16[16,128,640]{2,1,0:T(8,128)(2,1)}), bf16[16,128,640]{2,1,0:T(8,128)(2,1)S(1)}, u32[]{:S(2)}, u32[]{:S(2)}) %all-to-all-start.1) | async-done | bytes 2621472 | tf_op jit(solution)/shard_map/all_to_all | solution.py:746
  401.1 6.1 %all-to-all-start.2 = ((bf16[8,16,1920]{2,1,0:T(8,128)(2,1)}), bf16[8,16,1920]{2,1,0:T(8,128)(2,1)S(1)}, u32[]{:S(2)}, u32[]{:S(2)}) async-start(bf16[8,16,1920]{2,1,0:T(8,128)(2,1)} %bitcast.24), calls=%async_computation.3 | async-start | bytes 983040 | tf_op jit(solution)/shard_map/all_to_all | solution.py:756
  409.7 6.6 %all-to-all-done.2.refs_1_.got_ref = bf16[8,16,1920]{2,1,0:T(8,128)(2,1)S(1)} async-done(((bf16[8,16,1920]{2,1,0:T(8,128)(2,1)}), bf16[8,16,1920]{2,1,0:T(8,128)(2,1)S(1)}, u32[]{:S(2)}, u32[]{:S(2)}) %all-to-all-start.2) | async-done | bytes 491552 | tf_op jit(solution)/shard_map/all_to_all | solution.py:756
  417.1 6.5 %collective-permute-start.51 = (bf16[16,2048]{1,0:T(8,128)(2,1)}, bf16[16,2048]{1,0:T(8,128)(2,1)S(1)}, u32[]{:S(2)}, u32[]{:S(2)}) collective-permute-start(bf16[16,2048]{1,0:T(8,128)(2,1)} %tie.17), channel_id=1, source_target_pairs={{0,0},{2,1},{16,2},{18,3},{32,4},{34,5},{48,6},{50,7},{64,8},{66,9... | collective-permute-start | bytes 196616 | tf_op jit(solution)/shard_map/ppermute | solution.py:768
  (376 shorter events, 128.4 us)
Async XLA Ops:
  12.3 19.0 %all-to-all-start = ((bf16[8,16,1920]{2,1,0:T(8,128)(2,1)}), bf16[8,16,1920]{2,1,0:T(8,128)(2,1)S(1)}, u32[]{:S(2)}, u32[]{:S(2)}) async-start(bf16[8,16,1920]{2,1,0:T(8,128)(2,1)} %pack.1), calls=%async_computation | async-start | bytes 983040 | tf_op jit(solution)/shard_map/all_to_all | solution.py:669
  17.4 58.1 %all-gather.3.cloned.1.call-start = ((), (), s32[]{:S(2)}) async-start(), calls=%async_computation.4 | async-start | bytes 2785280 | tf_op jit(solution)/shard_map/all_gather | solution.py:674
  32.1 150.7 %all-gather.5.cloned.1.call-start = ((), (), s32[]{:S(2)}) async-start(), calls=%async_computation.5 | async-start | bytes 10027008 | tf_op jit(solution)/shard_map/all_gather | solution.py:681
  36.0 21.8 %collective-permute-start.2 = (bf16[128,2048]{1,0:T(8,128)(2,1)}, bf16[128,2048]{1,0:T(8,128)(2,1)S(1)}, u32[]{:S(2)}, u32[]{:S(2)}) collective-permute-start(bf16[128,2048]{1,0:T(8,128)(2,1)} %tie.9.refs_0_), channel_id=1, source_target_pairs={{0,8},{4,12},{8,0},{12,4},{1,9},{5,13},{9,1},{13,5},{2,10},{6,14},... | collective-permute-start | bytes 1572872 | tf_op jit(solution)/shard_map/ppermute | solution.py:536
  36.3 23.6 %collective-permute-start.3 = (bf16[128,2048]{1,0:T(8,128)(2,1)}, bf16[128,2048]{1,0:T(8,128)(2,1)S(1)}, u32[]{:S(2)}, u32[]{:S(2)}) collective-permute-start(bf16[128,2048]{1,0:T(8,128)(2,1)} %tie.9.refs_0_), channel_id=1, source_target_pairs={{0,1},{1,0},{2,3},{3,2},{4,5},{5,4},{6,7},{7,6},{8,9},{9,8},{10,11... | collective-permute-start | bytes 1572872 | tf_op jit(solution)/shard_map/ppermute | solution.py:540
  75.6 323.5 %reduce-scatter.2.cloned.1.call-start = ((), (), s32[]{:S(2)}) async-start(), calls=%async_computation.6 | async-start | bytes 10027008 | tf_op jit(solution)/shard_map/reduce_scatter | solution.py:719
  80.5 26.1 %collective-permute-start.9 = (bf16[128,2048]{1,0:T(8,128)(2,1)}, bf16[128,2048]{1,0:T(8,128)(2,1)S(1)}, u32[]{:S(2)}, u32[]{:S(2)}) collective-permute-start(bf16[128,2048]{1,0:T(8,128)(2,1)} %tie.10.refs_8_), channel_id=1, source_target_pairs={{0,4},{4,8},{8,12},{12,0},{1,5},{5,9},{9,13},{13,1},{2,6},{6,10},{... | collective-permute-start | bytes 1572872 | tf_op jit(solution)/shard_map/ppermute | solution.py:536
  81.8 24.9 %collective-permute-start.10 = (bf16[128,2048]{1,0:T(8,128)(2,1)}, bf16[128,2048]{1,0:T(8,128)(2,1)S(1)}, u32[]{:S(2)}, u32[]{:S(2)}) collective-permute-start(bf16[128,2048]{1,0:T(8,128)(2,1)} %tie.10.refs_8_), channel_id=1, source_target_pairs={{0,12},{4,0},{8,4},{12,8},{1,13},{5,1},{9,5},{13,9},{2,14},{6,2},{... | collective-permute-start | bytes 1572872 | tf_op jit(solution)/shard_map/ppermute | solution.py:536
  83.3 23.4 %collective-permute-start.11 = (bf16[128,2048]{1,0:T(8,128)(2,1)}, bf16[128,2048]{1,0:T(8,128)(2,1)S(1)}, u32[]{:S(2)}, u32[]{:S(2)}) collective-permute-start(bf16[128,2048]{1,0:T(8,128)(2,1)} %tie.10.refs_8_), channel_id=1, source_target_pairs={{0,8},{4,12},{8,0},{12,4},{1,9},{5,13},{9,1},{13,5},{2,10},{6,14},... | collective-permute-start | bytes 1572872 | tf_op jit(solution)/shard_map/ppermute | solution.py:536
  91.7 15.9 %collective-permute-start.8 = (bf16[1024,128]{1,0:T(8,128)(2,1)}, bf16[1024,128]{1,0:T(8,128)(2,1)S(1)}, u32[]{:S(2)}, u32[]{:S(2)}) collective-permute-start(bf16[1024,128]{1,0:T(8,128)(2,1)} %get-tuple-element.43.kv_ref), channel_id=1, source_target_pairs={{0,2},{2,0},{1,3},{3,1},{4,6},{6,4},{5,7},{7,5},{8,10},{10,8},{9,1... | collective-permute-start | bytes 786440 | tf_op jit(solution)/shard_map/ppermute | solution.py:696
  144.1 16.0 %collective-permute-start.26 = (bf16[128,2048]{1,0:T(8,128)(2,1)S(1)}, bf16[128,2048]{1,0:T(8,128)(2,1)S(1)}, u32[]{:S(2)}, u32[]{:S(2)}) collective-permute-start(bf16[128,2048]{1,0:T(8,128)(2,1)S(1)} %collective-permute-done.10.rest_4_.refs_10_), channel_id=1, source_target_pairs={{0,1},{1,0},{2,3},{3,2},{4,5},{5,4},{6,7},{7,6},{8,9},{9,8},{10,11... | collective-permute-start | bytes 1572872 | tf_op jit(solution)/shard_map/ppermute | solution.py:540
  153.2 17.6 %collective-permute-start.18 = (bf16[128,2048]{1,0:T(8,128)(2,1)S(1)}, bf16[128,2048]{1,0:T(8,128)(2,1)S(1)}, u32[]{:S(2)}, u32[]{:S(2)}) collective-permute-start(bf16[128,2048]{1,0:T(8,128)(2,1)S(1)} %multiply_convert_fusion.refs_0_), channel_id=1, source_target_pairs={{0,12},{4,0},{8,4},{12,8},{1,13},{5,1},{9,5},{13,9},{2,14},{6,2},{... | collective-permute-start | bytes 1572872 | tf_op jit(solution)/shard_map/ppermute | solution.py:536
  155.9 23.8 %collective-permute-start.19 = (bf16[128,2048]{1,0:T(8,128)(2,1)S(1)}, bf16[128,2048]{1,0:T(8,128)(2,1)S(1)}, u32[]{:S(2)}, u32[]{:S(2)}) collective-permute-start(bf16[128,2048]{1,0:T(8,128)(2,1)S(1)} %multiply_convert_fusion.refs_0_), channel_id=1, source_target_pairs={{0,8},{4,12},{8,0},{12,4},{1,9},{5,13},{9,1},{13,5},{2,10},{6,14},... | collective-permute-start | bytes 1572872 | tf_op jit(solution)/shard_map/ppermute | solution.py:536
  157.0 24.0 %collective-permute-start.27 = (bf16[128,2048]{1,0:T(8,128)(2,1)S(1)}, bf16[128,2048]{1,0:T(8,128)(2,1)S(1)}, u32[]{:S(2)}, u32[]{:S(2)}) collective-permute-start(bf16[128,2048]{1,0:T(8,128)(2,1)S(1)} %copy-done.14), channel_id=1, source_target_pairs={{0,1},{1,0},{2,3},{3,2},{4,5},{5,4},{6,7},{7,6},{8,9},{9,8},{10,11... | collective-permute-start | bytes 1572872 | tf_op jit(solution)/shard_map/ppermute | solution.py:540
  160.1 20.9 %collective-permute-start.20 = (bf16[128,2048]{1,0:T(8,128)(2,1)S(1)}, bf16[128,2048]{1,0:T(8,128)(2,1)S(1)}, u32[]{:S(2)}, u32[]{:S(2)}) collective-permute-start(bf16[128,2048]{1,0:T(8,128)(2,1)S(1)} %multiply_convert_fusion.refs_0_), channel_id=1, source_target_pairs={{0,1},{1,0},{2,3},{3,2},{4,5},{5,4},{6,7},{7,6},{8,9},{9,8},{10,11... | collective-permute-start | bytes 1572872 | tf_op jit(solution)/shard_map/ppermute | solution.py:540
  165.6 15.4 %collective-permute-start.21 = (bf16[128,2048]{1,0:T(8,128)(2,1)S(1)}, bf16[128,2048]{1,0:T(8,128)(2,1)S(1)}, u32[]{:S(2)}, u32[]{:S(2)}) collective-permute-start(bf16[128,2048]{1,0:T(8,128)(2,1)S(1)} %collective-permute-done.17.refs_1_), channel_id=1, source_target_pairs={{0,1},{1,0},{2,3},{3,2},{4,5},{5,4},{6,7},{7,6},{8,9},{9,8},{10,11... | collective-permute-start | bytes 1572872 | tf_op jit(solution)/shard_map/ppermute | solution.py:540
  232.4 20.0 %collective-permute-start.32 = (bf16[128,2048]{1,0:T(8,128)(2,1)S(1)}, bf16[128,2048]{1,0:T(8,128)(2,1)S(1)}, u32[]{:S(2)}, u32[]{:S(2)}) collective-permute-start(bf16[128,2048]{1,0:T(8,128)(2,1)S(1)} %pad_maximum_fusion.4.refs_19_), channel_id=1, source_target_pairs={{0,4},{4,8},{8,12},{12,0},{1,5},{5,9},{9,13},{13,1},{2,6},{6,10},{... | collective-permute-start | bytes 1572872 | tf_op jit(solution)/shard_map/ppermute | solution.py:536
  232.5 19.9 %collective-permute-start.30 = (bf16[128,2048]{1,0:T(8,128)(2,1)S(1)}, bf16[128,2048]{1,0:T(8,128)(2,1)S(1)}, u32[]{:S(2)}, u32[]{:S(2)}) collective-permute-start(bf16[128,2048]{1,0:T(8,128)(2,1)S(1)} %pad_maximum_fusion.3.refs_18_), channel_id=1, source_target_pairs={{0,12},{4,0},{8,4},{12,8},{1,13},{5,1},{9,5},{13,9},{2,14},{6,2},{... | collective-permute-start | bytes 1572872 | tf_op jit(solution)/shard_map/ppermute | solution.py:536
  256.9 29.5 %collective-permute-start.33 = (bf16[512,2048]{1,0:T(8,128)(2,1)}, bf16[512,2048]{1,0:T(8,128)(2,1)S(1)}, u32[]{:S(2)}, u32[]{:S(2)}) collective-permute-start(bf16[512,2048]{1,0:T(8,128)(2,1)} %tie.13), channel_id=1, source_target_pairs={{0,1},{1,0},{2,3},{3,2},{4,5},{5,4},{6,7},{7,6},{8,9},{9,8},{10,11... | collective-permute-start | bytes 6291464 | tf_op jit(solution)/shard_map/ppermute | solution.py:540
  259.1 26.8 %collective-permute-start.39 = (bf16[128,2048]{1,0:T(8,128)(2,1)S(1)}, bf16[128,2048]{1,0:T(8,128)(2,1)S(1)}, u32[]{:S(2)}, u32[]{:S(2)}) collective-permute-start(bf16[128,2048]{1,0:T(8,128)(2,1)S(1)} %copy-done.30), channel_id=1, source_target_pairs={{0,12},{4,0},{8,4},{12,8},{1,13},{5,1},{9,5},{13,9},{2,14},{6,2},{... | collective-permute-start | bytes 1572872 | tf_op jit(solution)/shard_map/ppermute | solution.py:536
  261.7 24.2 %collective-permute-start.40 = (bf16[128,2048]{1,0:T(8,128)(2,1)S(1)}, bf16[128,2048]{1,0:T(8,128)(2,1)S(1)}, u32[]{:S(2)}, u32[]{:S(2)}) collective-permute-start(bf16[128,2048]{1,0:T(8,128)(2,1)S(1)} %copy-done.30), channel_id=1, source_target_pairs={{0,8},{4,12},{8,0},{12,4},{1,9},{5,13},{9,1},{13,5},{2,10},{6,14},... | collective-permute-start | bytes 1572872 | tf_op jit(solution)/shard_map/ppermute | solution.py:536
  261.7 32.4 %collective-permute-start.41 = (bf16[128,2048]{1,0:T(8,128)(2,1)S(1)}, bf16[128,2048]{1,0:T(8,128)(2,1)S(1)}, u32[]{:S(2)}, u32[]{:S(2)}) collective-permute-start(bf16[128,2048]{1,0:T(8,128)(2,1)S(1)} %copy-done.30), channel_id=1, source_target_pairs={{0,1},{1,0},{2,3},{3,2},{4,5},{5,4},{6,7},{7,6},{8,9},{9,8},{10,11... | collective-permute-start | bytes 1572872 | tf_op jit(solution)/shard_map/ppermute | solution.py:540
  273.9 20.3 %collective-permute-start.42 = (bf16[128,2048]{1,0:T(8,128)(2,1)S(1)}, bf16[128,2048]{1,0:T(8,128)(2,1)S(1)}, u32[]{:S(2)}, u32[]{:S(2)}) collective-permute-start(bf16[128,2048]{1,0:T(8,128)(2,1)S(1)} %collective-permute-done.38.refs_1_), channel_id=1, source_target_pairs={{0,1},{1,0},{2,3},{3,2},{4,5},{5,4},{6,7},{7,6},{8,9},{9,8},{10,11... | collective-permute-start | bytes 1572872 | tf_op jit(solution)/shard_map/ppermute | solution.py:540
  291.8 28.0 %collective-permute-start.34 = (bf16[64,2048]{1,0:T(8,128)(2,1)}, bf16[64,2048]{1,0:T(8,128)(2,1)}, u32[]{:S(2)}, u32[]{:S(2)}) collective-permute-start(bf16[64,2048]{1,0:T(8,128)(2,1)} %get-tuple-element.101), channel_id=1, source_target_pairs={{0,12},{4,0},{8,4},{12,8},{1,13},{5,1},{9,5},{13,9},{2,14},{6,2},{... | collective-permute-start | bytes 786440 | tf_op jit(solution)/shard_map/ppermute | solution.py:536
  294.2 25.6 %collective-permute-start.36 = (bf16[64,2048]{1,0:T(8,128)(2,1)S(1)}, bf16[64,2048]{1,0:T(8,128)(2,1)}, u32[]{:S(2)}, u32[]{:S(2)}) collective-permute-start(bf16[64,2048]{1,0:T(8,128)(2,1)S(1)} %get-tuple-element.102), channel_id=1, source_target_pairs={{0,4},{4,8},{8,12},{12,0},{1,5},{5,9},{9,13},{13,1},{2,6},{6,10},{... | collective-permute-start | bytes 786440 | tf_op jit(solution)/shard_map/ppermute | solution.py:536
  319.3 17.8 %collective-permute-start.45 = (bf16[1024,128]{1,0:T(8,128)(2,1)S(1)}, bf16[1024,128]{1,0:T(8,128)(2,1)S(1)}, u32[]{:S(2)}, u32[]{:S(2)}) collective-permute-start(bf16[1024,128]{1,0:T(8,128)(2,1)S(1)} %convert_element_type.192), channel_id=1, source_target_pairs={{0,2},{2,0},{1,3},{3,1},{4,6},{6,4},{5,7},{7,5},{8,10},{10,8},{9,1... | collective-permute-start | bytes 786440 | tf_op jit(solution)/shard_map/ppermute | solution.py:726
  321.0 17.2 %collective-permute-start.37 = (bf16[128,2048]{1,0:T(8,128)(2,1)S(1)}, bf16[128,2048]{1,0:T(8,128)(2,1)S(1)}, u32[]{:S(2)}, u32[]{:S(2)}) collective-permute-start(bf16[128,2048]{1,0:T(8,128)(2,1)S(1)} %pad_maximum_fusion.6.rest_2_), channel_id=1, source_target_pairs={{0,4},{4,8},{8,12},{12,0},{1,5},{5,9},{9,13},{13,1},{2,6},{6,10},{... | collective-permute-start | bytes 1572872 | tf_op jit(solution)/shard_map/ppermute | solution.py:536
  321.1 17.0 %collective-permute-start.35 = (bf16[128,2048]{1,0:T(8,128)(2,1)S(1)}, bf16[128,2048]{1,0:T(8,128)(2,1)}, u32[]{:S(2)}, u32[]{:S(2)}) collective-permute-start(bf16[128,2048]{1,0:T(8,128)(2,1)S(1)} %pad_maximum_fusion.5.rest_1_), channel_id=1, source_target_pairs={{0,12},{4,0},{8,4},{12,8},{1,13},{5,1},{9,5},{13,9},{2,14},{6,2},{... | collective-permute-start | bytes 1572872 | tf_op jit(solution)/shard_map/ppermute | solution.py:536
  353.2 40.1 %all-to-all-start.1 = ((bf16[16,128,640]{2,1,0:T(8,128)(2,1)}), bf16[16,128,640]{2,1,0:T(8,128)(2,1)S(1)}, u32[]{:S(2)}, u32[]{:S(2)}) async-start(bf16[16,128,640]{2,1,0:T(8,128)(2,1)} %attn_grads.1.refs_1_), calls=%async_computation.1 | async-start | bytes 5242880 | tf_op jit(solution)/shard_map/all_to_all | solution.py:746
  373.8 20.5 %collective-permute-start.50 = (bf16[128,2048]{1,0:T(8,128)(2,1)}, bf16[128,2048]{1,0:T(8,128)(2,1)}, u32[]{:S(2)}, u32[]{:S(2)}) collective-permute-start(bf16[128,2048]{1,0:T(8,128)(2,1)} %pad_maximum_fusion.8), channel_id=1, source_target_pairs={{0,4},{4,8},{8,12},{12,0},{1,5},{5,9},{9,13},{13,1},{2,6},{6,10},{... | collective-permute-start | bytes 1572872 | tf_op jit(solution)/shard_map/ppermute | solution.py:536
  374.7 19.7 %collective-permute-start.48 = (bf16[128,2048]{1,0:T(8,128)(2,1)}, bf16[128,2048]{1,0:T(8,128)(2,1)}, u32[]{:S(2)}, u32[]{:S(2)}) collective-permute-start(bf16[128,2048]{1,0:T(8,128)(2,1)} %pad_maximum_fusion.7), channel_id=1, source_target_pairs={{0,12},{4,0},{8,4},{12,8},{1,13},{5,1},{9,5},{13,9},{2,14},{6,2},{... | collective-permute-start | bytes 1572872 | tf_op jit(solution)/shard_map/ppermute | solution.py:536
  401.1 15.2 %all-to-all-start.2 = ((bf16[8,16,1920]{2,1,0:T(8,128)(2,1)}), bf16[8,16,1920]{2,1,0:T(8,128)(2,1)S(1)}, u32[]{:S(2)}, u32[]{:S(2)}) async-start(bf16[8,16,1920]{2,1,0:T(8,128)(2,1)} %bitcast.24), calls=%async_computation.3 | async-start | bytes 983040 | tf_op jit(solution)/shard_map/all_to_all | solution.py:756
  (111 other events, 1021.9 us)
Sparse Core Ops, SparseCore 0:
  32.3 43.2 all-gather.2
  78.3 80.1 all-gather.4
  257.0 85.5 reduce-scatter.1

commit v5 on v4

--- a/solution.py
+++ b/solution.py
@@ -87,6 +87,11 @@
     return pltpu.CompilerParams(vmem_limit_bytes=mib * 1024 * 1024)
 
 
+def natural_rows(block, piece):
+    first = (block % 2) * 512 + (block // 2) * 64 + 128 * piece
+    return pl.ds(pl.multiple_of(first, 64), 64)
+
+
 def attend_kernel(first, q_ref, kv_ref, kp_ref, lo_ref, hi_ref, *rest):
     turned = rest[-1]
 
@@ -94,58 +99,68 @@
     def _():
         turned[...] = kv_ref[...].T
 
-    key_pos = kp_ref[...]
-    high = hi_ref[...]
-    allowed = (key_pos >= lo_ref[...]) & (key_pos <= high)
-    keys = kv_ref[:, :HD]
-    for h in range(4):
-        cols = slice(h * HD, (h + 1) * HD)
-        row = slice(h, h + 1)
-        s = jnp.where(allowed, dot_nt(keys, q_ref[:, cols]), big_negative)
-        peak = jnp.max(s, axis=0, keepdims=True)
-        if not first:
-            out_before, peak_before, total_before = rest[:3]
-            peak = jnp.maximum(peak, peak_before[row, :])
-        p = jnp.exp(s - peak)
-        total = jnp.sum(p, axis=0, keepdims=True)
-        out = dot_nn(turned[HD:, :], p.astype(BF))
-        if first:
-            out_ref, peak_ref, total_ref = rest[-4:-1]
-            out_ref[cols, :] = out
-            peak_ref[row, :] = peak
-            total_ref[row, :] = total
-        else:
-            o_ref, lse_ref = rest[-3:-1]
-            fade = jnp.exp(peak_before[row, :] - peak)
-            total = total + fade * total_before[row, :]
-            out = out + fade * out_before[cols, :]
-            out = out * jnp.where(high >= 0, 1.0 / total, 0.0)
-            o_ref[:, cols] = out.T.astype(BF)
-            lse_ref[row, :] = peak + jnp.log(total)
+    def over(count):
+        key_pos = kp_ref[:count, :]
+        high = hi_ref[...]
+        allowed = (key_pos >= lo_ref[...]) & (key_pos <= high)
+        keys = kv_ref[:count, :HD]
+        for h in range(4):
+            cols = slice(h * HD, (h + 1) * HD)
+            row = slice(h, h + 1)
+            s = jnp.where(allowed, dot_nt(keys, q_ref[:, cols]), big_negative)
+            peak = jnp.max(s, axis=0, keepdims=True)
+            if not first:
+                out_before, peak_before, total_before = rest[:3]
+                peak = jnp.maximum(peak, peak_before[row, :])
+            p = jnp.exp(s - peak)
+            total = jnp.sum(p, axis=0, keepdims=True)
+            out = dot_nn(turned[HD:, :count], p.astype(BF))
+            if first:
+                out_ref, peak_ref, total_ref = rest[-4:-1]
+                out_ref[cols, :] = out
+                peak_ref[row, :] = peak
+                total_ref[row, :] = total
+            else:
+                natural_ref, o_ref, lse_ref = rest[-4:-1]
+                fade = jnp.exp(peak_before[row, :] - peak)
+                total = total + fade * total_before[row, :]
+                out = out + fade * out_before[cols, :]
+                out = out * jnp.where(high >= 0, 1.0 / total, 0.0)
+                out = out.T.astype(BF)
+                o_ref[:, cols] = out
+                for piece in range(4):
+                    natural_ref[natural_rows(pl.program_id(0), piece), cols] = out[
+                        64 * piece : 64 * piece + 64
+                    ]
+                lse_ref[row, :] = peak + jnp.log(total)
+
+    pl.when(pl.program_id(0) < 2)(lambda: over(ROWS // 2))
+    pl.when(pl.program_id(0) >= 2)(lambda: over(ROWS))
 
 
 def attend(q, kv, kp, lo, hi, before, *earlier):
     first = before is None
-    count = kv.shape[0]
     row = pl.BlockSpec((1, QB), lambda i: (0, i))
     rows = pl.BlockSpec((4, QB), lambda i: (0, i))
     flat = pl.BlockSpec((256, QB), lambda i: (0, i))
     block = pl.BlockSpec((QB, 256), lambda i: (i, 0))
+    held = pl.BlockSpec((ROWS, 256), lambda i: (0, 0))
     stat = jax.ShapeDtypeStruct((4, ROWS), F32)
+    result = jax.ShapeDtypeStruct((ROWS, 256), BF)
     carried = [] if first else list(before)
     return pl.pallas_call(
         functools.partial(attend_kernel, first),
         grid=(ROWS // QB,),
-        in_specs=[block, fixed((count, 2 * HD)), fixed((count, QB)), row, row]
+        in_specs=[block, fixed((ROWS, 2 * HD)), fixed((ROWS, QB)), row, row]
         + [flat, rows, rows][: len(carried)]
         + [ANYWHERE] * len(earlier),
-        out_specs=[flat, rows, rows] if first else [block, rows],
+        out_specs=[flat, rows, rows] if first else [held, block, rows],
         out_shape=[jax.ShapeDtypeStruct((256, ROWS), F32), stat, stat]
         if first
-        else [jax.ShapeDtypeStruct((ROWS, 256), BF), stat],
-        scratch_shapes=[pltpu.VMEM((2 * HD, count), BF)],
+        else [result, result, stat],
+        scratch_shapes=[pltpu.VMEM((2 * HD, ROWS), BF)],
         compiler_params=params(40),
-        cost_estimate=takes(11),
+        cost_estimate=takes(10),
         name="attend",
     )(q, kv, kp, lo, hi, *carried, *earlier)
 
@@ -159,54 +174,59 @@
         turned[...] = kv_ref[...].T
         values[...] = kv_ref[:, HD:]
 
-    key_pos = kp_ref[...]
-    allowed = (key_pos >= lo_ref[...]) & (key_pos <= hi_ref[...])
-    keys = kv_ref[:, :HD]
-    delta_all = (do_ref[...].astype(F32) * o_ref[...].astype(F32)).T
-    for h in range(4):
-        cols = slice(h * HD, (h + 1) * HD)
-        qh = q_ref[:, cols]
-        doh = do_ref[:, cols]
-        delta = jnp.sum(delta_all[cols], axis=0, keepdims=True)
-        s = dot_nt(keys, qh)
-        p = jnp.where(allowed, jnp.exp(s - lse_ref[h : h + 1, :]), 0.0)
-        ds = (p * (dot_nt(values[...], doh) - delta)).astype(BF)
-        dkv_ref[:, :HD] += dot_nn(ds, qh)
-        dkv_ref[:, HD:] += dot_nn(p.astype(BF), doh)
-        dq = dot_nn(turned[:HD, :], ds) * HD**-0.5
-        if first:
-            dq_ref[cols, :] = dq
-        else:
-            dq_ref[:, cols] = (dq + rest[0][cols, :]).T.astype(BF)
+    def over(count):
+        key_pos = kp_ref[:count, :]
+        allowed = (key_pos >= lo_ref[...]) & (key_pos <= hi_ref[...])
+        keys = kv_ref[:count, :HD]
+        delta_all = (do_ref[...].astype(F32) * o_ref[...].astype(F32)).T
+        for h in range(4):
+            cols = slice(h * HD, (h + 1) * HD)
+            qh = q_ref[:, cols]
+            doh = do_ref[:, cols]
+            delta = jnp.sum(delta_all[cols], axis=0, keepdims=True)
+            s = dot_nt(keys, qh)
+            p = jnp.where(allowed, jnp.exp(s - lse_ref[h : h + 1, :]), 0.0)
+            ds = (p * (dot_nt(values[:count, :], doh) - delta)).astype(BF)
+            dkv_ref[:count, :HD] += dot_nn(ds, qh)
+            dkv_ref[:count, HD:] += dot_nn(p.astype(BF), doh)
+            dq = dot_nn(turned[:HD, :count], ds) * HD**-0.5
+            if first:
+                dq_ref[cols, :] = dq
+            else:
+                dq = (dq + rest[0][cols, :]).T.astype(BF)
+                for piece in range(4):
+                    dq_ref[natural_rows(pl.program_id(0), piece), cols] = dq[
+                        64 * piece : 64 * piece + 64
+                    ]
+
+    pl.when(pl.program_id(0) < 2)(lambda: over(ROWS // 2))
+    pl.when(pl.program_id(0) >= 2)(lambda: over(ROWS))
 
 
 def attend_back(q, do, o, kv, kp, lo, hi, lse, earlier_dq, *earlier):
     first = earlier_dq is None
-    count = kv.shape[0]
     row = pl.BlockSpec((1, QB), lambda i: (0, i))
     block = pl.BlockSpec((QB, 256), lambda i: (i, 0))
     flat = pl.BlockSpec((256, QB), lambda i: (0, i))
+    held = lambda cols: pl.BlockSpec((ROWS, cols), lambda i: (0, 0))
     carried = [] if first else [earlier_dq]
     return pl.pallas_call(
         functools.partial(attend_back_kernel, first),
         grid=(ROWS // QB,),
-        in_specs=[block, block, block, fixed((count, 2 * HD)), fixed((count, QB)), row, row]
+        in_specs=[block, block, block, fixed((ROWS, 2 * HD)), fixed((ROWS, QB)), row, row]
         + [pl.BlockSpec((4, QB), lambda i: (0, i))]
         + [flat] * len(carried)
         + [ANYWHERE] * len(earlier),
-        out_specs=[
-            flat if first else block,
-            pl.BlockSpec((count, 2 * HD), lambda i: (0, 0)),
-        ],
+        out_specs=[flat if first else held(256), held(2 * HD)],
         out_shape=[
             jax.ShapeDtypeStruct((256, ROWS), F32)
             if first
             else jax.ShapeDtypeStruct((ROWS, 256), BF),
-            jax.ShapeDtypeStruct((count, 2 * HD), F32),
+            jax.ShapeDtypeStruct((ROWS, 2 * HD), F32),
         ],
-        scratch_shapes=[pltpu.VMEM((2 * HD, count), BF), pltpu.VMEM((count, HD), BF)],
+        scratch_shapes=[pltpu.VMEM((2 * HD, ROWS), BF), pltpu.VMEM((ROWS, HD), BF)],
         compiler_params=params(40),
-        cost_estimate=takes(12.5),
+        cost_estimate=takes(10),
         name="attend_back",
     )(q, do, o, kv, kp, lo, hi, lse, *carried, *earlier)
 
@@ -243,8 +263,12 @@
     for k in range(2):
         rows = slice(512 * k, 512 * k + 512)
         product = dot_nn(hat[rows, :], w_ref[...]).astype(BF)
-        q_ref[rows, :] = product[:, :256] * BF(HD**-0.5)
-        kv_ref[rows, :] = product[:, 256:]
+        for piece in range(4):
+            for late in range(2):
+                here = slice(128 * piece + 64 * late, 128 * piece + 64 * late + 64)
+                there = 512 * late + 256 * k + 64 * piece
+                q_ref[there : there + 64, :] = product[here, :256] * BF(HD**-0.5)
+                kv_ref[there : there + 64, :] = product[here, 256:]
 
 
 def project(pieces, raw):
@@ -272,7 +296,12 @@
     grad_att_ref, sum_ref, grad, sems = refs[-4:]
     for copy in fetch(pieces, grad, sems):
         copy.wait()
-    grad_att_ref[...] = dot_nt(grad[...], w_ref[...]).astype(BF)
+    grad_att = dot_nt(grad[...], w_ref[...]).astype(BF)
+    for piece in range(8):
+        for late in range(2):
+            here = 128 * piece + 64 * late
+            there = 512 * late + 64 * piece
+            grad_att_ref[there : there + 64, :] = grad_att[here : here + 64]
     for k in range(4):
         cols = slice(512 * k, 512 * k + 512)
         sum_ref[:, cols] = dot_tn(att_ref[...], grad[:, cols]).astype(BF)
@@ -624,7 +653,8 @@
     holders = jnp.stack([((x - dx) % 4 * 2 + zl) * 2 + (c + dc) % 2 for dx, dc in ORDER])
     picked = (holders[:, None] == jnp.arange(16, dtype=jnp.int32)[None, :]).astype(jnp.int32)
     spans = jnp.sum(picked[:, :, None] * span_order.reshape(1, 16, 2), axis=1)
-    return (spans.reshape(16, 1) * 64 + jnp.arange(64, dtype=jnp.int32)[None, :]).reshape(ROWS)
+    spans = spans.T.reshape(16, 1)
+    return (spans * 64 + jnp.arange(64, dtype=jnp.int32)[None, :]).reshape(ROWS)
 
 
 def norm_scale(rows):
@@ -695,7 +725,7 @@
     queries, own_kv, w_qkv, w_out = project(hat_pieces, attn_all)
     other_kv = lax.ppermute(own_kv, "zl", [(0, 1), (1, 0)])
     before = attend(queries, own_kv, key_pos[:ROWS], low_pos, high_pos, None)
-    att, lse = attend(
+    att, att_early, lse = attend(
         queries, other_kv, key_pos[ROWS:], low_pos, high_pos, before, *grad_pieces[1:4]
     )
     att_other = dot_nn(att[512:], w_out).astype(BF)
@@ -721,14 +751,14 @@
     grad_att, sum_out = hidden_products(hidden_pieces, att, w_out, ahead)
 
     grad_q, grad_kv = attend_back(
-        queries, grad_att, att, other_kv, key_pos[ROWS:], low_pos, high_pos, lse, None, ahead
+        queries, grad_att, att_early, other_kv, key_pos[ROWS:], low_pos, high_pos, lse, None, ahead
     )
     arrived = lax.ppermute(grad_kv.astype(BF), "zl", [(0, 1), (1, 0)])
     ahead_left, ahead_right, ahead_stays = scatter_second(ahead)
     grad_q, grad_kv = attend_back(
         queries,
         grad_att,
-        att,
+        att_early,
         own_kv,
         key_pos[:ROWS],
         low_pos,
@@ -740,7 +770,9 @@
     )
     ahead = scatter_third(ahead_left, ahead_right)
     block_out = (hidden + total((ahead_stays, *ahead))).astype(BF)
-    grad_mixed = jnp.concatenate([grad_q, (grad_kv + arrived.astype(F32)).astype(BF)], axis=1)
+    grad_kv = (grad_kv + arrived.astype(F32)).astype(BF)
+    grad_kv = grad_kv.reshape(2, 8, 64, 2 * HD).transpose(1, 0, 2, 3).reshape(ROWS, 2 * HD)
+    grad_mixed = jnp.concatenate([grad_q, grad_kv], axis=1)
     grad_mixed = tie(grad_mixed, *ahead)
     attn_parts = attn_grads(hat_pieces, grad_mixed, sum_out)
     attn_sums = lax.all_to_all(attn_parts, REP, 0, 0, tiled=True)
@@ -749,10 +781,11 @@
     last_other = dot_nt(last_rows[512:], w_qkv).astype(BF)
     last_mine = dot_nt(last_rows[:512], w_qkv)
     to_left, to_right, stays = scatter_second(scatter_first(last_mine, last_other))
-    grad_hat_one = total((stays, *scatter_third(to_left, to_right)))
+    last_thirds = scatter_third(to_left, to_right)
+    got = jnp.concatenate([attn_sums[:, :384], sums[:128]], axis=1).reshape(8, 16, 1920)
+    grad_hat_one = total((tie(stays, got), *last_thirds))
     in_grad = norm_back(grad_hat_one, hat_one, scale_one, grad_hidden).astype(BF)
-
-    got = jnp.concatenate([attn_sums[:, :384], sums[:128]], axis=1).reshape(8, 16, 1920)
+    sum_out = tie(attn_sums[:, 384:], got)
     got = lax.all_to_all(got, TP, 0, 0, tiled=True)
     got_qkv = got[:, :, :384].transpose(1, 0, 2).astype(F32)
     got_kv = got_qkv[:, :, 256:].reshape(16, 4, 2, 2, HD).sum(axis=2)
@@ -764,8 +797,8 @@
         ],
         axis=1,
     )
-    sum_out = attn_sums[:, 384:].reshape(8, 16, 256).transpose(1, 0, 2).reshape(16, 2048)
-    got_out = lax.ppermute(tie(sum_out, got), ALL, back(SPREAD)).astype(F32)
+    sum_out = sum_out.reshape(8, 16, 256).transpose(1, 0, 2).reshape(16, 2048)
+    got_out = lax.ppermute(sum_out, ALL, back(SPREAD)).astype(F32)
     tail = [sums[176:192, 512 * part : 512 * part + 512] for part in range(3)]
     got_down = jnp.concatenate([sums[128:176], jnp.concatenate(tail, axis=0)], axis=1)
     got_down = got_down[:44].astype(F32)

time: 446 us -> 431 us (0.966)
  Pallas kernels: 124 us -> 115 us
  waiting for transfers between devices: 121 us -> 114 us
    all_to_all x1, waiting for transfers between devices: 6.56 us -> 0.01 us  [body(): got = lax.all_to_all(got, TP, 0, 0, tiled=True)]
    pallas_call x2, Pallas kernels: 25.4 us -> 20.1 us  [attend_back(): pl.pallas_call(functools.partial(attend_back_kernel, first), grid=(ROWS /...]
    unnamed x173 -> x174, local copies, waits for them, and re-layouts: 18.7 us -> 16.8 us
  transfers between devices with their start and end apart: 58 -> 58, of which waited for: 19 -> 18; matrix products, arithmetic and copies ran while one was open for 9% -> 10% of each run, Pallas kernels for 21% -> 19%
where the time goes in v5:
time: 431 us; the launch traced here: 424 us
  Pallas kernels  115 us (27%)
  waiting for transfers between devices  114 us (26%)
  starting transfers between devices  110 us (26%)
  other arithmetic  33.7 us (8%)
  local copies, waits for them, and re-layouts  25.8 us (6%)
  between operations  17 us (4%)
  matrix products  8.41 us (2%)
    ppermute x28, waiting for transfers between devices, shift(): return lax.ppermute(block, 'x', [(i, (i + distance) % 4) for i in range(4)])  72 us
    ppermute x20, starting transfers between devices, swap(): return lax.ppermute(block, 'c', [(0, 1), (1, 0)])  41.9 us
    ppermute x28, starting transfers between devices, shift(): return lax.ppermute(block, 'x', [(i, (i + distance) % 4) for i in range(4)])  33.7 us
    pallas_call x1, Pallas kernels, feed_forward(): pl.pallas_call(feed_forward_kernel, grid=(2,), in_specs=[ANYWHERE] * 17,...  30.9 us
    pallas_call x2, Pallas kernels, attend(): pl.pallas_call(functools.partial(attend_kernel, first), grid=(ROWS // QB,...  20.4 us
    pallas_call x2, Pallas kernels, attend_back(): pl.pallas_call(functools.partial(attend_back_kernel, first), grid=(ROWS /...  20.1 us
    pallas_call x1, Pallas kernels, weight_grads(): pl.pallas_call(weight_grads_kernel, grid=(4,), in_specs=[pl.BlockSpec((12...  17.1 us
    unnamed x174, local copies, waits for them, and re-layouts  16.8 us
  transfers between devices with their start and end apart: 58, of which 18 were waited for; matrix products, arithmetic and copies ran while one was open for 10% of the time, Pallas kernels for 19%

profile of v5, /device:TPU:17, one launch (start us, length us, event | category | flops | bytes accessed | tf_op | source)
XLA Modules:
  0.0 424.1 jit_solution(8144931325063833636)
XLA Ops:
  12.3 5.1 %all-to-all-start = ((bf16[8,16,1920]{2,1,0:T(8,128)(2,1)}), bf16[8,16,1920]{2,1,0:T(8,128)(2,1)S(1)}, u32[]{:S(2)}, u32[]{:S(2)}) async-start(bf16[8,16,1920]{2,1,0:T(8,128)(2,1)} %pack.1), calls=%async_computation | async-start | bytes 983040 | tf_op jit(solution)/shard_map/all_to_all | solution.py:699
  17.5 6.3 %collective-permute-start.7 = (bf16[16,2048]{1,0:T(8,128)(2,1)S(1)}, bf16[16,2048]{1,0:T(8,128)(2,1)S(1)}, u32[]{:S(2)}, u32[]{:S(2)}) collective-permute-start(bf16[16,2048]{1,0:T(8,128)(2,1)S(1)} %convert_element_type.166), channel_id=1, source_target_pairs={{0,0},{1,2},{2,16},{3,18},{4,32},{5,34},{6,48},{7,50},{8,64},{9,66... | collective-permute-start | bytes 196616 | tf_op jit(solution)/shard_map/ppermute | solution.py:701
  23.8 7.6 %collective-permute-done.7 = bf16[16,2048]{1,0:T(8,128)(2,1)S(1)} collective-permute-done((bf16[16,2048]{1,0:T(8,128)(2,1)S(1)}, bf16[16,2048]{1,0:T(8,128)(2,1)S(1)}, u32[]{:S(2)}, u32[]{:S(2)}) %collective-permute-start.7) | collective-permute-done | bytes 65568 | tf_op jit(solution)/shard_map/ppermute | solution.py:701
  36.4 10.6 %collective-permute-done.refs_1_.refs_2_ = bf16[128,2048]{1,0:T(8,128)(2,1)S(1)} collective-permute-done((bf16[128,2048]{1,0:T(8,128)(2,1)}, bf16[128,2048]{1,0:T(8,128)(2,1)S(1)}, u32[]{:S(2)}, u32[]{:S(2)}) %collective-permute-start) | collective-permute-done | bytes 524320 | tf_op jit(solution)/shard_map/ppermute | solution.py:565
  48.8 9.1 %collective-permute-done.2.refs_3_.refs_4_ = bf16[128,2048]{1,0:T(8,128)(2,1)S(1)} collective-permute-done((bf16[128,2048]{1,0:T(8,128)(2,1)}, bf16[128,2048]{1,0:T(8,128)(2,1)S(1)}, u32[]{:S(2)}, u32[]{:S(2)}) %collective-permute-start.2) | collective-permute-done | bytes 524320 | tf_op jit(solution)/shard_map/ppermute | solution.py:565
  60.8 14.8 %all-gather.3.cloned.1.call-done.refs_8_.refs_1_ = bf16[2048,640]{1,0:T(8,128)(2,1)} async-done(((bf16[128,640]{1,0:T(8,128)(2,1)}), bf16[2048,640]{1,0:T(8,128)(2,1)}) %all-gather.3.cloned.1.call-update) | async-done | bytes 2621456 | tf_op jit(solution)/shard_map/all_gather | solution.py:704
  84.6 6.9 %project.1 = (bf16[1024,256]{1,0:T(8,128)(2,1)}, bf16[1024,128]{1,0:T(8,128)(2,1)}, bf16[2048,384]{1,0:T(8,128)(2,1)}, bf16[256,2048]{1,0:T(8,128)(2,1)}) custom-call(bf16[128,2048]{1,0:T(8,128)(2,1)} %tie.10.refs_0_, bf16[128,2048]{1,0:T(8,128)(2,1)} %copy-done.35, bf16[128,2048]{1,0:T(8,128)(2,1)} %copy-done.36, bf16[128,2048]{1,0:T(8,128)(2,1)} %copy-done.37, ...), custom_call_target="tpu_custom_call" | custom-call | flops 5750000128 | bytes 1048576 | tf_op jit(solution)/shard_map/project/pallas_call | solution.py:276
  94.5 9.8 %attend.2 = (f32[256,1024]{1,0:T(8,128)S(1)}, f32[4,1024]{1,0:T(4,128)S(1)}, f32[4,1024]{1,0:T(4,128)S(1)}) custom-call(bf16[1024,256]{1,0:T(8,128)(2,1)S(1)} %copy-done.14, bf16[1024,128]{1,0:T(8,128)(2,1)S(1)} %copy-done.12, s32[1024,256]{1,0:T(8,128)S(1)} %broadcast_in_dim.17.kp_ref, s32[1,1024]{1,0:T(1,128)S(1)} %get-tuple-element.129.lo_ref, ...), custom_call_target="tpu_custom_call" | custom-call | flops 11500000256 | bytes 1048576 | tf_op jit(solution)/shard_map/attend/pallas_call | solution.py:151
  108.1 10.6 %attend.3 = (bf16[1024,256]{1,0:T(8,128)(2,1)S(1)}, bf16[1024,256]{1,0:T(8,128)(2,1)S(1)}, f32[4,1024]{1,0:T(4,128)S(1)}) custom-call(bf16[1024,256]{1,0:T(8,128)(2,1)S(1)} %copy-done.15, bf16[1024,128]{1,0:T(8,128)(2,1)S(1)} %collective-permute-done.8.kv_ref, s32[1024,256]{1,0:T(8,128)S(1)} %broadcast_in_dim.13.kp_ref, ...), custom_call_target="tpu_custom_call" | custom-call | flops 11500000256 | bytes 1048576 | tf_op jit(solution)/shard_map/attend/pallas_call | solution.py:151
  121.8 3.8 collective-permute-done.12
  128.3 5.8 %collective-permute-done.13 = bf16[64,2048]{1,0:T(8,128)(2,1)S(1)} collective-permute-done((bf16[64,2048]{1,0:T(8,128)(2,1)S(1)}, bf16[64,2048]{1,0:T(8,128)(2,1)S(1)}, u32[]{:S(2)}, u32[]{:S(2)}) %collective-permute-start.13) | collective-permute-done | bytes 262176 | tf_op jit(solution)/shard_map/ppermute | solution.py:565
  142.3 8.0 %collective-permute-done.16 = bf16[128,2048]{1,0:T(8,128)(2,1)S(1)} collective-permute-done((bf16[128,2048]{1,0:T(8,128)(2,1)S(1)}, bf16[128,2048]{1,0:T(8,128)(2,1)S(1)}, u32[]{:S(2)}, u32[]{:S(2)}) %collective-permute-start.16) | collective-permute-done | bytes 524320 | tf_op jit(solution)/shard_map/ppermute | solution.py:565
  158.0 5.4 %collective-permute-done.17.refs_1_ = bf16[128,2048]{1,0:T(8,128)(2,1)S(1)} collective-permute-done((bf16[128,2048]{1,0:T(8,128)(2,1)S(1)}, bf16[128,2048]{1,0:T(8,128)(2,1)S(1)}, u32[]{:S(2)}, u32[]{:S(2)}) %collective-permute-start.17) | collective-permute-done | bytes 524320 | tf_op jit(solution)/shard_map/ppermute | solution.py:565
  163.4 5.2 %collective-permute-start.21 = (bf16[128,2048]{1,0:T(8,128)(2,1)S(1)}, bf16[128,2048]{1,0:T(8,128)(2,1)S(1)}, u32[]{:S(2)}, u32[]{:S(2)}) collective-permute-start(bf16[128,2048]{1,0:T(8,128)(2,1)S(1)} %collective-permute-done.17.refs_1_), channel_id=1, source_target_pairs={{0,1},{1,0},{2,3},{3,2},{4,5},{5,4},{6,7},{7,6},{8,9},{9,8},{10,11... | collective-permute-start | bytes 1572872 | tf_op jit(solution)/shard_map/ppermute | solution.py:569
  168.6 8.5 %collective-permute-start.22 = (bf16[128,2048]{1,0:T(8,128)(2,1)S(1)}, bf16[128,2048]{1,0:T(8,128)(2,1)S(1)}, u32[]{:S(2)}, u32[]{:S(2)}) collective-permute-start(bf16[128,2048]{1,0:T(8,128)(2,1)S(1)} %collective-permute-done.18.refs_2_), channel_id=1, source_target_pairs={{0,1},{1,0},{2,3},{3,2},{4,5},{5,4},{6,7},{7,6},{8,9},{9,8},{10,11... | collective-permute-start | bytes 1572872 | tf_op jit(solution)/shard_map/ppermute | solution.py:569
  181.1 30.9 %feed_forward.1 = (bf16[1024,768]{1,0:T(8,128)(2,1)}, bf16[1024,1536]{1,0:T(8,128)(2,1)}, bf16[512,2048]{1,0:T(8,128)(2,1)}, bf16[512,2048]{1,0:T(8,128)(2,1)}, ...) custom-call(bf16[128,2048]{1,0:T(8,128)(2,1)} %copy-done.49, bf16[128,2048]{1,0:T(8,128)(2,1)} %copy-done.71, ...), custom_call_target="tpu_custom_call" | custom-call | flops 32199999488 | bytes 1048576 | tf_op jit(solution)/shard_map/feed_forward/pallas_call | solution.py:418
  212.5 4.2 collective-permute-done.28
  221.2 5.9 %collective-permute-done.29 = bf16[64,2048]{1,0:T(8,128)(2,1)S(1)} collective-permute-done((bf16[64,2048]{1,0:T(8,128)(2,1)S(1)}, bf16[64,2048]{1,0:T(8,128)(2,1)S(1)}, u32[]{:S(2)}, u32[]{:S(2)}) %collective-permute-start.29) | collective-permute-done | bytes 262176 | tf_op jit(solution)/shard_map/ppermute | solution.py:565
  232.7 17.1 %weight_grads.1 = bf16[16,192,1536]{2,1,0:T(8,128)(2,1)} custom-call(bf16[128,2048]{1,0:T(8,128)(2,1)} %copy-done.49, bf16[128,2048]{1,0:T(8,128)(2,1)} %copy-done.71, bf16[128,2048]{1,0:T(8,128)(2,1)} %copy-done.72, bf16[128,2048]{1,0:T(8,128)(2,1)} %copy-done.73, bf16[128,2048]{1,0:T(8,128)(2,1)} %copy-done.75, bf16[128,2048]{1,0:T(8,128)(2,1)} %copy-done.76, ...), custom_call_target="tpu_custom_call" | custom-call | flops 18975000576 | bytes 1048576 | tf_op jit(solution)/shard_map/weight_grads/pallas_call | solution.py:465
  260.7 10.6 %collective-permute-done.38.refs_1_ = bf16[128,2048]{1,0:T(8,128)(2,1)S(1)} collective-permute-done((bf16[128,2048]{1,0:T(8,128)(2,1)S(1)}, bf16[128,2048]{1,0:T(8,128)(2,1)S(1)}, u32[]{:S(2)}, u32[]{:S(2)}) %collective-permute-start.38) | collective-permute-done | bytes 524320 | tf_op jit(solution)/shard_map/ppermute | solution.py:565
  271.3 12.0 %collective-permute-start.42 = (bf16[128,2048]{1,0:T(8,128)(2,1)S(1)}, bf16[128,2048]{1,0:T(8,128)(2,1)S(1)}, u32[]{:S(2)}, u32[]{:S(2)}) collective-permute-start(bf16[128,2048]{1,0:T(8,128)(2,1)S(1)} %collective-permute-done.38.refs_1_), channel_id=1, source_target_pairs={{0,1},{1,0},{2,3},{3,2},{4,5},{5,4},{6,7},{7,6},{8,9},{9,8},{10,11... | collective-permute-start | bytes 1572872 | tf_op jit(solution)/shard_map/ppermute | solution.py:569
  283.8 4.5 %fusion.35 = (bf16[512,2048]{1,0:T(8,128)(2,1)S(1)}, f32[512,2048]{1,0:T(8,128)}) fusion(bf16[512,2048]{1,0:T(8,128)(2,1)S(1)} %collective-permute-done.33, bf16[512,2048]{1,0:T(8,128)(2,1)} %get-tuple-element.50), kind=kLoop, calls=%fused_computation.115 | loop fusion | flops 4194304 | bytes 10485760 | tf_op jit(solution)/shard_map/convert.15
  293.6 7.4 %hidden_products.1 = (bf16[1024,256]{1,0:T(8,128)(2,1)}, bf16[256,2048]{1,0:T(8,128)(2,1)}) custom-call(bf16[128,2048]{1,0:T(8,128)(2,1)} %tie.13.refs_1_.refs_0_, bf16[128,2048]{1,0:T(8,128)(2,1)} %copy-done.78, bf16[128,2048]{1,0:T(8,128)(2,1)} %copy-done.79, bf16[128,2048]{1,0:T(8,128)(2,1)} %copy-done.80, bf16[128,2048]{1,0:T(8,128)(2,1)} %copy-done.81, ...), custom_call_target="tpu_custom_call" | custom-call | flops 6899999744 | bytes 1048576 | tf_op jit(solution)/shard_map/hidden_products/pallas_call | solution.py:311
  304.4 9.7 %attend_back.2 = (f32[256,1024]{1,0:T(8,128)S(1)}, f32[1024,128]{1,0:T(8,128)S(1)}) custom-call(bf16[1024,256]{1,0:T(8,128)(2,1)S(1)} %copy-done.16, bf16[1024,256]{1,0:T(8,128)(2,1)S(1)} %copy-done.17, bf16[1024,256]{1,0:T(8,128)(2,1)S(1)} %copy-done.20, bf16[1024,128]{1,0:T(8,128)(2,1)S(1)} %collective-permute-done.8.kv_ref, ...), custom_call_target="tpu_custom_call" | custom-call | flops 11500000256 | bytes 1048576 | tf_op jit(solution)/shard_map/attend_back/pallas_call | solution.py:213
  318.8 10.4 %attend_back.3 = (bf16[1024,256]{1,0:T(8,128)(2,1)S(1)}, f32[1024,128]{1,0:T(8,128)S(1)}) custom-call(bf16[1024,256]{1,0:T(8,128)(2,1)S(1)} %copy-done.16, bf16[1024,256]{1,0:T(8,128)(2,1)S(1)} %copy-done.18, bf16[1024,256]{1,0:T(8,128)(2,1)S(1)} %copy-done.20, bf16[1024,128]{1,0:T(8,128)(2,1)S(1)} %copy-done.13, s32[1024,256]{1,0:T(8,128)S(1)} %broadcast_in_dim.17.kp_ref, ...), custom_call_target="tpu_custom_call" | custom-call | flops 11500000256 | bytes 1048576 | tf_op jit(solution)/shard_map/attend_back/pallas_call | solution.py:213
  331.0 7.7 %attn_grads.1.refs_1_ = bf16[16,128,640]{2,1,0:T(8,128)(2,1)} custom-call(bf16[128,2048]{1,0:T(8,128)(2,1)} %tie.10.refs_0_, bf16[128,2048]{1,0:T(8,128)(2,1)} %copy-done.35, bf16[128,2048]{1,0:T(8,128)(2,1)} %copy-done.36, bf16[128,2048]{1,0:T(8,128)(2,1)} %copy-done.37, bf16[128,2048]{1,0:T(8,128)(2,1)} %copy-done.46, bf16[128,2048]{1,0:T(8,128)(2,1)} %copy-done.47, ...), custom_call_target="tpu_custom_call" | custom-call | flops 4600000000 | bytes 1048576 | tf_op jit(solution)/shard_map/attn_grads/pallas_call | solution.py:638
  340.2 3.6 convolution_convert_fusion.1
  345.3 6.8 %all-to-all-start.1 = ((bf16[16,128,640]{2,1,0:T(8,128)(2,1)}), bf16[16,128,640]{2,1,0:T(8,128)(2,1)S(1)}, u32[]{:S(2)}, u32[]{:S(2)}) async-start(bf16[16,128,640]{2,1,0:T(8,128)(2,1)} %attn_grads.1.refs_1_), calls=%async_computation.1 | async-start | bytes 5242880 | tf_op jit(solution)/shard_map/all_to_all | solution.py:778
  357.6 5.1 %collective-permute-done.47 = bf16[64,2048]{1,0:T(8,128)(2,1)S(1)} collective-permute-done((bf16[64,2048]{1,0:T(8,128)(2,1)S(1)}, bf16[64,2048]{1,0:T(8,128)(2,1)S(1)}, u32[]{:S(2)}, u32[]{:S(2)}) %collective-permute-start.47) | collective-permute-done | bytes 262176 | tf_op jit(solution)/shard_map/ppermute | solution.py:565
  373.8 11.9 %all-to-all-done.1 = bf16[16,128,640]{2,1,0:T(8,128)(2,1)S(1)} async-done(((bf16[16,128,640]{2,1,0:T(8,128)(2,1)}), bf16[16,128,640]{2,1,0:T(8,128)(2,1)S(1)}, u32[]{:S(2)}, u32[]{:S(2)}) %all-to-all-start.1) | async-done | bytes 2621472 | tf_op jit(solution)/shard_map/all_to_all | solution.py:778
  388.5 5.9 %all-to-all-start.2 = ((bf16[8,16,1920]{2,1,0:T(8,128)(2,1)}), bf16[8,16,1920]{2,1,0:T(8,128)(2,1)S(1)}, u32[]{:S(2)}, u32[]{:S(2)}) async-start(bf16[8,16,1920]{2,1,0:T(8,128)(2,1)} %bitcast.29.refs_1_), calls=%async_computation.3 | async-start | bytes 983040 | tf_op jit(solution)/shard_map/all_to_all | solution.py:789
  397.4 8.8 %collective-permute-start.51 = (bf16[16,2048]{1,0:T(8,128)(2,1)S(1)}, bf16[16,2048]{1,0:T(8,128)(2,1)S(1)}, u32[]{:S(2)}, u32[]{:S(2)}) collective-permute-start(bf16[16,2048]{1,0:T(8,128)(2,1)S(1)} %bitcast.73), channel_id=1, source_target_pairs={{0,0},{2,1},{16,2},{18,3},{32,4},{34,5},{48,6},{50,7},{64,8},{66,9... | collective-permute-start | bytes 196616 | tf_op jit(solution)/shard_map/ppermute | solution.py:801
  (379 shorter events, 127.1 us)
Async XLA Ops:
  12.3 19.0 %all-to-all-start = ((bf16[8,16,1920]{2,1,0:T(8,128)(2,1)}), bf16[8,16,1920]{2,1,0:T(8,128)(2,1)S(1)}, u32[]{:S(2)}, u32[]{:S(2)}) async-start(bf16[8,16,1920]{2,1,0:T(8,128)(2,1)} %pack.1), calls=%async_computation | async-start | bytes 983040 | tf_op jit(solution)/shard_map/all_to_all | solution.py:699
  17.4 58.2 %all-gather.3.cloned.1.call-start = ((), (), s32[]{:S(2)}) async-start(), calls=%async_computation.4 | async-start | bytes 2785280 | tf_op jit(solution)/shard_map/all_gather | solution.py:704
  32.1 149.0 %all-gather.5.cloned.1.call-start = ((), (), s32[]{:S(2)}) async-start(), calls=%async_computation.5 | async-start | bytes 10027008 | tf_op jit(solution)/shard_map/all_gather | solution.py:711
  36.0 21.8 %collective-permute-start.2 = (bf16[128,2048]{1,0:T(8,128)(2,1)}, bf16[128,2048]{1,0:T(8,128)(2,1)S(1)}, u32[]{:S(2)}, u32[]{:S(2)}) collective-permute-start(bf16[128,2048]{1,0:T(8,128)(2,1)} %tie.10.refs_0_), channel_id=1, source_target_pairs={{0,8},{4,12},{8,0},{12,4},{1,9},{5,13},{9,1},{13,5},{2,10},{6,14},... | collective-permute-start | bytes 1572872 | tf_op jit(solution)/shard_map/ppermute | solution.py:565
  36.3 23.6 %collective-permute-start.3 = (bf16[128,2048]{1,0:T(8,128)(2,1)}, bf16[128,2048]{1,0:T(8,128)(2,1)S(1)}, u32[]{:S(2)}, u32[]{:S(2)}) collective-permute-start(bf16[128,2048]{1,0:T(8,128)(2,1)} %tie.10.refs_0_), channel_id=1, source_target_pairs={{0,1},{1,0},{2,3},{3,2},{4,5},{5,4},{6,7},{7,6},{8,9},{9,8},{10,11... | collective-permute-start | bytes 1572872 | tf_op jit(solution)/shard_map/ppermute | solution.py:569
  75.6 311.0 %reduce-scatter.2.cloned.1.call-start = ((), (), s32[]{:S(2)}) async-start(), calls=%async_computation.6 | async-start | bytes 10027008 | tf_op jit(solution)/shard_map/reduce_scatter | solution.py:749
  80.4 24.0 %collective-permute-start.9 = (bf16[128,2048]{1,0:T(8,128)(2,1)}, bf16[128,2048]{1,0:T(8,128)(2,1)S(1)}, u32[]{:S(2)}, u32[]{:S(2)}) collective-permute-start(bf16[128,2048]{1,0:T(8,128)(2,1)} %tie.11.refs_8_), channel_id=1, source_target_pairs={{0,4},{4,8},{8,12},{12,0},{1,5},{5,9},{9,13},{13,1},{2,6},{6,10},{... | collective-permute-start | bytes 1572872 | tf_op jit(solution)/shard_map/ppermute | solution.py:565
  81.6 22.8 %collective-permute-start.10 = (bf16[128,2048]{1,0:T(8,128)(2,1)}, bf16[128,2048]{1,0:T(8,128)(2,1)S(1)}, u32[]{:S(2)}, u32[]{:S(2)}) collective-permute-start(bf16[128,2048]{1,0:T(8,128)(2,1)} %tie.11.refs_8_), channel_id=1, source_target_pairs={{0,12},{4,0},{8,4},{12,8},{1,13},{5,1},{9,5},{13,9},{2,14},{6,2},{... | collective-permute-start | bytes 1572872 | tf_op jit(solution)/shard_map/ppermute | solution.py:565
  83.1 23.0 %collective-permute-start.11 = (bf16[128,2048]{1,0:T(8,128)(2,1)}, bf16[128,2048]{1,0:T(8,128)(2,1)S(1)}, u32[]{:S(2)}, u32[]{:S(2)}) collective-permute-start(bf16[128,2048]{1,0:T(8,128)(2,1)} %tie.11.refs_8_), channel_id=1, source_target_pairs={{0,8},{4,12},{8,0},{12,4},{1,9},{5,13},{9,1},{13,5},{2,10},{6,14},... | collective-permute-start | bytes 1572872 | tf_op jit(solution)/shard_map/ppermute | solution.py:565
  91.5 15.4 %collective-permute-start.8 = (bf16[1024,128]{1,0:T(8,128)(2,1)}, bf16[1024,128]{1,0:T(8,128)(2,1)S(1)}, u32[]{:S(2)}, u32[]{:S(2)}) collective-permute-start(bf16[1024,128]{1,0:T(8,128)(2,1)} %get-tuple-element.44.kv_ref), channel_id=1, source_target_pairs={{0,2},{2,0},{1,3},{3,1},{4,6},{6,4},{5,7},{7,5},{8,10},{10,8},{9,1... | collective-permute-start | bytes 786440 | tf_op jit(solution)/shard_map/ppermute | solution.py:726
  141.9 16.0 %collective-permute-start.26 = (bf16[128,2048]{1,0:T(8,128)(2,1)S(1)}, bf16[128,2048]{1,0:T(8,128)(2,1)S(1)}, u32[]{:S(2)}, u32[]{:S(2)}) collective-permute-start(bf16[128,2048]{1,0:T(8,128)(2,1)S(1)} %collective-permute-done.10.rest_4_.refs_10_), channel_id=1, source_target_pairs={{0,1},{1,0},{2,3},{3,2},{4,5},{5,4},{6,7},{7,6},{8,9},{9,8},{10,11... | collective-permute-start | bytes 1572872 | tf_op jit(solution)/shard_map/ppermute | solution.py:569
  151.0 17.6 %collective-permute-start.18 = (bf16[128,2048]{1,0:T(8,128)(2,1)S(1)}, bf16[128,2048]{1,0:T(8,128)(2,1)S(1)}, u32[]{:S(2)}, u32[]{:S(2)}) collective-permute-start(bf16[128,2048]{1,0:T(8,128)(2,1)S(1)} %multiply_convert_fusion.refs_0_), channel_id=1, source_target_pairs={{0,12},{4,0},{8,4},{12,8},{1,13},{5,1},{9,5},{13,9},{2,14},{6,2},{... | collective-permute-start | bytes 1572872 | tf_op jit(solution)/shard_map/ppermute | solution.py:565
  153.7 23.4 %collective-permute-start.19 = (bf16[128,2048]{1,0:T(8,128)(2,1)S(1)}, bf16[128,2048]{1,0:T(8,128)(2,1)S(1)}, u32[]{:S(2)}, u32[]{:S(2)}) collective-permute-start(bf16[128,2048]{1,0:T(8,128)(2,1)S(1)} %multiply_convert_fusion.refs_0_), channel_id=1, source_target_pairs={{0,8},{4,12},{8,0},{12,4},{1,9},{5,13},{9,1},{13,5},{2,10},{6,14},... | collective-permute-start | bytes 1572872 | tf_op jit(solution)/shard_map/ppermute | solution.py:565
  154.8 24.5 %collective-permute-start.27 = (bf16[128,2048]{1,0:T(8,128)(2,1)S(1)}, bf16[128,2048]{1,0:T(8,128)(2,1)S(1)}, u32[]{:S(2)}, u32[]{:S(2)}) collective-permute-start(bf16[128,2048]{1,0:T(8,128)(2,1)S(1)} %copy-done.11), channel_id=1, source_target_pairs={{0,1},{1,0},{2,3},{3,2},{4,5},{5,4},{6,7},{7,6},{8,9},{9,8},{10,11... | collective-permute-start | bytes 1572872 | tf_op jit(solution)/shard_map/ppermute | solution.py:569
  157.9 21.4 %collective-permute-start.20 = (bf16[128,2048]{1,0:T(8,128)(2,1)S(1)}, bf16[128,2048]{1,0:T(8,128)(2,1)S(1)}, u32[]{:S(2)}, u32[]{:S(2)}) collective-permute-start(bf16[128,2048]{1,0:T(8,128)(2,1)S(1)} %multiply_convert_fusion.refs_0_), channel_id=1, source_target_pairs={{0,1},{1,0},{2,3},{3,2},{4,5},{5,4},{6,7},{7,6},{8,9},{9,8},{10,11... | collective-permute-start | bytes 1572872 | tf_op jit(solution)/shard_map/ppermute | solution.py:569
  163.4 15.9 %collective-permute-start.21 = (bf16[128,2048]{1,0:T(8,128)(2,1)S(1)}, bf16[128,2048]{1,0:T(8,128)(2,1)S(1)}, u32[]{:S(2)}, u32[]{:S(2)}) collective-permute-start(bf16[128,2048]{1,0:T(8,128)(2,1)S(1)} %collective-permute-done.17.refs_1_), channel_id=1, source_target_pairs={{0,1},{1,0},{2,3},{3,2},{4,5},{5,4},{6,7},{7,6},{8,9},{9,8},{10,11... | collective-permute-start | bytes 1572872 | tf_op jit(solution)/shard_map/ppermute | solution.py:569
  229.9 20.0 %collective-permute-start.32 = (bf16[128,2048]{1,0:T(8,128)(2,1)S(1)}, bf16[128,2048]{1,0:T(8,128)(2,1)S(1)}, u32[]{:S(2)}, u32[]{:S(2)}) collective-permute-start(bf16[128,2048]{1,0:T(8,128)(2,1)S(1)} %pad_maximum_fusion.4.refs_19_), channel_id=1, source_target_pairs={{0,4},{4,8},{8,12},{12,0},{1,5},{5,9},{9,13},{13,1},{2,6},{6,10},{... | collective-permute-start | bytes 1572872 | tf_op jit(solution)/shard_map/ppermute | solution.py:565
  230.0 19.9 %collective-permute-start.30 = (bf16[128,2048]{1,0:T(8,128)(2,1)S(1)}, bf16[128,2048]{1,0:T(8,128)(2,1)S(1)}, u32[]{:S(2)}, u32[]{:S(2)}) collective-permute-start(bf16[128,2048]{1,0:T(8,128)(2,1)S(1)} %pad_maximum_fusion.3.refs_18_), channel_id=1, source_target_pairs={{0,12},{4,0},{8,4},{12,8},{1,13},{5,1},{9,5},{13,9},{2,14},{6,2},{... | collective-permute-start | bytes 1572872 | tf_op jit(solution)/shard_map/ppermute | solution.py:565
  254.4 29.4 %collective-permute-start.33 = (bf16[512,2048]{1,0:T(8,128)(2,1)}, bf16[512,2048]{1,0:T(8,128)(2,1)S(1)}, u32[]{:S(2)}, u32[]{:S(2)}) collective-permute-start(bf16[512,2048]{1,0:T(8,128)(2,1)} %tie.14), channel_id=1, source_target_pairs={{0,1},{1,0},{2,3},{3,2},{4,5},{5,4},{6,7},{7,6},{8,9},{9,8},{10,11... | collective-permute-start | bytes 6291464 | tf_op jit(solution)/shard_map/ppermute | solution.py:569
  256.5 14.8 %collective-permute-start.38 = (bf16[128,2048]{1,0:T(8,128)(2,1)S(1)}, bf16[128,2048]{1,0:T(8,128)(2,1)S(1)}, u32[]{:S(2)}, u32[]{:S(2)}) collective-permute-start(bf16[128,2048]{1,0:T(8,128)(2,1)S(1)} %copy-done.30), channel_id=1, source_target_pairs={{0,4},{4,8},{8,12},{12,0},{1,5},{5,9},{9,13},{13,1},{2,6},{6,10},{... | collective-permute-start | bytes 1572872 | tf_op jit(solution)/shard_map/ppermute | solution.py:565
  256.5 26.8 %collective-permute-start.39 = (bf16[128,2048]{1,0:T(8,128)(2,1)S(1)}, bf16[128,2048]{1,0:T(8,128)(2,1)S(1)}, u32[]{:S(2)}, u32[]{:S(2)}) collective-permute-start(bf16[128,2048]{1,0:T(8,128)(2,1)S(1)} %copy-done.30), channel_id=1, source_target_pairs={{0,12},{4,0},{8,4},{12,8},{1,13},{5,1},{9,5},{13,9},{2,14},{6,2},{... | collective-permute-start | bytes 1572872 | tf_op jit(solution)/shard_map/ppermute | solution.py:565
  259.2 24.2 %collective-permute-start.40 = (bf16[128,2048]{1,0:T(8,128)(2,1)S(1)}, bf16[128,2048]{1,0:T(8,128)(2,1)S(1)}, u32[]{:S(2)}, u32[]{:S(2)}) collective-permute-start(bf16[128,2048]{1,0:T(8,128)(2,1)S(1)} %copy-done.30), channel_id=1, source_target_pairs={{0,8},{4,12},{8,0},{12,4},{1,9},{5,13},{9,1},{13,5},{2,10},{6,14},... | collective-permute-start | bytes 1572872 | tf_op jit(solution)/shard_map/ppermute | solution.py:565
  259.2 32.4 %collective-permute-start.41 = (bf16[128,2048]{1,0:T(8,128)(2,1)S(1)}, bf16[128,2048]{1,0:T(8,128)(2,1)S(1)}, u32[]{:S(2)}, u32[]{:S(2)}) collective-permute-start(bf16[128,2048]{1,0:T(8,128)(2,1)S(1)} %copy-done.30), channel_id=1, source_target_pairs={{0,1},{1,0},{2,3},{3,2},{4,5},{5,4},{6,7},{7,6},{8,9},{9,8},{10,11... | collective-permute-start | bytes 1572872 | tf_op jit(solution)/shard_map/ppermute | solution.py:569
  271.3 20.5 %collective-permute-start.42 = (bf16[128,2048]{1,0:T(8,128)(2,1)S(1)}, bf16[128,2048]{1,0:T(8,128)(2,1)S(1)}, u32[]{:S(2)}, u32[]{:S(2)}) collective-permute-start(bf16[128,2048]{1,0:T(8,128)(2,1)S(1)} %collective-permute-done.38.refs_1_), channel_id=1, source_target_pairs={{0,1},{1,0},{2,3},{3,2},{4,5},{5,4},{6,7},{7,6},{8,9},{9,8},{10,11... | collective-permute-start | bytes 1572872 | tf_op jit(solution)/shard_map/ppermute | solution.py:569
  289.2 25.1 %collective-permute-start.34 = (bf16[64,2048]{1,0:T(8,128)(2,1)}, bf16[64,2048]{1,0:T(8,128)(2,1)}, u32[]{:S(2)}, u32[]{:S(2)}) collective-permute-start(bf16[64,2048]{1,0:T(8,128)(2,1)} %get-tuple-element.103), channel_id=1, source_target_pairs={{0,12},{4,0},{8,4},{12,8},{1,13},{5,1},{9,5},{13,9},{2,14},{6,2},{... | collective-permute-start | bytes 786440 | tf_op jit(solution)/shard_map/ppermute | solution.py:565
  291.6 22.8 %collective-permute-start.36 = (bf16[64,2048]{1,0:T(8,128)(2,1)S(1)}, bf16[64,2048]{1,0:T(8,128)(2,1)}, u32[]{:S(2)}, u32[]{:S(2)}) collective-permute-start(bf16[64,2048]{1,0:T(8,128)(2,1)S(1)} %get-tuple-element.104), channel_id=1, source_target_pairs={{0,4},{4,8},{8,12},{12,0},{1,5},{5,9},{9,13},{13,1},{2,6},{6,10},{... | collective-permute-start | bytes 786440 | tf_op jit(solution)/shard_map/ppermute | solution.py:565
  314.2 15.0 %collective-permute-start.45 = (bf16[1024,128]{1,0:T(8,128)(2,1)S(1)}, bf16[1024,128]{1,0:T(8,128)(2,1)S(1)}, u32[]{:S(2)}, u32[]{:S(2)}) collective-permute-start(bf16[1024,128]{1,0:T(8,128)(2,1)S(1)} %convert_element_type.192), channel_id=1, source_target_pairs={{0,2},{2,0},{1,3},{3,1},{4,6},{6,4},{5,7},{7,5},{8,10},{10,8},{9,1... | collective-permute-start | bytes 786440 | tf_op jit(solution)/shard_map/ppermute | solution.py:756
  315.6 14.6 %collective-permute-start.37 = (bf16[128,2048]{1,0:T(8,128)(2,1)S(1)}, bf16[128,2048]{1,0:T(8,128)(2,1)S(1)}, u32[]{:S(2)}, u32[]{:S(2)}) collective-permute-start(bf16[128,2048]{1,0:T(8,128)(2,1)S(1)} %pad_maximum_fusion.6.rest_2_), channel_id=1, source_target_pairs={{0,4},{4,8},{8,12},{12,0},{1,5},{5,9},{9,13},{13,1},{2,6},{6,10},{... | collective-permute-start | bytes 1572872 | tf_op jit(solution)/shard_map/ppermute | solution.py:565
  345.3 40.4 %all-to-all-start.1 = ((bf16[16,128,640]{2,1,0:T(8,128)(2,1)}), bf16[16,128,640]{2,1,0:T(8,128)(2,1)S(1)}, u32[]{:S(2)}, u32[]{:S(2)}) async-start(bf16[16,128,640]{2,1,0:T(8,128)(2,1)} %attn_grads.1.refs_1_), calls=%async_computation.1 | async-start | bytes 5242880 | tf_op jit(solution)/shard_map/all_to_all | solution.py:778
  366.5 28.0 %collective-permute-start.50 = (bf16[128,2048]{1,0:T(8,128)(2,1)}, bf16[128,2048]{1,0:T(8,128)(2,1)}, u32[]{:S(2)}, u32[]{:S(2)}) collective-permute-start(bf16[128,2048]{1,0:T(8,128)(2,1)} %pad_maximum_fusion.8), channel_id=1, source_target_pairs={{0,4},{4,8},{8,12},{12,0},{1,5},{5,9},{9,13},{13,1},{2,6},{6,10},{... | collective-permute-start | bytes 1572872 | tf_op jit(solution)/shard_map/ppermute | solution.py:565
  367.3 27.2 %collective-permute-start.48 = (bf16[128,2048]{1,0:T(8,128)(2,1)}, bf16[128,2048]{1,0:T(8,128)(2,1)}, u32[]{:S(2)}, u32[]{:S(2)}) collective-permute-start(bf16[128,2048]{1,0:T(8,128)(2,1)} %pad_maximum_fusion.7), channel_id=1, source_target_pairs={{0,12},{4,0},{8,4},{12,8},{1,13},{5,1},{9,5},{13,9},{2,14},{6,2},{... | collective-permute-start | bytes 1572872 | tf_op jit(solution)/shard_map/ppermute | solution.py:565
  388.5 23.2 %all-to-all-start.2 = ((bf16[8,16,1920]{2,1,0:T(8,128)(2,1)}), bf16[8,16,1920]{2,1,0:T(8,128)(2,1)S(1)}, u32[]{:S(2)}, u32[]{:S(2)}) async-start(bf16[8,16,1920]{2,1,0:T(8,128)(2,1)} %bitcast.29.refs_1_), calls=%async_computation.3 | async-start | bytes 983040 | tf_op jit(solution)/shard_map/all_to_all | solution.py:789
  (112 other events, 966.0 us)
Sparse Core Ops, SparseCore 0:
  32.3 43.2 all-gather.2
  78.3 79.9 all-gather.4
  254.5 85.3 reduce-scatter.1

commit v6 on v5

--- a/solution.py
+++ b/solution.py
@@ -314,7 +314,7 @@
         out_specs=[WHOLE] * 2,
         out_shape=[jax.ShapeDtypeStruct((ROWS, 256), BF), jax.ShapeDtypeStruct((256, 2048), BF)],
         scratch_shapes=[pltpu.VMEM((ROWS, 2048), BF), pltpu.SemaphoreType.DMA((8,))],
-        compiler_params=params(60),
+        compiler_params=params(40),
         cost_estimate=takes(6),
         name="hidden_products",
     )(*pieces, att, w_out, *earlier)
@@ -589,8 +589,10 @@
     )(value, *earlier)
 
 
-def gather_pieces(block):
+def gather_pieces(block, *earlier):
     mine = [block, shift(block, 1), shift(block, -1), shift(block, 2)]
+    if earlier:
+        mine[1] = tie(mine[1], *earlier)
     return mine + [swap(piece) for piece in mine]
 
 
@@ -745,9 +747,9 @@
     sums = weight_grads(hat_two_pieces, grad_pieces, grad_gu, hid, to_left, to_right)
     sums = sums.reshape(16 * 192, 1536)
     grad_hidden_low = tie(grad_hidden.astype(BF), sums)
-    hidden_pieces = gather_pieces(grad_hidden_low)
+    ahead = scatter_first(ahead_mine, tie(ahead_other, grad_hidden_low))
+    hidden_pieces = gather_pieces(grad_hidden_low, ahead)
     sums = lax.psum_scatter(tie(sums, grad_hidden_low), REP, scatter_dimension=0, tiled=True)
-    ahead = scatter_first(ahead_mine, tie(ahead_other, hidden_pieces[0]))
     grad_att, sum_out = hidden_products(hidden_pieces, att, w_out, ahead)
 
     grad_q, grad_kv = attend_back(

time: 431 us -> 424 us (0.984)
  starting transfers between devices: 110 us -> 102 us
  waiting for transfers between devices: 114 us -> 119 us
    ppermute x20, starting transfers between devices: 41.9 us -> 34.4 us  [swap(): return lax.ppermute(block, 'c', [(0, 1), (1, 0)])]
    unnamed x174 -> x158, local copies, waits for them, and re-layouts: 16.8 us -> 12.8 us
  transfers between devices with their start and end apart: 58 -> 58, of which waited for: 18 -> 20; matrix products, arithmetic and copies ran while one was open for 10% -> 10% of each run, Pallas kernels for 19% -> 18%
where the time goes in v6:
time: 424 us; the launch traced here: 417 us
  waiting for transfers between devices  119 us (28%)
  Pallas kernels  112 us (26%)
  starting transfers between devices  102 us (24%)
  other arithmetic  37.6 us (9%)
  local copies, waits for them, and re-layouts  22 us (5%)
  between operations  16.9 us (4%)
  matrix products  8.46 us (2%)
    ppermute x28, waiting for transfers between devices, shift(): return lax.ppermute(block, 'x', [(i, (i + distance) % 4) for i in range(4)])  75 us
    ppermute x20, starting transfers between devices, swap(): return lax.ppermute(block, 'c', [(0, 1), (1, 0)])  34.4 us
    ppermute x28, starting transfers between devices, shift(): return lax.ppermute(block, 'x', [(i, (i + distance) % 4) for i in range(4)])  33.1 us
    pallas_call x1, Pallas kernels, feed_forward(): pl.pallas_call(feed_forward_kernel, grid=(2,), in_specs=[ANYWHERE] * 17,...  30.9 us
    pallas_call x2, Pallas kernels, attend(): pl.pallas_call(functools.partial(attend_kernel, first), grid=(ROWS // QB,...  20.4 us
    pallas_call x2, Pallas kernels, attend_back(): pl.pallas_call(functools.partial(attend_back_kernel, first), grid=(ROWS /...  20.1 us
    pallas_call x1, Pallas kernels, weight_grads(): pl.pallas_call(weight_grads_kernel, grid=(4,), in_specs=[pl.BlockSpec((12...  17.1 us
    all_gather x1, waiting for transfers between devices, body(): attn_all = lax.all_gather(attn_part, REP, axis=0, tiled=True)  14.8 us
  transfers between devices with their start and end apart: 58, of which 20 were waited for; matrix products, arithmetic and copies ran while one was open for 10% of the time, Pallas kernels for 18%

profile of v6, /device:TPU:17, one launch (start us, length us, event | category | flops | bytes accessed | tf_op | source)
XLA Modules:
  0.0 417.5 jit_solution(9573927340834382961)
XLA Ops:
  12.3 5.1 %all-to-all-start = ((bf16[8,16,1920]{2,1,0:T(8,128)(2,1)}), bf16[8,16,1920]{2,1,0:T(8,128)(2,1)S(1)}, u32[]{:S(2)}, u32[]{:S(2)}) async-start(bf16[8,16,1920]{2,1,0:T(8,128)(2,1)} %pack.1), calls=%async_computation | async-start | bytes 983040 | tf_op jit(solution)/shard_map/all_to_all | solution.py:701
  17.5 6.3 %collective-permute-start.7 = (bf16[16,2048]{1,0:T(8,128)(2,1)S(1)}, bf16[16,2048]{1,0:T(8,128)(2,1)S(1)}, u32[]{:S(2)}, u32[]{:S(2)}) collective-permute-start(bf16[16,2048]{1,0:T(8,128)(2,1)S(1)} %convert_element_type.166), channel_id=1, source_target_pairs={{0,0},{1,2},{2,16},{3,18},{4,32},{5,34},{6,48},{7,50},{8,64},{9,66... | collective-permute-start | bytes 196616 | tf_op jit(solution)/shard_map/ppermute | solution.py:703
  23.8 7.6 %collective-permute-done.7 = bf16[16,2048]{1,0:T(8,128)(2,1)S(1)} collective-permute-done((bf16[16,2048]{1,0:T(8,128)(2,1)S(1)}, bf16[16,2048]{1,0:T(8,128)(2,1)S(1)}, u32[]{:S(2)}, u32[]{:S(2)}) %collective-permute-start.7) | collective-permute-done | bytes 65568 | tf_op jit(solution)/shard_map/ppermute | solution.py:703
  36.4 10.6 %collective-permute-done.refs_1_.refs_2_ = bf16[128,2048]{1,0:T(8,128)(2,1)S(1)} collective-permute-done((bf16[128,2048]{1,0:T(8,128)(2,1)}, bf16[128,2048]{1,0:T(8,128)(2,1)S(1)}, u32[]{:S(2)}, u32[]{:S(2)}) %collective-permute-start) | collective-permute-done | bytes 524320 | tf_op jit(solution)/shard_map/ppermute | solution.py:565
  48.8 9.1 %collective-permute-done.2.refs_3_.refs_4_ = bf16[128,2048]{1,0:T(8,128)(2,1)S(1)} collective-permute-done((bf16[128,2048]{1,0:T(8,128)(2,1)}, bf16[128,2048]{1,0:T(8,128)(2,1)S(1)}, u32[]{:S(2)}, u32[]{:S(2)}) %collective-permute-start.2) | collective-permute-done | bytes 524320 | tf_op jit(solution)/shard_map/ppermute | solution.py:565
  60.8 14.8 %all-gather.3.cloned.1.call-done.refs_8_.refs_1_ = bf16[2048,640]{1,0:T(8,128)(2,1)} async-done(((bf16[128,640]{1,0:T(8,128)(2,1)}), bf16[2048,640]{1,0:T(8,128)(2,1)}) %all-gather.3.cloned.1.call-update) | async-done | bytes 2621456 | tf_op jit(solution)/shard_map/all_gather | solution.py:706
  84.6 6.9 %project.1 = (bf16[1024,256]{1,0:T(8,128)(2,1)}, bf16[1024,128]{1,0:T(8,128)(2,1)}, bf16[2048,384]{1,0:T(8,128)(2,1)}, bf16[256,2048]{1,0:T(8,128)(2,1)}) custom-call(bf16[128,2048]{1,0:T(8,128)(2,1)} %tie.11.refs_0_, bf16[128,2048]{1,0:T(8,128)(2,1)} %copy-done.37, bf16[128,2048]{1,0:T(8,128)(2,1)} %copy-done.38, bf16[128,2048]{1,0:T(8,128)(2,1)} %copy-done.39, ...), custom_call_target="tpu_custom_call" | custom-call | flops 5750000128 | bytes 1048576 | tf_op jit(solution)/shard_map/project/pallas_call | solution.py:276
  94.5 9.8 %attend.2 = (f32[256,1024]{1,0:T(8,128)S(1)}, f32[4,1024]{1,0:T(4,128)S(1)}, f32[4,1024]{1,0:T(4,128)S(1)}) custom-call(bf16[1024,256]{1,0:T(8,128)(2,1)S(1)} %copy-done.21, bf16[1024,128]{1,0:T(8,128)(2,1)S(1)} %copy-done.18, s32[1024,256]{1,0:T(8,128)S(1)} %broadcast_in_dim.17.kp_ref, s32[1,1024]{1,0:T(1,128)S(1)} %get-tuple-element.129.lo_ref, ...), custom_call_target="tpu_custom_call" | custom-call | flops 11500000256 | bytes 1048576 | tf_op jit(solution)/shard_map/attend/pallas_call | solution.py:151
  106.3 10.6 %attend.3 = (bf16[1024,256]{1,0:T(8,128)(2,1)S(1)}, bf16[1024,256]{1,0:T(8,128)(2,1)S(1)}, f32[4,1024]{1,0:T(4,128)S(1)}) custom-call(bf16[1024,256]{1,0:T(8,128)(2,1)S(1)} %copy-done.22, bf16[1024,128]{1,0:T(8,128)(2,1)S(1)} %collective-permute-done.8.kv_ref, s32[1024,256]{1,0:T(8,128)S(1)} %broadcast_in_dim.13.kp_ref, ...), custom_call_target="tpu_custom_call" | custom-call | flops 11500000256 | bytes 1048576 | tf_op jit(solution)/shard_map/attend/pallas_call | solution.py:151
  120.0 3.8 collective-permute-done.12
  126.5 5.8 %collective-permute-done.13 = bf16[64,2048]{1,0:T(8,128)(2,1)S(1)} collective-permute-done((bf16[64,2048]{1,0:T(8,128)(2,1)S(1)}, bf16[64,2048]{1,0:T(8,128)(2,1)S(1)}, u32[]{:S(2)}, u32[]{:S(2)}) %collective-permute-start.13) | collective-permute-done | bytes 262176 | tf_op jit(solution)/shard_map/ppermute | solution.py:565
  140.6 8.0 %collective-permute-done.16 = bf16[128,2048]{1,0:T(8,128)(2,1)S(1)} collective-permute-done((bf16[128,2048]{1,0:T(8,128)(2,1)S(1)}, bf16[128,2048]{1,0:T(8,128)(2,1)S(1)}, u32[]{:S(2)}, u32[]{:S(2)}) %collective-permute-start.16) | collective-permute-done | bytes 524320 | tf_op jit(solution)/shard_map/ppermute | solution.py:565
  156.3 5.3 %collective-permute-done.17.refs_1_ = bf16[128,2048]{1,0:T(8,128)(2,1)S(1)} collective-permute-done((bf16[128,2048]{1,0:T(8,128)(2,1)S(1)}, bf16[128,2048]{1,0:T(8,128)(2,1)S(1)}, u32[]{:S(2)}, u32[]{:S(2)}) %collective-permute-start.17) | collective-permute-done | bytes 524320 | tf_op jit(solution)/shard_map/ppermute | solution.py:565
  161.6 5.2 %collective-permute-start.21 = (bf16[128,2048]{1,0:T(8,128)(2,1)S(1)}, bf16[128,2048]{1,0:T(8,128)(2,1)S(1)}, u32[]{:S(2)}, u32[]{:S(2)}) collective-permute-start(bf16[128,2048]{1,0:T(8,128)(2,1)S(1)} %collective-permute-done.17.refs_1_), channel_id=1, source_target_pairs={{0,1},{1,0},{2,3},{3,2},{4,5},{5,4},{6,7},{7,6},{8,9},{9,8},{10,11... | collective-permute-start | bytes 1572872 | tf_op jit(solution)/shard_map/ppermute | solution.py:569
  166.8 8.5 %collective-permute-start.22 = (bf16[128,2048]{1,0:T(8,128)(2,1)S(1)}, bf16[128,2048]{1,0:T(8,128)(2,1)S(1)}, u32[]{:S(2)}, u32[]{:S(2)}) collective-permute-start(bf16[128,2048]{1,0:T(8,128)(2,1)S(1)} %collective-permute-done.18.refs_2_), channel_id=1, source_target_pairs={{0,1},{1,0},{2,3},{3,2},{4,5},{5,4},{6,7},{7,6},{8,9},{9,8},{10,11... | collective-permute-start | bytes 1572872 | tf_op jit(solution)/shard_map/ppermute | solution.py:569
  179.2 30.9 %feed_forward.1 = (bf16[1024,768]{1,0:T(8,128)(2,1)}, bf16[1024,1536]{1,0:T(8,128)(2,1)}, bf16[512,2048]{1,0:T(8,128)(2,1)}, bf16[512,2048]{1,0:T(8,128)(2,1)}, ...) custom-call(bf16[128,2048]{1,0:T(8,128)(2,1)} %copy-done.50, bf16[128,2048]{1,0:T(8,128)(2,1)} %copy-done.70, ...), custom_call_target="tpu_custom_call" | custom-call | flops 32199999488 | bytes 1048576 | tf_op jit(solution)/shard_map/feed_forward/pallas_call | solution.py:418
  210.7 4.1 collective-permute-done.28
  219.5 5.6 %collective-permute-done.29 = bf16[64,2048]{1,0:T(8,128)(2,1)S(1)} collective-permute-done((bf16[64,2048]{1,0:T(8,128)(2,1)S(1)}, bf16[64,2048]{1,0:T(8,128)(2,1)S(1)}, u32[]{:S(2)}, u32[]{:S(2)}) %collective-permute-start.29) | collective-permute-done | bytes 262176 | tf_op jit(solution)/shard_map/ppermute | solution.py:565
  232.4 17.1 %weight_grads.1 = bf16[16,192,1536]{2,1,0:T(8,128)(2,1)} custom-call(bf16[128,2048]{1,0:T(8,128)(2,1)} %copy-done.50, bf16[128,2048]{1,0:T(8,128)(2,1)} %copy-done.70, bf16[128,2048]{1,0:T(8,128)(2,1)} %copy-done.71, bf16[128,2048]{1,0:T(8,128)(2,1)} %copy-done.72, bf16[128,2048]{1,0:T(8,128)(2,1)} %copy-done.74, bf16[128,2048]{1,0:T(8,128)(2,1)} %copy-done.75, ...), custom_call_target="tpu_custom_call" | custom-call | flops 18975000576 | bytes 1048576 | tf_op jit(solution)/shard_map/weight_grads/pallas_call | solution.py:465
  260.2 4.6 %fusion.35 = (bf16[512,2048]{1,0:T(8,128)(2,1)S(1)}, f32[512,2048]{1,0:T(8,128)}) fusion(bf16[512,2048]{1,0:T(8,128)(2,1)S(1)} %collective-permute-done.33, bf16[512,2048]{1,0:T(8,128)(2,1)} %get-tuple-element.50), kind=kLoop, calls=%fused_computation.115 | loop fusion | flops 4194304 | bytes 10485760 | tf_op jit(solution)/shard_map/convert.15
  267.2 12.9 %collective-permute-done.38.refs_0_ = bf16[128,2048]{1,0:T(8,128)(2,1)S(1)} collective-permute-done((bf16[128,2048]{1,0:T(8,128)(2,1)S(1)}, bf16[128,2048]{1,0:T(8,128)(2,1)S(1)}, u32[]{:S(2)}, u32[]{:S(2)}) %collective-permute-start.38) | collective-permute-done | bytes 524320 | tf_op jit(solution)/shard_map/ppermute | solution.py:565
  280.0 4.4 %collective-permute-start.41 = (bf16[128,2048]{1,0:T(8,128)(2,1)S(1)}, bf16[128,2048]{1,0:T(8,128)(2,1)}, u32[]{:S(2)}, u32[]{:S(2)}) collective-permute-start(bf16[128,2048]{1,0:T(8,128)(2,1)S(1)} %copy-done.1), channel_id=1, source_target_pairs={{0,1},{1,0},{2,3},{3,2},{4,5},{5,4},{6,7},{7,6},{8,9},{9,8},{10,11... | collective-permute-start | bytes 1572872 | tf_op jit(solution)/shard_map/ppermute | solution.py:569
  291.5 3.7 collective-permute-start.35
  297.4 4.4 %hidden_products.1 = (bf16[1024,256]{1,0:T(8,128)(2,1)S(1)}, bf16[256,2048]{1,0:T(8,128)(2,1)S(1)}) custom-call(bf16[128,2048]{1,0:T(8,128)(2,1)S(1)} %copy-done.1, bf16[128,2048]{1,0:T(8,128)(2,1)S(1)} %copy-done.6, bf16[128,2048]{1,0:T(8,128)(2,1)} %collective-permute-done.39.refs_2_, bf16[128,2048]{1,0:T(8,128)(2,1)} %collective-permute-done.40.refs_3_, ...), custom_call_target="tpu_custom_call" | custom-call | flops 6899999744 | bytes 1048576 | tf_op jit(solution)/shard_map/hidden_products/pallas_call | solution.py:311
  302.8 9.7 %attend_back.2 = (f32[256,1024]{1,0:T(8,128)S(1)}, f32[1024,128]{1,0:T(8,128)S(1)}) custom-call(bf16[1024,256]{1,0:T(8,128)(2,1)S(1)} %copy-done.23, bf16[1024,256]{1,0:T(8,128)(2,1)S(1)} %get-tuple-element.56.do_ref, bf16[1024,256]{1,0:T(8,128)(2,1)S(1)} %copy-done.25, bf16[1024,128]{1,0:T(8,128)(2,1)S(1)} %collective-permute-done.8.kv_ref, ...), custom_call_target="tpu_custom_call" | custom-call | flops 11500000256 | bytes 1048576 | tf_op jit(solution)/shard_map/attend_back/pallas_call | solution.py:213
  313.1 10.3 %attend_back.3 = (bf16[1024,256]{1,0:T(8,128)(2,1)S(1)}, f32[1024,128]{1,0:T(8,128)S(1)}) custom-call(bf16[1024,256]{1,0:T(8,128)(2,1)S(1)} %copy-done.23, bf16[1024,256]{1,0:T(8,128)(2,1)S(1)} %get-tuple-element.56.do_ref, bf16[1024,256]{1,0:T(8,128)(2,1)S(1)} %copy-done.25, bf16[1024,128]{1,0:T(8,128)(2,1)S(1)} %copy-done.19, ...), custom_call_target="tpu_custom_call" | custom-call | flops 11500000256 | bytes 1048576 | tf_op jit(solution)/shard_map/attend_back/pallas_call | solution.py:213
  325.3 7.7 %attn_grads.1.refs_1_ = bf16[16,128,640]{2,1,0:T(8,128)(2,1)} custom-call(bf16[128,2048]{1,0:T(8,128)(2,1)} %tie.11.refs_0_, bf16[128,2048]{1,0:T(8,128)(2,1)} %copy-done.37, bf16[128,2048]{1,0:T(8,128)(2,1)} %copy-done.38, bf16[128,2048]{1,0:T(8,128)(2,1)} %copy-done.39, bf16[128,2048]{1,0:T(8,128)(2,1)} %copy-done.47, bf16[128,2048]{1,0:T(8,128)(2,1)} %copy-done.48, ...), custom_call_target="tpu_custom_call" | custom-call | flops 4600000000 | bytes 1048576 | tf_op jit(solution)/shard_map/attn_grads/pallas_call | solution.py:640
  338.8 6.7 %all-to-all-start.1 = ((bf16[16,128,640]{2,1,0:T(8,128)(2,1)}), bf16[16,128,640]{2,1,0:T(8,128)(2,1)S(1)}, u32[]{:S(2)}, u32[]{:S(2)}) async-start(bf16[16,128,640]{2,1,0:T(8,128)(2,1)} %attn_grads.1.refs_1_), calls=%async_computation.1 | async-start | bytes 5242880 | tf_op jit(solution)/shard_map/all_to_all | solution.py:780
  350.9 5.3 %collective-permute-done.47 = bf16[64,2048]{1,0:T(8,128)(2,1)S(1)} collective-permute-done((bf16[64,2048]{1,0:T(8,128)(2,1)S(1)}, bf16[64,2048]{1,0:T(8,128)(2,1)S(1)}, u32[]{:S(2)}, u32[]{:S(2)}) %collective-permute-start.47) | collective-permute-done | bytes 262176 | tf_op jit(solution)/shard_map/ppermute | solution.py:565
  367.0 12.1 %all-to-all-done.1 = bf16[16,128,640]{2,1,0:T(8,128)(2,1)S(1)} async-done(((bf16[16,128,640]{2,1,0:T(8,128)(2,1)}), bf16[16,128,640]{2,1,0:T(8,128)(2,1)S(1)}, u32[]{:S(2)}, u32[]{:S(2)}) %all-to-all-start.1) | async-done | bytes 2621472 | tf_op jit(solution)/shard_map/all_to_all | solution.py:780
  382.0 5.9 %all-to-all-start.2 = ((bf16[8,16,1920]{2,1,0:T(8,128)(2,1)}), bf16[8,16,1920]{2,1,0:T(8,128)(2,1)S(1)}, u32[]{:S(2)}, u32[]{:S(2)}) async-start(bf16[8,16,1920]{2,1,0:T(8,128)(2,1)} %bitcast.29.refs_1_), calls=%async_computation.3 | async-start | bytes 983040 | tf_op jit(solution)/shard_map/all_to_all | solution.py:791
  390.8 8.8 %collective-permute-start.51 = (bf16[16,2048]{1,0:T(8,128)(2,1)S(1)}, bf16[16,2048]{1,0:T(8,128)(2,1)S(1)}, u32[]{:S(2)}, u32[]{:S(2)}) collective-permute-start(bf16[16,2048]{1,0:T(8,128)(2,1)S(1)} %bitcast.73), channel_id=1, source_target_pairs={{0,0},{2,1},{16,2},{18,3},{32,4},{34,5},{48,6},{50,7},{64,8},{66,9... | collective-permute-start | bytes 196616 | tf_op jit(solution)/shard_map/ppermute | solution.py:803
  (364 shorter events, 129.2 us)
Async XLA Ops:
  12.3 19.0 %all-to-all-start = ((bf16[8,16,1920]{2,1,0:T(8,128)(2,1)}), bf16[8,16,1920]{2,1,0:T(8,128)(2,1)S(1)}, u32[]{:S(2)}, u32[]{:S(2)}) async-start(bf16[8,16,1920]{2,1,0:T(8,128)(2,1)} %pack.1), calls=%async_computation | async-start | bytes 983040 | tf_op jit(solution)/shard_map/all_to_all | solution.py:701
  17.4 58.1 %all-gather.3.cloned.1.call-start = ((), (), s32[]{:S(2)}) async-start(), calls=%async_computation.4 | async-start | bytes 2785280 | tf_op jit(solution)/shard_map/all_gather | solution.py:706
  17.5 13.9 %collective-permute-start.7 = (bf16[16,2048]{1,0:T(8,128)(2,1)S(1)}, bf16[16,2048]{1,0:T(8,128)(2,1)S(1)}, u32[]{:S(2)}, u32[]{:S(2)}) collective-permute-start(bf16[16,2048]{1,0:T(8,128)(2,1)S(1)} %convert_element_type.166), channel_id=1, source_target_pairs={{0,0},{1,2},{2,16},{3,18},{4,32},{5,34},{6,48},{7,50},{8,64},{9,66... | collective-permute-start | bytes 196616 | tf_op jit(solution)/shard_map/ppermute | solution.py:703
  32.1 147.1 %all-gather.5.cloned.1.call-start = ((), (), s32[]{:S(2)}) async-start(), calls=%async_computation.5 | async-start | bytes 10027008 | tf_op jit(solution)/shard_map/all_gather | solution.py:713
  34.4 14.3 %collective-permute-start.1 = (bf16[128,2048]{1,0:T(8,128)(2,1)}, bf16[128,2048]{1,0:T(8,128)(2,1)S(1)}, u32[]{:S(2)}, u32[]{:S(2)}) collective-permute-start(bf16[128,2048]{1,0:T(8,128)(2,1)} %tie.11.refs_0_), channel_id=1, source_target_pairs={{0,12},{4,0},{8,4},{12,8},{1,13},{5,1},{9,5},{13,9},{2,14},{6,2},{... | collective-permute-start | bytes 1572872 | tf_op jit(solution)/shard_map/ppermute | solution.py:565
  36.0 21.8 %collective-permute-start.2 = (bf16[128,2048]{1,0:T(8,128)(2,1)}, bf16[128,2048]{1,0:T(8,128)(2,1)S(1)}, u32[]{:S(2)}, u32[]{:S(2)}) collective-permute-start(bf16[128,2048]{1,0:T(8,128)(2,1)} %tie.11.refs_0_), channel_id=1, source_target_pairs={{0,8},{4,12},{8,0},{12,4},{1,9},{5,13},{9,1},{13,5},{2,10},{6,14},... | collective-permute-start | bytes 1572872 | tf_op jit(solution)/shard_map/ppermute | solution.py:565
  36.3 23.6 %collective-permute-start.3 = (bf16[128,2048]{1,0:T(8,128)(2,1)}, bf16[128,2048]{1,0:T(8,128)(2,1)S(1)}, u32[]{:S(2)}, u32[]{:S(2)}) collective-permute-start(bf16[128,2048]{1,0:T(8,128)(2,1)} %tie.11.refs_0_), channel_id=1, source_target_pairs={{0,1},{1,0},{2,3},{3,2},{4,5},{5,4},{6,7},{7,6},{8,9},{9,8},{10,11... | collective-permute-start | bytes 1572872 | tf_op jit(solution)/shard_map/ppermute | solution.py:569
  75.6 304.5 %reduce-scatter.2.cloned.1.call-start = ((), (), s32[]{:S(2)}) async-start(), calls=%async_computation.6 | async-start | bytes 10027008 | tf_op jit(solution)/shard_map/reduce_scatter | solution.py:752
  80.4 24.0 %collective-permute-start.9 = (bf16[128,2048]{1,0:T(8,128)(2,1)}, bf16[128,2048]{1,0:T(8,128)(2,1)S(1)}, u32[]{:S(2)}, u32[]{:S(2)}) collective-permute-start(bf16[128,2048]{1,0:T(8,128)(2,1)} %tie.12.refs_8_), channel_id=1, source_target_pairs={{0,4},{4,8},{8,12},{12,0},{1,5},{5,9},{9,13},{13,1},{2,6},{6,10},{... | collective-permute-start | bytes 1572872 | tf_op jit(solution)/shard_map/ppermute | solution.py:565
  81.6 22.8 %collective-permute-start.10 = (bf16[128,2048]{1,0:T(8,128)(2,1)}, bf16[128,2048]{1,0:T(8,128)(2,1)S(1)}, u32[]{:S(2)}, u32[]{:S(2)}) collective-permute-start(bf16[128,2048]{1,0:T(8,128)(2,1)} %tie.12.refs_8_), channel_id=1, source_target_pairs={{0,12},{4,0},{8,4},{12,8},{1,13},{5,1},{9,5},{13,9},{2,14},{6,2},{... | collective-permute-start | bytes 1572872 | tf_op jit(solution)/shard_map/ppermute | solution.py:565
  83.1 23.0 %collective-permute-start.11 = (bf16[128,2048]{1,0:T(8,128)(2,1)}, bf16[128,2048]{1,0:T(8,128)(2,1)S(1)}, u32[]{:S(2)}, u32[]{:S(2)}) collective-permute-start(bf16[128,2048]{1,0:T(8,128)(2,1)} %tie.12.refs_8_), channel_id=1, source_target_pairs={{0,8},{4,12},{8,0},{12,4},{1,9},{5,13},{9,1},{13,5},{2,10},{6,14},... | collective-permute-start | bytes 1572872 | tf_op jit(solution)/shard_map/ppermute | solution.py:565
  91.5 14.6 %collective-permute-start.8 = (bf16[1024,128]{1,0:T(8,128)(2,1)}, bf16[1024,128]{1,0:T(8,128)(2,1)S(1)}, u32[]{:S(2)}, u32[]{:S(2)}) collective-permute-start(bf16[1024,128]{1,0:T(8,128)(2,1)} %get-tuple-element.44.kv_ref), channel_id=1, source_target_pairs={{0,2},{2,0},{1,3},{3,1},{4,6},{6,4},{5,7},{7,5},{8,10},{10,8},{9,1... | collective-permute-start | bytes 786440 | tf_op jit(solution)/shard_map/ppermute | solution.py:728
  138.1 13.8 %collective-permute-start.24 = (bf16[128,2048]{1,0:T(8,128)(2,1)S(1)}, bf16[128,2048]{1,0:T(8,128)(2,1)S(1)}, u32[]{:S(2)}, u32[]{:S(2)}) collective-permute-start(bf16[128,2048]{1,0:T(8,128)(2,1)S(1)} %copy-done.42), channel_id=1, source_target_pairs={{0,1},{1,0},{2,3},{3,2},{4,5},{5,4},{6,7},{7,6},{8,9},{9,8},{10,11... | collective-permute-start | bytes 1572872 | tf_op jit(solution)/shard_map/ppermute | solution.py:569
  140.2 16.0 %collective-permute-start.26 = (bf16[128,2048]{1,0:T(8,128)(2,1)S(1)}, bf16[128,2048]{1,0:T(8,128)(2,1)S(1)}, u32[]{:S(2)}, u32[]{:S(2)}) collective-permute-start(bf16[128,2048]{1,0:T(8,128)(2,1)S(1)} %collective-permute-done.10.rest_4_.refs_10_), channel_id=1, source_target_pairs={{0,1},{1,0},{2,3},{3,2},{4,5},{5,4},{6,7},{7,6},{8,9},{9,8},{10,11... | collective-permute-start | bytes 1572872 | tf_op jit(solution)/shard_map/ppermute | solution.py:569
  149.3 17.6 %collective-permute-start.18 = (bf16[128,2048]{1,0:T(8,128)(2,1)S(1)}, bf16[128,2048]{1,0:T(8,128)(2,1)S(1)}, u32[]{:S(2)}, u32[]{:S(2)}) collective-permute-start(bf16[128,2048]{1,0:T(8,128)(2,1)S(1)} %multiply_convert_fusion.refs_0_), channel_id=1, source_target_pairs={{0,12},{4,0},{8,4},{12,8},{1,13},{5,1},{9,5},{13,9},{2,14},{6,2},{... | collective-permute-start | bytes 1572872 | tf_op jit(solution)/shard_map/ppermute | solution.py:565
  151.9 23.4 %collective-permute-start.19 = (bf16[128,2048]{1,0:T(8,128)(2,1)S(1)}, bf16[128,2048]{1,0:T(8,128)(2,1)S(1)}, u32[]{:S(2)}, u32[]{:S(2)}) collective-permute-start(bf16[128,2048]{1,0:T(8,128)(2,1)S(1)} %multiply_convert_fusion.refs_0_), channel_id=1, source_target_pairs={{0,8},{4,12},{8,0},{12,4},{1,9},{5,13},{9,1},{13,5},{2,10},{6,14},... | collective-permute-start | bytes 1572872 | tf_op jit(solution)/shard_map/ppermute | solution.py:565
  153.0 24.5 %collective-permute-start.27 = (bf16[128,2048]{1,0:T(8,128)(2,1)S(1)}, bf16[128,2048]{1,0:T(8,128)(2,1)S(1)}, u32[]{:S(2)}, u32[]{:S(2)}) collective-permute-start(bf16[128,2048]{1,0:T(8,128)(2,1)S(1)} %collective-permute-done.11.rest_5_.refs_11_), channel_id=1, source_target_pairs={{0,1},{1,0},{2,3},{3,2},{4,5},{5,4},{6,7},{7,6},{8,9},{9,8},{10,11... | collective-permute-start | bytes 1572872 | tf_op jit(solution)/shard_map/ppermute | solution.py:569
  156.2 21.3 %collective-permute-start.20 = (bf16[128,2048]{1,0:T(8,128)(2,1)S(1)}, bf16[128,2048]{1,0:T(8,128)(2,1)S(1)}, u32[]{:S(2)}, u32[]{:S(2)}) collective-permute-start(bf16[128,2048]{1,0:T(8,128)(2,1)S(1)} %multiply_convert_fusion.refs_0_), channel_id=1, source_target_pairs={{0,1},{1,0},{2,3},{3,2},{4,5},{5,4},{6,7},{7,6},{8,9},{9,8},{10,11... | collective-permute-start | bytes 1572872 | tf_op jit(solution)/shard_map/ppermute | solution.py:569
  161.6 15.9 %collective-permute-start.21 = (bf16[128,2048]{1,0:T(8,128)(2,1)S(1)}, bf16[128,2048]{1,0:T(8,128)(2,1)S(1)}, u32[]{:S(2)}, u32[]{:S(2)}) collective-permute-start(bf16[128,2048]{1,0:T(8,128)(2,1)S(1)} %collective-permute-done.17.refs_1_), channel_id=1, source_target_pairs={{0,1},{1,0},{2,3},{3,2},{4,5},{5,4},{6,7},{7,6},{8,9},{9,8},{10,11... | collective-permute-start | bytes 1572872 | tf_op jit(solution)/shard_map/ppermute | solution.py:569
  228.9 20.7 %collective-permute-start.32 = (bf16[128,2048]{1,0:T(8,128)(2,1)}, bf16[128,2048]{1,0:T(8,128)(2,1)}, u32[]{:S(2)}, u32[]{:S(2)}) collective-permute-start(bf16[128,2048]{1,0:T(8,128)(2,1)} %pad_maximum_fusion.4.refs_19_), channel_id=1, source_target_pairs={{0,4},{4,8},{8,12},{12,0},{1,5},{5,9},{9,13},{13,1},{2,6},{6,10},{... | collective-permute-start | bytes 1572872 | tf_op jit(solution)/shard_map/ppermute | solution.py:565
  229.8 19.8 %collective-permute-start.30 = (bf16[128,2048]{1,0:T(8,128)(2,1)}, bf16[128,2048]{1,0:T(8,128)(2,1)}, u32[]{:S(2)}, u32[]{:S(2)}) collective-permute-start(bf16[128,2048]{1,0:T(8,128)(2,1)} %pad_maximum_fusion.3.refs_18_), channel_id=1, source_target_pairs={{0,12},{4,0},{8,4},{12,8},{1,13},{5,1},{9,5},{13,9},{2,14},{6,2},{... | collective-permute-start | bytes 1572872 | tf_op jit(solution)/shard_map/ppermute | solution.py:565
  256.2 23.9 %collective-permute-start.38 = (bf16[128,2048]{1,0:T(8,128)(2,1)S(1)}, bf16[128,2048]{1,0:T(8,128)(2,1)S(1)}, u32[]{:S(2)}, u32[]{:S(2)}) collective-permute-start(bf16[128,2048]{1,0:T(8,128)(2,1)S(1)} %copy-done.1), channel_id=1, source_target_pairs={{0,4},{4,8},{8,12},{12,0},{1,5},{5,9},{9,13},{13,1},{2,6},{6,10},{... | collective-permute-start | bytes 1572872 | tf_op jit(solution)/shard_map/ppermute | solution.py:565
  256.2 28.2 %collective-permute-start.39 = (bf16[128,2048]{1,0:T(8,128)(2,1)S(1)}, bf16[128,2048]{1,0:T(8,128)(2,1)}, u32[]{:S(2)}, u32[]{:S(2)}) collective-permute-start(bf16[128,2048]{1,0:T(8,128)(2,1)S(1)} %copy-done.1), channel_id=1, source_target_pairs={{0,12},{4,0},{8,4},{12,8},{1,13},{5,1},{9,5},{13,9},{2,14},{6,2},{... | collective-permute-start | bytes 1572872 | tf_op jit(solution)/shard_map/ppermute | solution.py:565
  258.8 25.7 %collective-permute-start.40 = (bf16[128,2048]{1,0:T(8,128)(2,1)S(1)}, bf16[128,2048]{1,0:T(8,128)(2,1)}, u32[]{:S(2)}, u32[]{:S(2)}) collective-permute-start(bf16[128,2048]{1,0:T(8,128)(2,1)S(1)} %copy-done.1), channel_id=1, source_target_pairs={{0,8},{4,12},{8,0},{12,4},{1,9},{5,13},{9,1},{13,5},{2,10},{6,14},... | collective-permute-start | bytes 1572872 | tf_op jit(solution)/shard_map/ppermute | solution.py:565
  265.7 20.1 %collective-permute-start.34 = (bf16[64,2048]{1,0:T(8,128)(2,1)}, bf16[64,2048]{1,0:T(8,128)(2,1)}, u32[]{:S(2)}, u32[]{:S(2)}) collective-permute-start(bf16[64,2048]{1,0:T(8,128)(2,1)} %get-tuple-element.103), channel_id=1, source_target_pairs={{0,12},{4,0},{8,4},{12,8},{1,13},{5,1},{9,5},{13,9},{2,14},{6,2},{... | collective-permute-start | bytes 786440 | tf_op jit(solution)/shard_map/ppermute | solution.py:565
  265.7 22.2 %collective-permute-start.36 = (bf16[64,2048]{1,0:T(8,128)(2,1)}, bf16[64,2048]{1,0:T(8,128)(2,1)}, u32[]{:S(2)}, u32[]{:S(2)}) collective-permute-start(bf16[64,2048]{1,0:T(8,128)(2,1)} %get-tuple-element.104), channel_id=1, source_target_pairs={{0,4},{4,8},{8,12},{12,0},{1,5},{5,9},{9,13},{13,1},{2,6},{6,10},{... | collective-permute-start | bytes 786440 | tf_op jit(solution)/shard_map/ppermute | solution.py:565
  290.4 34.1 %collective-permute-start.37 = (bf16[128,2048]{1,0:T(8,128)(2,1)S(1)}, bf16[128,2048]{1,0:T(8,128)(2,1)S(1)}, u32[]{:S(2)}, u32[]{:S(2)}) collective-permute-start(bf16[128,2048]{1,0:T(8,128)(2,1)S(1)} %pad_maximum_fusion.6.rest_2_), channel_id=1, source_target_pairs={{0,4},{4,8},{8,12},{12,0},{1,5},{5,9},{9,13},{13,1},{2,6},{6,10},{... | collective-permute-start | bytes 1572872 | tf_op jit(solution)/shard_map/ppermute | solution.py:565
  291.5 33.0 %collective-permute-start.35 = (bf16[128,2048]{1,0:T(8,128)(2,1)S(1)}, bf16[128,2048]{1,0:T(8,128)(2,1)}, u32[]{:S(2)}, u32[]{:S(2)}) collective-permute-start(bf16[128,2048]{1,0:T(8,128)(2,1)S(1)} %pad_maximum_fusion.5.rest_1_), channel_id=1, source_target_pairs={{0,12},{4,0},{8,4},{12,8},{1,13},{5,1},{9,5},{13,9},{2,14},{6,2},{... | collective-permute-start | bytes 1572872 | tf_op jit(solution)/shard_map/ppermute | solution.py:565
  338.8 40.3 %all-to-all-start.1 = ((bf16[16,128,640]{2,1,0:T(8,128)(2,1)}), bf16[16,128,640]{2,1,0:T(8,128)(2,1)S(1)}, u32[]{:S(2)}, u32[]{:S(2)}) async-start(bf16[16,128,640]{2,1,0:T(8,128)(2,1)} %attn_grads.1.refs_1_), calls=%async_computation.1 | async-start | bytes 5242880 | tf_op jit(solution)/shard_map/all_to_all | solution.py:780
  359.8 28.1 %collective-permute-start.50 = (bf16[128,2048]{1,0:T(8,128)(2,1)}, bf16[128,2048]{1,0:T(8,128)(2,1)}, u32[]{:S(2)}, u32[]{:S(2)}) collective-permute-start(bf16[128,2048]{1,0:T(8,128)(2,1)} %pad_maximum_fusion.8), channel_id=1, source_target_pairs={{0,4},{4,8},{8,12},{12,0},{1,5},{5,9},{9,13},{13,1},{2,6},{6,10},{... | collective-permute-start | bytes 1572872 | tf_op jit(solution)/shard_map/ppermute | solution.py:565
  360.6 27.3 %collective-permute-start.48 = (bf16[128,2048]{1,0:T(8,128)(2,1)}, bf16[128,2048]{1,0:T(8,128)(2,1)}, u32[]{:S(2)}, u32[]{:S(2)}) collective-permute-start(bf16[128,2048]{1,0:T(8,128)(2,1)} %pad_maximum_fusion.7), channel_id=1, source_target_pairs={{0,12},{4,0},{8,4},{12,8},{1,13},{5,1},{9,5},{13,9},{2,14},{6,2},{... | collective-permute-start | bytes 1572872 | tf_op jit(solution)/shard_map/ppermute | solution.py:565
  382.0 23.1 %all-to-all-start.2 = ((bf16[8,16,1920]{2,1,0:T(8,128)(2,1)}), bf16[8,16,1920]{2,1,0:T(8,128)(2,1)S(1)}, u32[]{:S(2)}, u32[]{:S(2)}) async-start(bf16[8,16,1920]{2,1,0:T(8,128)(2,1)} %bitcast.29.refs_1_), calls=%async_computation.3 | async-start | bytes 983040 | tf_op jit(solution)/shard_map/all_to_all | solution.py:791
  (104 other events, 975.0 us)
Sparse Core Ops, SparseCore 0:
  32.3 43.2 all-gather.2
  78.3 80.0 all-gather.4
  254.2 85.5 reduce-scatter.1

commit v7 on v6

--- a/solution.py
+++ b/solution.py
@@ -66,7 +66,7 @@
     return lax.dot_general(a, b, (((0,), (0,)), ((), ())), preferred_element_type=F32)
 
 
-QB = 256
+QB = 512
 
 
 def takes(microseconds):
@@ -88,7 +88,7 @@
 
 
 def natural_rows(block, piece):
-    first = (block % 2) * 512 + (block // 2) * 64 + 128 * piece
+    first = block * 64 + 128 * piece
     return pl.ds(pl.multiple_of(first, 64), 64)
 
 
@@ -128,14 +128,14 @@
                 out = out * jnp.where(high >= 0, 1.0 / total, 0.0)
                 out = out.T.astype(BF)
                 o_ref[:, cols] = out
-                for piece in range(4):
+                for piece in range(8):
                     natural_ref[natural_rows(pl.program_id(0), piece), cols] = out[
                         64 * piece : 64 * piece + 64
                     ]
                 lse_ref[row, :] = peak + jnp.log(total)
 
-    pl.when(pl.program_id(0) < 2)(lambda: over(ROWS // 2))
-    pl.when(pl.program_id(0) >= 2)(lambda: over(ROWS))
+    pl.when(pl.program_id(0) < 1)(lambda: over(ROWS // 2))
+    pl.when(pl.program_id(0) >= 1)(lambda: over(ROWS))
 
 
 def attend(q, kv, kp, lo, hi, before, *earlier):
@@ -194,13 +194,13 @@
                 dq_ref[cols, :] = dq
             else:
                 dq = (dq + rest[0][cols, :]).T.astype(BF)
-                for piece in range(4):
+                for piece in range(8):
                     dq_ref[natural_rows(pl.program_id(0), piece), cols] = dq[
                         64 * piece : 64 * piece + 64
                     ]
 
-    pl.when(pl.program_id(0) < 2)(lambda: over(ROWS // 2))
-    pl.when(pl.program_id(0) >= 2)(lambda: over(ROWS))
+    pl.when(pl.program_id(0) < 1)(lambda: over(ROWS // 2))
+    pl.when(pl.program_id(0) >= 1)(lambda: over(ROWS))
 
 
 def attend_back(q, do, o, kv, kp, lo, hi, lse, earlier_dq, *earlier):
@@ -302,9 +302,10 @@
             here = 128 * piece + 64 * late
             there = 512 * late + 64 * piece
             grad_att_ref[there : there + 64, :] = grad_att[here : here + 64]
+    turned = att_ref[...].T
     for k in range(4):
         cols = slice(512 * k, 512 * k + 512)
-        sum_ref[:, cols] = dot_tn(att_ref[...], grad[:, cols]).astype(BF)
+        sum_ref[:, cols] = dot_nn(turned, grad[:, cols]).astype(BF)
 
 
 def hidden_products(pieces, att, w_out, *earlier):

time: 424 us -> 419 us (0.988)
  Pallas kernels: 112 us -> 105 us
    pallas_call x2, Pallas kernels: 20.4 us -> 14.5 us  [attend(): pl.pallas_call(functools.partial(attend_kernel, first), grid=(ROWS // QB,...]
  transfers between devices with their start and end apart: 58 -> 58, of which waited for: 20 -> 20; matrix products, arithmetic and copies ran while one was open for 10% -> 11% of each run, Pallas kernels for 18% -> 17%
where the time goes in v7:
time: 419 us; the launch traced here: 412 us
  waiting for transfers between devices  123 us (29%)
  Pallas kernels  105 us (25%)
  starting transfers between devices  102 us (24%)
  other arithmetic  37.3 us (9%)
  local copies, waits for them, and re-layouts  19 us (5%)
  between operations  16.6 us (4%)
  matrix products  8.48 us (2%)
    ppermute x28, waiting for transfers between devices, shift(): return lax.ppermute(block, 'x', [(i, (i + distance) % 4) for i in range(4)])  79.1 us
    ppermute x20, starting transfers between devices, swap(): return lax.ppermute(block, 'c', [(0, 1), (1, 0)])  34.1 us
    ppermute x28, starting transfers between devices, shift(): return lax.ppermute(block, 'x', [(i, (i + distance) % 4) for i in range(4)])  33.3 us
    pallas_call x1, Pallas kernels, feed_forward(): pl.pallas_call(feed_forward_kernel, grid=(2,), in_specs=[ANYWHERE] * 17,...  31.1 us
    pallas_call x2, Pallas kernels, attend_back(): pl.pallas_call(functools.partial(attend_back_kernel, first), grid=(ROWS /...  18.9 us
    pallas_call x1, Pallas kernels, weight_grads(): pl.pallas_call(weight_grads_kernel, grid=(4,), in_specs=[pl.BlockSpec((12...  17.1 us
    all_gather x1, waiting for transfers between devices, body(): attn_all = lax.all_gather(attn_part, REP, axis=0, tiled=True)  14.8 us
    pallas_call x2, Pallas kernels, attend(): pl.pallas_call(functools.partial(attend_kernel, first), grid=(ROWS // QB,...  14.5 us
  transfers between devices with their start and end apart: 58, of which 20 were waited for; matrix products, arithmetic and copies ran while one was open for 11% of the time, Pallas kernels for 17%

profile of v7, /device:TPU:17, one launch (start us, length us, event | category | flops | bytes accessed | tf_op | source)
XLA Modules:
  0.0 412.3 jit_solution(4849361713514829545)
XLA Ops:
  12.3 5.1 %all-to-all-start = ((bf16[8,16,1920]{2,1,0:T(8,128)(2,1)}), bf16[8,16,1920]{2,1,0:T(8,128)(2,1)S(1)}, u32[]{:S(2)}, u32[]{:S(2)}) async-start(bf16[8,16,1920]{2,1,0:T(8,128)(2,1)} %pack.1), calls=%async_computation | async-start | bytes 983040 | tf_op jit(solution)/shard_map/all_to_all | solution.py:702
  17.5 6.3 %collective-permute-start.7 = (bf16[16,2048]{1,0:T(8,128)(2,1)S(1)}, bf16[16,2048]{1,0:T(8,128)(2,1)S(1)}, u32[]{:S(2)}, u32[]{:S(2)}) collective-permute-start(bf16[16,2048]{1,0:T(8,128)(2,1)S(1)} %convert_element_type.166), channel_id=1, source_target_pairs={{0,0},{1,2},{2,16},{3,18},{4,32},{5,34},{6,48},{7,50},{8,64},{9,66... | collective-permute-start | bytes 196616 | tf_op jit(solution)/shard_map/ppermute | solution.py:704
  23.8 7.6 %collective-permute-done.7 = bf16[16,2048]{1,0:T(8,128)(2,1)S(1)} collective-permute-done((bf16[16,2048]{1,0:T(8,128)(2,1)S(1)}, bf16[16,2048]{1,0:T(8,128)(2,1)S(1)}, u32[]{:S(2)}, u32[]{:S(2)}) %collective-permute-start.7) | collective-permute-done | bytes 65568 | tf_op jit(solution)/shard_map/ppermute | solution.py:704
  36.4 10.6 %collective-permute-done.refs_1_.refs_2_ = bf16[128,2048]{1,0:T(8,128)(2,1)S(1)} collective-permute-done((bf16[128,2048]{1,0:T(8,128)(2,1)}, bf16[128,2048]{1,0:T(8,128)(2,1)S(1)}, u32[]{:S(2)}, u32[]{:S(2)}) %collective-permute-start) | collective-permute-done | bytes 524320 | tf_op jit(solution)/shard_map/ppermute | solution.py:566
  48.8 9.1 %collective-permute-done.2.refs_3_.refs_4_ = bf16[128,2048]{1,0:T(8,128)(2,1)S(1)} collective-permute-done((bf16[128,2048]{1,0:T(8,128)(2,1)}, bf16[128,2048]{1,0:T(8,128)(2,1)S(1)}, u32[]{:S(2)}, u32[]{:S(2)}) %collective-permute-start.2) | collective-permute-done | bytes 524320 | tf_op jit(solution)/shard_map/ppermute | solution.py:566
  60.8 14.8 %all-gather.3.cloned.1.call-done.refs_8_.refs_1_ = bf16[2048,640]{1,0:T(8,128)(2,1)} async-done(((bf16[128,640]{1,0:T(8,128)(2,1)}), bf16[2048,640]{1,0:T(8,128)(2,1)}) %all-gather.3.cloned.1.call-update) | async-done | bytes 2621456 | tf_op jit(solution)/shard_map/all_gather | solution.py:707
  84.6 6.9 %project.1 = (bf16[1024,256]{1,0:T(8,128)(2,1)}, bf16[1024,128]{1,0:T(8,128)(2,1)}, bf16[2048,384]{1,0:T(8,128)(2,1)}, bf16[256,2048]{1,0:T(8,128)(2,1)}) custom-call(bf16[128,2048]{1,0:T(8,128)(2,1)} %tie.11.refs_0_, bf16[128,2048]{1,0:T(8,128)(2,1)} %copy-done.37, bf16[128,2048]{1,0:T(8,128)(2,1)} %copy-done.38, bf16[128,2048]{1,0:T(8,128)(2,1)} %copy-done.39, ...), custom_call_target="tpu_custom_call" | custom-call | flops 5750000128 | bytes 1048576 | tf_op jit(solution)/shard_map/project/pallas_call | solution.py:276
  92.9 6.9 %attend.2 = (f32[256,1024]{1,0:T(8,128)S(1)}, f32[4,1024]{1,0:T(4,128)S(1)}, f32[4,1024]{1,0:T(4,128)S(1)}) custom-call(bf16[1024,256]{1,0:T(8,128)(2,1)S(1)} %copy-done.22, bf16[1024,128]{1,0:T(8,128)(2,1)S(1)} %copy-done.18, s32[1024,512]{1,0:T(8,128)S(1)} %broadcast_in_dim.17.kp_ref, s32[1,1024]{1,0:T(1,128)S(1)} %get-tuple-element.129.lo_ref, ...), custom_call_target="tpu_custom_call" | custom-call | flops 11500000256 | bytes 1048576 | tf_op jit(solution)/shard_map/attend/pallas_call | solution.py:151
  99.8 6.3 %collective-permute-done.11.rest_5_.refs_11_ = bf16[128,2048]{1,0:T(8,128)(2,1)S(1)} collective-permute-done((bf16[128,2048]{1,0:T(8,128)(2,1)}, bf16[128,2048]{1,0:T(8,128)(2,1)S(1)}, u32[]{:S(2)}, u32[]{:S(2)}) %collective-permute-start.11) | collective-permute-done | bytes 524320 | tf_op jit(solution)/shard_map/ppermute | solution.py:566
  106.3 7.6 %attend.3 = (bf16[1024,256]{1,0:T(8,128)(2,1)S(1)}, bf16[1024,256]{1,0:T(8,128)(2,1)S(1)}, f32[4,1024]{1,0:T(4,128)S(1)}) custom-call(bf16[1024,256]{1,0:T(8,128)(2,1)S(1)} %copy-done.22, bf16[1024,128]{1,0:T(8,128)(2,1)S(1)} %collective-permute-done.8.kv_ref, s32[1024,512]{1,0:T(8,128)S(1)} %broadcast_in_dim.13.kp_ref, ...), custom_call_target="tpu_custom_call" | custom-call | flops 11500000256 | bytes 1048576 | tf_op jit(solution)/shard_map/attend/pallas_call | solution.py:151
  117.0 3.8 collective-permute-done.12
  123.5 5.8 %collective-permute-done.13 = bf16[64,2048]{1,0:T(8,128)(2,1)S(1)} collective-permute-done((bf16[64,2048]{1,0:T(8,128)(2,1)S(1)}, bf16[64,2048]{1,0:T(8,128)(2,1)S(1)}, u32[]{:S(2)}, u32[]{:S(2)}) %collective-permute-start.13) | collective-permute-done | bytes 262176 | tf_op jit(solution)/shard_map/ppermute | solution.py:566
  137.6 8.0 %collective-permute-done.16 = bf16[128,2048]{1,0:T(8,128)(2,1)S(1)} collective-permute-done((bf16[128,2048]{1,0:T(8,128)(2,1)S(1)}, bf16[128,2048]{1,0:T(8,128)(2,1)S(1)}, u32[]{:S(2)}, u32[]{:S(2)}) %collective-permute-start.16) | collective-permute-done | bytes 524320 | tf_op jit(solution)/shard_map/ppermute | solution.py:566
  153.7 4.9 %collective-permute-done.17.refs_1_ = bf16[128,2048]{1,0:T(8,128)(2,1)S(1)} collective-permute-done((bf16[128,2048]{1,0:T(8,128)(2,1)S(1)}, bf16[128,2048]{1,0:T(8,128)(2,1)S(1)}, u32[]{:S(2)}, u32[]{:S(2)}) %collective-permute-start.17) | collective-permute-done | bytes 524320 | tf_op jit(solution)/shard_map/ppermute | solution.py:566
  158.7 5.2 %collective-permute-start.21 = (bf16[128,2048]{1,0:T(8,128)(2,1)S(1)}, bf16[128,2048]{1,0:T(8,128)(2,1)S(1)}, u32[]{:S(2)}, u32[]{:S(2)}) collective-permute-start(bf16[128,2048]{1,0:T(8,128)(2,1)S(1)} %collective-permute-done.17.refs_1_), channel_id=1, source_target_pairs={{0,1},{1,0},{2,3},{3,2},{4,5},{5,4},{6,7},{7,6},{8,9},{9,8},{10,11... | collective-permute-start | bytes 1572872 | tf_op jit(solution)/shard_map/ppermute | solution.py:570
  163.8 8.5 %collective-permute-start.22 = (bf16[128,2048]{1,0:T(8,128)(2,1)S(1)}, bf16[128,2048]{1,0:T(8,128)(2,1)S(1)}, u32[]{:S(2)}, u32[]{:S(2)}) collective-permute-start(bf16[128,2048]{1,0:T(8,128)(2,1)S(1)} %collective-permute-done.18.refs_2_), channel_id=1, source_target_pairs={{0,1},{1,0},{2,3},{3,2},{4,5},{5,4},{6,7},{7,6},{8,9},{9,8},{10,11... | collective-permute-start | bytes 1572872 | tf_op jit(solution)/shard_map/ppermute | solution.py:570
  175.8 31.1 %feed_forward.1 = (bf16[1024,768]{1,0:T(8,128)(2,1)}, bf16[1024,1536]{1,0:T(8,128)(2,1)}, bf16[512,2048]{1,0:T(8,128)(2,1)}, bf16[512,2048]{1,0:T(8,128)(2,1)}, ...) custom-call(bf16[128,2048]{1,0:T(8,128)(2,1)} %copy-done.50, bf16[128,2048]{1,0:T(8,128)(2,1)} %copy-done.70, ...), custom_call_target="tpu_custom_call" | custom-call | flops 32199999488 | bytes 1048576 | tf_op jit(solution)/shard_map/feed_forward/pallas_call | solution.py:419
  207.4 4.1 collective-permute-done.28
  216.6 5.3 %collective-permute-done.29 = bf16[64,2048]{1,0:T(8,128)(2,1)S(1)} collective-permute-done((bf16[64,2048]{1,0:T(8,128)(2,1)S(1)}, bf16[64,2048]{1,0:T(8,128)(2,1)S(1)}, u32[]{:S(2)}, u32[]{:S(2)}) %collective-permute-start.29) | collective-permute-done | bytes 262176 | tf_op jit(solution)/shard_map/ppermute | solution.py:566
  229.5 17.1 %weight_grads.1 = bf16[16,192,1536]{2,1,0:T(8,128)(2,1)} custom-call(bf16[128,2048]{1,0:T(8,128)(2,1)} %copy-done.50, bf16[128,2048]{1,0:T(8,128)(2,1)} %copy-done.70, bf16[128,2048]{1,0:T(8,128)(2,1)} %copy-done.71, bf16[128,2048]{1,0:T(8,128)(2,1)} %copy-done.72, bf16[128,2048]{1,0:T(8,128)(2,1)} %copy-done.74, bf16[128,2048]{1,0:T(8,128)(2,1)} %copy-done.75, ...), custom_call_target="tpu_custom_call" | custom-call | flops 18975000576 | bytes 1048576 | tf_op jit(solution)/shard_map/weight_grads/pallas_call | solution.py:466
  257.0 4.6 %fusion.35 = (bf16[512,2048]{1,0:T(8,128)(2,1)S(1)}, f32[512,2048]{1,0:T(8,128)}) fusion(bf16[512,2048]{1,0:T(8,128)(2,1)S(1)} %collective-permute-done.33, bf16[512,2048]{1,0:T(8,128)(2,1)} %get-tuple-element.50), kind=kLoop, calls=%fused_computation.115 | loop fusion | flops 4194304 | bytes 10485760 | tf_op jit(solution)/shard_map/convert.15
  264.0 12.8 %collective-permute-done.38.refs_0_ = bf16[128,2048]{1,0:T(8,128)(2,1)S(1)} collective-permute-done((bf16[128,2048]{1,0:T(8,128)(2,1)S(1)}, bf16[128,2048]{1,0:T(8,128)(2,1)S(1)}, u32[]{:S(2)}, u32[]{:S(2)}) %collective-permute-start.38) | collective-permute-done | bytes 524320 | tf_op jit(solution)/shard_map/ppermute | solution.py:566
  276.8 4.4 %collective-permute-start.41 = (bf16[128,2048]{1,0:T(8,128)(2,1)S(1)}, bf16[128,2048]{1,0:T(8,128)(2,1)}, u32[]{:S(2)}, u32[]{:S(2)}) collective-permute-start(bf16[128,2048]{1,0:T(8,128)(2,1)S(1)} %copy-done.1), channel_id=1, source_target_pairs={{0,1},{1,0},{2,3},{3,2},{4,5},{5,4},{6,7},{7,6},{8,9},{9,8},{10,11... | collective-permute-start | bytes 1572872 | tf_op jit(solution)/shard_map/ppermute | solution.py:570
  293.1 4.3 %hidden_products.1 = (bf16[1024,256]{1,0:T(8,128)(2,1)S(1)}, bf16[256,2048]{1,0:T(8,128)(2,1)S(1)}) custom-call(bf16[128,2048]{1,0:T(8,128)(2,1)S(1)} %copy-done.1, bf16[128,2048]{1,0:T(8,128)(2,1)S(1)} %copy-done.8, bf16[128,2048]{1,0:T(8,128)(2,1)S(1)} %collective-permute-done.39.refs_2_, bf16[128,2048]{1,0:T(8,128)(2,1)} %collective-permute-done.40.refs_3_, ...), custom_call_target="tpu_custom_call" | custom-call | flops 6899999744 | bytes 1048576 | tf_op jit(solution)/shard_map/hidden_products/pallas_call | solution.py:312
  298.4 9.2 %attend_back.2 = (f32[256,1024]{1,0:T(8,128)S(1)}, f32[1024,128]{1,0:T(8,128)S(1)}) custom-call(bf16[1024,256]{1,0:T(8,128)(2,1)S(1)} %copy-done.23, bf16[1024,256]{1,0:T(8,128)(2,1)S(1)} %get-tuple-element.56.do_ref, bf16[1024,256]{1,0:T(8,128)(2,1)S(1)} %copy-done.25, bf16[1024,128]{1,0:T(8,128)(2,1)S(1)} %copy-done.20, s32[1024,512]{1,0:T(8,128)S(1)} %copy-done.6, ...), custom_call_target="tpu_custom_call" | custom-call | flops 11500000256 | bytes 1048576 | tf_op jit(solution)/shard_map/attend_back/pallas_call | solution.py:213
  308.3 9.8 %attend_back.3 = (bf16[1024,256]{1,0:T(8,128)(2,1)S(1)}, f32[1024,128]{1,0:T(8,128)S(1)}) custom-call(bf16[1024,256]{1,0:T(8,128)(2,1)S(1)} %copy-done.23, bf16[1024,256]{1,0:T(8,128)(2,1)S(1)} %get-tuple-element.56.do_ref, bf16[1024,256]{1,0:T(8,128)(2,1)S(1)} %copy-done.25, bf16[1024,128]{1,0:T(8,128)(2,1)S(1)} %copy-done.18, s32[1024,512]{1,0:T(8,128)S(1)} %copy-done.4, ...), custom_call_target="tpu_custom_call" | custom-call | flops 11500000256 | bytes 1048576 | tf_op jit(solution)/shard_map/attend_back/pallas_call | solution.py:213
  320.0 8.0 %attn_grads.1.refs_1_ = bf16[16,128,640]{2,1,0:T(8,128)(2,1)} custom-call(bf16[128,2048]{1,0:T(8,128)(2,1)} %tie.11.refs_0_, bf16[128,2048]{1,0:T(8,128)(2,1)} %copy-done.37, bf16[128,2048]{1,0:T(8,128)(2,1)} %copy-done.38, bf16[128,2048]{1,0:T(8,128)(2,1)} %copy-done.39, bf16[128,2048]{1,0:T(8,128)(2,1)} %copy-done.47, bf16[128,2048]{1,0:T(8,128)(2,1)} %copy-done.48, ...), custom_call_target="tpu_custom_call" | custom-call | flops 4600000000 | bytes 1048576 | tf_op jit(solution)/shard_map/attn_grads/pallas_call | solution.py:641
  333.9 6.7 %all-to-all-start.1 = ((bf16[16,128,640]{2,1,0:T(8,128)(2,1)}), bf16[16,128,640]{2,1,0:T(8,128)(2,1)S(1)}, u32[]{:S(2)}, u32[]{:S(2)}) async-start(bf16[16,128,640]{2,1,0:T(8,128)(2,1)} %attn_grads.1.refs_1_), calls=%async_computation.1 | async-start | bytes 5242880 | tf_op jit(solution)/shard_map/all_to_all | solution.py:781
  345.7 5.6 %collective-permute-done.47 = bf16[64,2048]{1,0:T(8,128)(2,1)S(1)} collective-permute-done((bf16[64,2048]{1,0:T(8,128)(2,1)S(1)}, bf16[64,2048]{1,0:T(8,128)(2,1)S(1)}, u32[]{:S(2)}, u32[]{:S(2)}) %collective-permute-start.47) | collective-permute-done | bytes 262176 | tf_op jit(solution)/shard_map/ppermute | solution.py:566
  361.4 12.8 %all-to-all-done.1 = bf16[16,128,640]{2,1,0:T(8,128)(2,1)S(1)} async-done(((bf16[16,128,640]{2,1,0:T(8,128)(2,1)}), bf16[16,128,640]{2,1,0:T(8,128)(2,1)S(1)}, u32[]{:S(2)}, u32[]{:S(2)}) %all-to-all-start.1) | async-done | bytes 2621472 | tf_op jit(solution)/shard_map/all_to_all | solution.py:781
  377.1 5.9 %all-to-all-start.2 = ((bf16[8,16,1920]{2,1,0:T(8,128)(2,1)}), bf16[8,16,1920]{2,1,0:T(8,128)(2,1)S(1)}, u32[]{:S(2)}, u32[]{:S(2)}) async-start(bf16[8,16,1920]{2,1,0:T(8,128)(2,1)} %bitcast.29.refs_1_), calls=%async_computation.3 | async-start | bytes 983040 | tf_op jit(solution)/shard_map/all_to_all | solution.py:792
  385.9 8.8 %collective-permute-start.51 = (bf16[16,2048]{1,0:T(8,128)(2,1)S(1)}, bf16[16,2048]{1,0:T(8,128)(2,1)S(1)}, u32[]{:S(2)}, u32[]{:S(2)}) collective-permute-start(bf16[16,2048]{1,0:T(8,128)(2,1)S(1)} %bitcast.73), channel_id=1, source_target_pairs={{0,0},{2,1},{16,2},{18,3},{32,4},{34,5},{48,6},{50,7},{64,8},{66,9... | collective-permute-start | bytes 196616 | tf_op jit(solution)/shard_map/ppermute | solution.py:804
  (364 shorter events, 128.1 us)
Async XLA Ops:
  12.3 19.0 %all-to-all-start = ((bf16[8,16,1920]{2,1,0:T(8,128)(2,1)}), bf16[8,16,1920]{2,1,0:T(8,128)(2,1)S(1)}, u32[]{:S(2)}, u32[]{:S(2)}) async-start(bf16[8,16,1920]{2,1,0:T(8,128)(2,1)} %pack.1), calls=%async_computation | async-start | bytes 983040 | tf_op jit(solution)/shard_map/all_to_all | solution.py:702
  17.4 58.2 %all-gather.3.cloned.1.call-start = ((), (), s32[]{:S(2)}) async-start(), calls=%async_computation.4 | async-start | bytes 2785280 | tf_op jit(solution)/shard_map/all_gather | solution.py:707
  17.5 13.9 %collective-permute-start.7 = (bf16[16,2048]{1,0:T(8,128)(2,1)S(1)}, bf16[16,2048]{1,0:T(8,128)(2,1)S(1)}, u32[]{:S(2)}, u32[]{:S(2)}) collective-permute-start(bf16[16,2048]{1,0:T(8,128)(2,1)S(1)} %convert_element_type.166), channel_id=1, source_target_pairs={{0,0},{1,2},{2,16},{3,18},{4,32},{5,34},{6,48},{7,50},{8,64},{9,66... | collective-permute-start | bytes 196616 | tf_op jit(solution)/shard_map/ppermute | solution.py:704
  32.1 143.7 %all-gather.5.cloned.1.call-start = ((), (), s32[]{:S(2)}) async-start(), calls=%async_computation.5 | async-start | bytes 10027008 | tf_op jit(solution)/shard_map/all_gather | solution.py:714
  34.5 14.3 %collective-permute-start.1 = (bf16[128,2048]{1,0:T(8,128)(2,1)}, bf16[128,2048]{1,0:T(8,128)(2,1)S(1)}, u32[]{:S(2)}, u32[]{:S(2)}) collective-permute-start(bf16[128,2048]{1,0:T(8,128)(2,1)} %tie.11.refs_0_), channel_id=1, source_target_pairs={{0,12},{4,0},{8,4},{12,8},{1,13},{5,1},{9,5},{13,9},{2,14},{6,2},{... | collective-permute-start | bytes 1572872 | tf_op jit(solution)/shard_map/ppermute | solution.py:566
  36.0 21.8 %collective-permute-start.2 = (bf16[128,2048]{1,0:T(8,128)(2,1)}, bf16[128,2048]{1,0:T(8,128)(2,1)S(1)}, u32[]{:S(2)}, u32[]{:S(2)}) collective-permute-start(bf16[128,2048]{1,0:T(8,128)(2,1)} %tie.11.refs_0_), channel_id=1, source_target_pairs={{0,8},{4,12},{8,0},{12,4},{1,9},{5,13},{9,1},{13,5},{2,10},{6,14},... | collective-permute-start | bytes 1572872 | tf_op jit(solution)/shard_map/ppermute | solution.py:566
  36.3 23.6 %collective-permute-start.3 = (bf16[128,2048]{1,0:T(8,128)(2,1)}, bf16[128,2048]{1,0:T(8,128)(2,1)S(1)}, u32[]{:S(2)}, u32[]{:S(2)}) collective-permute-start(bf16[128,2048]{1,0:T(8,128)(2,1)} %tie.11.refs_0_), channel_id=1, source_target_pairs={{0,1},{1,0},{2,3},{3,2},{4,5},{5,4},{6,7},{7,6},{8,9},{9,8},{10,11... | collective-permute-start | bytes 1572872 | tf_op jit(solution)/shard_map/ppermute | solution.py:570
  75.6 299.6 %reduce-scatter.2.cloned.1.call-start = ((), (), s32[]{:S(2)}) async-start(), calls=%async_computation.6 | async-start | bytes 10027008 | tf_op jit(solution)/shard_map/reduce_scatter | solution.py:753
  80.4 19.4 %collective-permute-start.9 = (bf16[128,2048]{1,0:T(8,128)(2,1)}, bf16[128,2048]{1,0:T(8,128)(2,1)S(1)}, u32[]{:S(2)}, u32[]{:S(2)}) collective-permute-start(bf16[128,2048]{1,0:T(8,128)(2,1)} %tie.12.refs_8_), channel_id=1, source_target_pairs={{0,4},{4,8},{8,12},{12,0},{1,5},{5,9},{9,13},{13,1},{2,6},{6,10},{... | collective-permute-start | bytes 1572872 | tf_op jit(solution)/shard_map/ppermute | solution.py:566
  81.6 18.2 %collective-permute-start.10 = (bf16[128,2048]{1,0:T(8,128)(2,1)}, bf16[128,2048]{1,0:T(8,128)(2,1)S(1)}, u32[]{:S(2)}, u32[]{:S(2)}) collective-permute-start(bf16[128,2048]{1,0:T(8,128)(2,1)} %tie.12.refs_8_), channel_id=1, source_target_pairs={{0,12},{4,0},{8,4},{12,8},{1,13},{5,1},{9,5},{13,9},{2,14},{6,2},{... | collective-permute-start | bytes 1572872 | tf_op jit(solution)/shard_map/ppermute | solution.py:566
  83.1 23.0 %collective-permute-start.11 = (bf16[128,2048]{1,0:T(8,128)(2,1)}, bf16[128,2048]{1,0:T(8,128)(2,1)S(1)}, u32[]{:S(2)}, u32[]{:S(2)}) collective-permute-start(bf16[128,2048]{1,0:T(8,128)(2,1)} %tie.12.refs_8_), channel_id=1, source_target_pairs={{0,8},{4,12},{8,0},{12,4},{1,9},{5,13},{9,1},{13,5},{2,10},{6,14},... | collective-permute-start | bytes 1572872 | tf_op jit(solution)/shard_map/ppermute | solution.py:566
  91.6 14.5 %collective-permute-start.8 = (bf16[1024,128]{1,0:T(8,128)(2,1)}, bf16[1024,128]{1,0:T(8,128)(2,1)S(1)}, u32[]{:S(2)}, u32[]{:S(2)}) collective-permute-start(bf16[1024,128]{1,0:T(8,128)(2,1)} %get-tuple-element.44.kv_ref), channel_id=1, source_target_pairs={{0,2},{2,0},{1,3},{3,1},{4,6},{6,4},{5,7},{7,5},{8,10},{10,8},{9,1... | collective-permute-start | bytes 786440 | tf_op jit(solution)/shard_map/ppermute | solution.py:729
  135.1 13.9 %collective-permute-start.24 = (bf16[128,2048]{1,0:T(8,128)(2,1)S(1)}, bf16[128,2048]{1,0:T(8,128)(2,1)S(1)}, u32[]{:S(2)}, u32[]{:S(2)}) collective-permute-start(bf16[128,2048]{1,0:T(8,128)(2,1)S(1)} %copy-done.42), channel_id=1, source_target_pairs={{0,1},{1,0},{2,3},{3,2},{4,5},{5,4},{6,7},{7,6},{8,9},{9,8},{10,11... | collective-permute-start | bytes 1572872 | tf_op jit(solution)/shard_map/ppermute | solution.py:570
  137.2 16.5 %collective-permute-start.26 = (bf16[128,2048]{1,0:T(8,128)(2,1)S(1)}, bf16[128,2048]{1,0:T(8,128)(2,1)S(1)}, u32[]{:S(2)}, u32[]{:S(2)}) collective-permute-start(bf16[128,2048]{1,0:T(8,128)(2,1)S(1)} %collective-permute-done.10.rest_4_.refs_10_), channel_id=1, source_target_pairs={{0,1},{1,0},{2,3},{3,2},{4,5},{5,4},{6,7},{7,6},{8,9},{9,8},{10,11... | collective-permute-start | bytes 1572872 | tf_op jit(solution)/shard_map/ppermute | solution.py:570
  146.3 17.6 %collective-permute-start.18 = (bf16[128,2048]{1,0:T(8,128)(2,1)S(1)}, bf16[128,2048]{1,0:T(8,128)(2,1)S(1)}, u32[]{:S(2)}, u32[]{:S(2)}) collective-permute-start(bf16[128,2048]{1,0:T(8,128)(2,1)S(1)} %multiply_convert_fusion.refs_0_), channel_id=1, source_target_pairs={{0,12},{4,0},{8,4},{12,8},{1,13},{5,1},{9,5},{13,9},{2,14},{6,2},{... | collective-permute-start | bytes 1572872 | tf_op jit(solution)/shard_map/ppermute | solution.py:566
  148.9 23.4 %collective-permute-start.19 = (bf16[128,2048]{1,0:T(8,128)(2,1)S(1)}, bf16[128,2048]{1,0:T(8,128)(2,1)S(1)}, u32[]{:S(2)}, u32[]{:S(2)}) collective-permute-start(bf16[128,2048]{1,0:T(8,128)(2,1)S(1)} %multiply_convert_fusion.refs_0_), channel_id=1, source_target_pairs={{0,8},{4,12},{8,0},{12,4},{1,9},{5,13},{9,1},{13,5},{2,10},{6,14},... | collective-permute-start | bytes 1572872 | tf_op jit(solution)/shard_map/ppermute | solution.py:566
  150.5 23.6 %collective-permute-start.27 = (bf16[128,2048]{1,0:T(8,128)(2,1)S(1)}, bf16[128,2048]{1,0:T(8,128)(2,1)S(1)}, u32[]{:S(2)}, u32[]{:S(2)}) collective-permute-start(bf16[128,2048]{1,0:T(8,128)(2,1)S(1)} %collective-permute-done.11.rest_5_.refs_11_), channel_id=1, source_target_pairs={{0,1},{1,0},{2,3},{3,2},{4,5},{5,4},{6,7},{7,6},{8,9},{9,8},{10,11... | collective-permute-start | bytes 1572872 | tf_op jit(solution)/shard_map/ppermute | solution.py:570
  153.6 20.5 %collective-permute-start.20 = (bf16[128,2048]{1,0:T(8,128)(2,1)S(1)}, bf16[128,2048]{1,0:T(8,128)(2,1)S(1)}, u32[]{:S(2)}, u32[]{:S(2)}) collective-permute-start(bf16[128,2048]{1,0:T(8,128)(2,1)S(1)} %multiply_convert_fusion.refs_0_), channel_id=1, source_target_pairs={{0,1},{1,0},{2,3},{3,2},{4,5},{5,4},{6,7},{7,6},{8,9},{9,8},{10,11... | collective-permute-start | bytes 1572872 | tf_op jit(solution)/shard_map/ppermute | solution.py:570
  158.7 15.4 %collective-permute-start.21 = (bf16[128,2048]{1,0:T(8,128)(2,1)S(1)}, bf16[128,2048]{1,0:T(8,128)(2,1)S(1)}, u32[]{:S(2)}, u32[]{:S(2)}) collective-permute-start(bf16[128,2048]{1,0:T(8,128)(2,1)S(1)} %collective-permute-done.17.refs_1_), channel_id=1, source_target_pairs={{0,1},{1,0},{2,3},{3,2},{4,5},{5,4},{6,7},{7,6},{8,9},{9,8},{10,11... | collective-permute-start | bytes 1572872 | tf_op jit(solution)/shard_map/ppermute | solution.py:570
  225.9 20.7 %collective-permute-start.32 = (bf16[128,2048]{1,0:T(8,128)(2,1)}, bf16[128,2048]{1,0:T(8,128)(2,1)S(1)}, u32[]{:S(2)}, u32[]{:S(2)}) collective-permute-start(bf16[128,2048]{1,0:T(8,128)(2,1)} %pad_maximum_fusion.4.refs_19_), channel_id=1, source_target_pairs={{0,4},{4,8},{8,12},{12,0},{1,5},{5,9},{9,13},{13,1},{2,6},{6,10},{... | collective-permute-start | bytes 1572872 | tf_op jit(solution)/shard_map/ppermute | solution.py:566
  226.8 19.8 %collective-permute-start.30 = (bf16[128,2048]{1,0:T(8,128)(2,1)}, bf16[128,2048]{1,0:T(8,128)(2,1)}, u32[]{:S(2)}, u32[]{:S(2)}) collective-permute-start(bf16[128,2048]{1,0:T(8,128)(2,1)} %pad_maximum_fusion.3.refs_18_), channel_id=1, source_target_pairs={{0,12},{4,0},{8,4},{12,8},{1,13},{5,1},{9,5},{13,9},{2,14},{6,2},{... | collective-permute-start | bytes 1572872 | tf_op jit(solution)/shard_map/ppermute | solution.py:566
  253.0 23.9 %collective-permute-start.38 = (bf16[128,2048]{1,0:T(8,128)(2,1)S(1)}, bf16[128,2048]{1,0:T(8,128)(2,1)S(1)}, u32[]{:S(2)}, u32[]{:S(2)}) collective-permute-start(bf16[128,2048]{1,0:T(8,128)(2,1)S(1)} %copy-done.1), channel_id=1, source_target_pairs={{0,4},{4,8},{8,12},{12,0},{1,5},{5,9},{9,13},{13,1},{2,6},{6,10},{... | collective-permute-start | bytes 1572872 | tf_op jit(solution)/shard_map/ppermute | solution.py:566
  253.0 28.2 %collective-permute-start.39 = (bf16[128,2048]{1,0:T(8,128)(2,1)S(1)}, bf16[128,2048]{1,0:T(8,128)(2,1)S(1)}, u32[]{:S(2)}, u32[]{:S(2)}) collective-permute-start(bf16[128,2048]{1,0:T(8,128)(2,1)S(1)} %copy-done.1), channel_id=1, source_target_pairs={{0,12},{4,0},{8,4},{12,8},{1,13},{5,1},{9,5},{13,9},{2,14},{6,2},{... | collective-permute-start | bytes 1572872 | tf_op jit(solution)/shard_map/ppermute | solution.py:566
  255.7 25.7 %collective-permute-start.40 = (bf16[128,2048]{1,0:T(8,128)(2,1)S(1)}, bf16[128,2048]{1,0:T(8,128)(2,1)}, u32[]{:S(2)}, u32[]{:S(2)}) collective-permute-start(bf16[128,2048]{1,0:T(8,128)(2,1)S(1)} %copy-done.1), channel_id=1, source_target_pairs={{0,8},{4,12},{8,0},{12,4},{1,9},{5,13},{9,1},{13,5},{2,10},{6,14},... | collective-permute-start | bytes 1572872 | tf_op jit(solution)/shard_map/ppermute | solution.py:566
  262.5 20.1 %collective-permute-start.34 = (bf16[64,2048]{1,0:T(8,128)(2,1)}, bf16[64,2048]{1,0:T(8,128)(2,1)}, u32[]{:S(2)}, u32[]{:S(2)}) collective-permute-start(bf16[64,2048]{1,0:T(8,128)(2,1)} %get-tuple-element.103), channel_id=1, source_target_pairs={{0,12},{4,0},{8,4},{12,8},{1,13},{5,1},{9,5},{13,9},{2,14},{6,2},{... | collective-permute-start | bytes 786440 | tf_op jit(solution)/shard_map/ppermute | solution.py:566
  262.5 22.2 %collective-permute-start.36 = (bf16[64,2048]{1,0:T(8,128)(2,1)}, bf16[64,2048]{1,0:T(8,128)(2,1)}, u32[]{:S(2)}, u32[]{:S(2)}) collective-permute-start(bf16[64,2048]{1,0:T(8,128)(2,1)} %get-tuple-element.104), channel_id=1, source_target_pairs={{0,4},{4,8},{8,12},{12,0},{1,5},{5,9},{9,13},{13,1},{2,6},{6,10},{... | collective-permute-start | bytes 786440 | tf_op jit(solution)/shard_map/ppermute | solution.py:566
  287.3 31.9 %collective-permute-start.37 = (bf16[128,2048]{1,0:T(8,128)(2,1)S(1)}, bf16[128,2048]{1,0:T(8,128)(2,1)S(1)}, u32[]{:S(2)}, u32[]{:S(2)}) collective-permute-start(bf16[128,2048]{1,0:T(8,128)(2,1)S(1)} %pad_maximum_fusion.6.rest_2_), channel_id=1, source_target_pairs={{0,4},{4,8},{8,12},{12,0},{1,5},{5,9},{9,13},{13,1},{2,6},{6,10},{... | collective-permute-start | bytes 1572872 | tf_op jit(solution)/shard_map/ppermute | solution.py:566
  288.4 30.8 %collective-permute-start.35 = (bf16[128,2048]{1,0:T(8,128)(2,1)S(1)}, bf16[128,2048]{1,0:T(8,128)(2,1)}, u32[]{:S(2)}, u32[]{:S(2)}) collective-permute-start(bf16[128,2048]{1,0:T(8,128)(2,1)S(1)} %pad_maximum_fusion.5.rest_1_), channel_id=1, source_target_pairs={{0,12},{4,0},{8,4},{12,8},{1,13},{5,1},{9,5},{13,9},{2,14},{6,2},{... | collective-permute-start | bytes 1572872 | tf_op jit(solution)/shard_map/ppermute | solution.py:566
  333.9 40.3 %all-to-all-start.1 = ((bf16[16,128,640]{2,1,0:T(8,128)(2,1)}), bf16[16,128,640]{2,1,0:T(8,128)(2,1)S(1)}, u32[]{:S(2)}, u32[]{:S(2)}) async-start(bf16[16,128,640]{2,1,0:T(8,128)(2,1)} %attn_grads.1.refs_1_), calls=%async_computation.1 | async-start | bytes 5242880 | tf_op jit(solution)/shard_map/all_to_all | solution.py:781
  354.4 28.5 %collective-permute-start.50 = (bf16[128,2048]{1,0:T(8,128)(2,1)}, bf16[128,2048]{1,0:T(8,128)(2,1)}, u32[]{:S(2)}, u32[]{:S(2)}) collective-permute-start(bf16[128,2048]{1,0:T(8,128)(2,1)} %pad_maximum_fusion.8), channel_id=1, source_target_pairs={{0,4},{4,8},{8,12},{12,0},{1,5},{5,9},{9,13},{13,1},{2,6},{6,10},{... | collective-permute-start | bytes 1572872 | tf_op jit(solution)/shard_map/ppermute | solution.py:566
  355.3 27.7 %collective-permute-start.48 = (bf16[128,2048]{1,0:T(8,128)(2,1)}, bf16[128,2048]{1,0:T(8,128)(2,1)}, u32[]{:S(2)}, u32[]{:S(2)}) collective-permute-start(bf16[128,2048]{1,0:T(8,128)(2,1)} %pad_maximum_fusion.7), channel_id=1, source_target_pairs={{0,12},{4,0},{8,4},{12,8},{1,13},{5,1},{9,5},{13,9},{2,14},{6,2},{... | collective-permute-start | bytes 1572872 | tf_op jit(solution)/shard_map/ppermute | solution.py:566
  377.1 23.1 %all-to-all-start.2 = ((bf16[8,16,1920]{2,1,0:T(8,128)(2,1)}), bf16[8,16,1920]{2,1,0:T(8,128)(2,1)S(1)}, u32[]{:S(2)}, u32[]{:S(2)}) async-start(bf16[8,16,1920]{2,1,0:T(8,128)(2,1)} %bitcast.29.refs_1_), calls=%async_computation.3 | async-start | bytes 983040 | tf_op jit(solution)/shard_map/all_to_all | solution.py:792
  (104 other events, 963.9 us)
Sparse Core Ops, SparseCore 0:
  32.3 43.2 all-gather.2
  78.3 80.2 all-gather.4
  250.9 85.9 reduce-scatter.1
